TPU v7x, 32 devices: a whole 2x2x4 slice. The times are simulated.
32 devices in a mesh: clouds: 8 (over z, y), pts: 4 (over x, core).
Axes of the slice: x: 2, y: 2, z: 4, core: 2. Of those that a mesh axis runs over, the one named last changes fastest.
Arguments:
- features: float32 [32, 1024, 64], P('clouds', 'pts')
- neighbours_one: int32 [32, 20, 1024], P('clouds', None, 'pts'), may hold values from 0 to 1023
- neighbours_two: int32 [32, 20, 1024], P('clouds', None, 'pts'), may hold values from 0 to 1023
- weight_one: float32 [128, 128], replicated, may hold values from -0.5 to 0.5
- gain_one: float32 [128], replicated, may hold values from 0.25 to 1.75
- shift_one: float32 [128], replicated, may hold values from -3 to 3
- weight_two: float32 [256, 256], replicated, may hold values from -0.375 to 0.375
- gain_two: float32 [256], replicated, may hold values from 0.25 to 1.75
- shift_two: float32 [256], replicated, may hold values from -3 to 3
- grad_act: float32 [32, 1024, 256], P('clouds', 'pts'), may hold values from -6 to 6
- grad_max: float32 [32, 256], P('clouds'), may hold values from -48 to 48
- grad_mean: float32 [32, 256], P('clouds'), may hold values from -48 to 48
Outputs:
- activations: float32 [32, 1024, 256], P('clouds', 'pts')
- pool_max: float32 [32, 256], P('clouds')
- pool_mean: float32 [32, 256], P('clouds')
- grad_features: float32 [32, 1024, 64], P('clouds', 'pts')
- grad_weight_one: float32 [128, 128], replicated
- grad_gain_one: float32 [128], replicated
- grad_shift_one: float32 [128], replicated
- grad_weight_two: float32 [256, 256], replicated
- grad_gain_two: float32 [256], replicated
- grad_shift_two: float32 [256], replicated
All inputs are finite; a program needn't handle non-finite values.
Results may differ from a plain program's by a relative error of at most 0.0003.
Values sent between devices are 32-bit elements; how exact they have to be, the bound alone decides.
No kernel may reach another device: no remote copies, remote signals or barrier semaphores. Data moves between devices by JAX's collectives and lax.ppermute only.
A program may use at most 256 MiB of HBM per device.

v0:
```python
import functools

import jax
import jax.numpy as jnp
from jax import lax
from jax.experimental import pallas as pl
from jax.experimental.pallas import tpu as pltpu
from jax.sharding import PartitionSpec as P

norm_eps = 1e-05
LOG2E = 1.4426950408889634
BOTH = ("clouds", "pts")
MIB = 2**20


def f32(*shape):
    return jax.ShapeDtypeStruct(shape, jnp.float32)


def in_hbm(*shape):
    return pltpu.HBM(shape, jnp.float32)


def from_hbm(x):
    return pltpu.with_memory_space_constraint(x, pltpu.HBM)


def params(mib):
    return pltpu.CompilerParams(vmem_limit_bytes=mib * MIB)


def whole(shape):
    return pl.BlockSpec(shape, lambda *step: (0,) * len(shape))


SMEM = pl.BlockSpec(memory_space=pltpu.SMEM)


def exchange(x, axes, mask):
    size = lax.axis_size(axes)
    return lax.ppermute(x, axes, [(i, i ^ mask) for i in range(size)])


def bit_groups(size):
    bits = [1 << i for i in range(size.bit_length() - 1)]
    groups = [bits[:1]] if bits else []
    rest = bits[1:]
    while rest:
        groups.append(rest[:2])
        rest = rest[2:]
    return groups


def stages():
    yield "pts", list(range(1, lax.axis_size("pts")))
    for bits in bit_groups(lax.axis_size("clouds")):
        masks = [0]
        for bit in bits:
            masks = masks + [mask | bit for mask in masks]
        yield "clouds", masks[1:]


def swap(x, axes, masks):
    return [x] + [exchange(x, axes, mask) for mask in masks]


def pair_sum(values):
    while len(values) > 1:
        values = [values[i] + values[i + 1] for i in range(0, len(values), 2)]
    return values[0]


def sum_stages(x, cloud_stages):
    for axis, masks in cloud_stages:
        x = pair_sum(swap(x, axis, masks))
    return x


def after(value, *others):
    return lax.optimization_barrier((value, *others))[0]


def sum_beside(message, received, work):
    (axis, masks), *rest = list(stages())[:0:-1]
    first = work[0](None)
    total = message(lax.optimization_barrier((*received, first))[:-1])
    moving = swap(total, axis, masks)
    second = work[1](total)
    total = pair_sum(list(lax.optimization_barrier((*moving, second))[:-1]))
    return sum_stages(total, rest), [first, second]


def join_stats(stat, count):
    for axis, masks in stages():
        parts = swap(stat, axis, masks)
        mean = pair_sum([part[0:1] for part in parts]) / len(parts)
        away = pair_sum([(part[0:1] - mean) ** 2 for part in parts])
        stat = jnp.concatenate([mean, pair_sum([part[1:2] for part in parts]) + count * away], axis=0)
        count = count * len(parts)
    return stat


def pack_kernel(slots, me_ref, *refs):
    sources, outs, fetched, sems = refs[:9], refs[9:-10], refs[-10:-1], refs[-1]
    parts, small_ref, weights = outs[:-3], outs[-3], outs[-2:]
    copies = [
        pltpu.make_async_copy(source, target, sems.at[i])
        for i, (source, target) in enumerate(zip(sources, fetched))
    ]
    for copy in copies:
        copy.start()
    for copy in copies:
        copy.wait()
    feat_ref, one_ref, two_ref = fetched[:3]
    me = me_ref[0]
    width, rows = feat_ref.shape[1], feat_ref.shape[2]
    for mask, out in enumerate(parts):
        cloud = me ^ mask
        out[0:width, :] = feat_ref[cloud]
        for k in range(slots):
            for at, ids in ((width, one_ref), (width + slots, two_ref)):
                row = ids[k, pl.ds(cloud, 1), :] ^ (cloud * rows)
                out[at + k : at + k + 1, :] = row.astype(jnp.float32)
    small_ref[...] = jnp.zeros_like(small_ref)
    for i, vector in enumerate(fetched[3:7]):
        small_ref[i : i + 1, 0 : vector.shape[1]] = vector[...]
    for kept, weight in zip(weights, fetched[7:9]):
        kept[...] = weight[...]


def pack(me, features, neighbours_one, neighbours_two, vectors, weights):
    clouds, rows, width = features.shape
    slots = neighbours_one.shape[1]
    operands = (
        jnp.swapaxes(features, 1, 2),
        jnp.swapaxes(neighbours_one, 0, 1),
        jnp.swapaxes(neighbours_two, 0, 1),
        *(v.reshape(1, -1) for v in vectors),
        *weights,
    )
    results = pl.pallas_call(
        functools.partial(pack_kernel, slots),
        in_specs=[SMEM] + [pl.BlockSpec(memory_space=pltpu.HBM)] * len(operands),
        out_shape=[f32(width + 2 * slots, rows)] * clouds
        + [f32(8, max(v.shape[0] for v in vectors))]
        + [f32(*w.shape) for w in weights],
        scratch_shapes=[pltpu.VMEM(v.shape, v.dtype) for v in operands]
        + [pltpu.SemaphoreType.DMA((len(operands),))],
        compiler_params=params(8),
        name="pack",
    )(me, *(from_hbm(v) for v in operands))
    return results[:clouds], results[clouds], results[clouds + 1 :]


def split_kernel(me_ref, x_ref, *outs):
    me = me_ref[0]
    for mask, out in enumerate(outs):
        out[...] = x_ref[me ^ mask]


def split(me, x):
    clouds, rows, width = x.shape
    return pl.pallas_call(
        split_kernel,
        in_specs=[SMEM, pl.BlockSpec(memory_space=pltpu.VMEM)],
        out_shape=[f32(rows, width)] * clouds,
        compiler_params=params(16),
        name="split",
    )(me, from_hbm(x))


def unpack_output_kernel(rows, me_ref, *refs):
    parts, (act_ref, max_ref, mean_ref) = refs[:-3], refs[-3:]
    me = me_ref[0]
    for mask, part in enumerate(parts):
        cloud = me ^ mask
        act_ref[cloud] = part[0:rows]
        max_ref[pl.ds(cloud, 1), :] = part[rows : rows + 1]
        mean_ref[pl.ds(cloud, 1), :] = part[rows + 1 : rows + 2]


def unpack_output(me, parts):
    clouds, width = len(parts), parts[0].shape[1]
    rows = parts[0].shape[0] - 8
    return pl.pallas_call(
        functools.partial(unpack_output_kernel, rows),
        in_specs=[SMEM] + [pl.BlockSpec(memory_space=pltpu.VMEM)] * clouds,
        out_shape=[f32(clouds, rows, width), f32(clouds, width), f32(clouds, width)],
        compiler_params=params(16),
        name="unpack_output",
    )(me, *parts)


def unpack_grad_kernel(me_ref, *refs):
    parts, (grad_ref, wgrad_ref) = refs[:-2], refs[-2:]
    me = me_ref[0]
    width = grad_ref.shape[1]
    piece = wgrad_ref.shape[0] // len(parts)
    for mask, part in enumerate(parts):
        other = me ^ mask
        grad_ref[other] = part[0:width]
        wgrad_ref[pl.ds(pl.multiple_of(other * piece, piece), piece), :] = part[width:]


def unpack_grad(me, parts, width):
    rows, lanes = parts[0].shape
    count = len(parts)
    return pl.pallas_call(
        unpack_grad_kernel,
        in_specs=[SMEM] + [pl.BlockSpec(memory_space=pltpu.VMEM)] * count,
        out_shape=[f32(count, width, lanes), f32(count * (rows - width), lanes)],
        compiler_params=params(16),
        name="unpack_grad",
    )(me, *parts)


def two_terms(x):
    high = x.astype(jnp.bfloat16)
    low = (x - high.astype(jnp.float32)).astype(jnp.bfloat16)
    return jnp.concatenate([high, low], axis=1)


def halves_sum(x):
    half = x.shape[1] // 2
    return x[:, :half] + x[:, half:]


def product(x, y, on_x, on_y):
    x_high, y_high = x.astype(jnp.bfloat16), y.astype(jnp.bfloat16)
    x_low = (x - x_high.astype(jnp.float32)).astype(jnp.bfloat16)
    y_low = (y - y_high.astype(jnp.float32)).astype(jnp.bfloat16)
    return lax.dot_general(
        jnp.concatenate([x_high, x_low, x_high], axis=on_x),
        jnp.concatenate([y_high, y_high, y_low], axis=on_y),
        (((on_x,), (on_y,)), ((), ())),
        preferred_element_type=jnp.float32,
    )


def column_sum(x):
    return jnp.sum(x, axis=0, keepdims=True)


def count_links(ids_ref, first, slots, wide, links):
    points, columns = links.shape
    block = 256
    here = lax.broadcasted_iota(jnp.int32, (16, columns), 0).astype(jnp.bfloat16)
    one = jnp.ones((16, columns), jnp.bfloat16)
    zero = jnp.zeros((16, columns), jnp.bfloat16)
    for start in range(0, points, block):
        for k in range(slots):
            local = ids_ref[first + k : first + k + 1, :] - float(start)
            local = jnp.where((local >= 0) & (local < block), local, -1.0)
            wide[k] = jnp.broadcast_to(local, (16, columns)).astype(jnp.bfloat16)

        def sixteen(step, carry):
            row = here + (step * 16).astype(jnp.float32).astype(jnp.bfloat16)
            total = zero
            for k in range(slots):
                total = total + jnp.where(wide[k] == row, one, zero)
            links[pl.ds(pl.multiple_of(start + step * 16, 16), 16), :] = total
            return carry

        lax.fori_loop(0, block // 16, sixteen, 0)


def links_kernel(firsts, slots, ids_ref, *refs):
    wide = refs[-1]
    for first, links in zip(firsts, refs[:-1]):
        count_links(ids_ref, first, slots, wide, links)


def part_links(part, firsts, slots, points):
    columns = part.shape[1]
    edges = len(firsts) * slots * points * columns
    return pl.pallas_call(
        functools.partial(links_kernel, firsts, slots),
        out_shape=[jax.ShapeDtypeStruct((points, columns), jnp.bfloat16)] * len(firsts),
        scratch_shapes=[pltpu.VMEM((slots, 16, columns), jnp.bfloat16)],
        compiler_params=params(8),
        cost_estimate=pl.CostEstimate(
            flops=100 * edges, bytes_accessed=2 * points * columns, transcendentals=0
        ),
        name="part_links",
    )(part)


def table_stats(x, weight, links, slots, a_ref, b_ref, in_ref, deg_ref, stat_ref):
    points, width = x.shape
    outs = weight.shape[1]
    upper, lower = weight[:width], weight[width:]
    joined = jnp.concatenate([upper - lower, lower], axis=1)
    middle = column_sum(x) / points
    level = jnp.dot(
        jnp.broadcast_to(middle, (8, width)), joined, precision=lax.Precision.HIGHEST
    )
    both = product(x - middle, joined, 1, 0) + level[0:1]
    a, b = both[:, :outs], both[:, outs:]
    mean_a = column_sum(a) / points
    a_off = a - mean_a
    terms = two_terms(a_off)
    seen = degree = 0.0
    for m, part in enumerate(links):
        columns = part.shape[1]
        some = terms[m * columns : (m + 1) * columns]
        seen = seen + jnp.dot(part[...], some, preferred_element_type=jnp.float32)
        degree = degree + jnp.sum(part[...].astype(jnp.float32), axis=1, keepdims=True)
    seen = halves_sum(seen)
    mean_b = column_sum(degree * b) / (points * slots)
    b_off = b - mean_b
    inward = seen + degree * b_off
    a_ref[...] = a
    b_ref[...] = b
    in_ref[...] = inward
    deg_ref[...] = jnp.broadcast_to(degree, deg_ref.shape)
    stat_ref[0:1, :] = mean_a + mean_b
    stat_ref[1:2, :] = slots * column_sum(a_off * a_off) + column_sum((seen + inward) * b_off)


def first_kernel(slots, width, count, *refs):
    parts, early, (weight_ref, x_ref, ids_ref, a_ref, b_ref, in_ref, deg_ref, stat_ref, *late, wide) = (
        refs[:count],
        refs[count : count + count // 2],
        refs[count + count // 2 :],
    )
    rows = parts[0].shape[1]
    fill = jnp.zeros((128 - parts[0].shape[0], rows), jnp.float32)
    for m, part in enumerate(parts):
        ids_ref[:, m * rows : (m + 1) * rows] = part[width:, :]
        x_ref[m * rows : (m + 1) * rows, :] = jnp.concatenate([part[...], fill], axis=0).T
    for part, links in zip(parts[len(early) :], late):
        count_links(part, width, slots, wide, links)
    table_stats(
        x_ref[:, :width], weight_ref[...], (*early, *late), slots, a_ref, b_ref, in_ref, deg_ref, stat_ref
    )


def first_tables(parts, early, weight, slots):
    count, columns = len(parts), parts[0].shape[1]
    points = count * columns
    width, outs = weight.shape[0] // 2, weight.shape[1]
    return pl.pallas_call(
        functools.partial(first_kernel, slots, width, count),
        out_shape=[
            f32(points, 128),
            f32(2 * slots, points),
            f32(points, outs),
            f32(points, outs),
            f32(points, outs),
            f32(points, 128),
            f32(2, outs),
        ],
        scratch_shapes=[pltpu.VMEM((points, columns), jnp.bfloat16)] * (count - len(early))
        + [pltpu.VMEM((slots, 16, columns), jnp.bfloat16)],
        compiler_params=params(24),
        name="first_tables",
    )(*parts, *early, weight)


def second_kernel(slots, x_ref, weight_ref, *refs):
    links, outs = refs[:-5], refs[-5:]
    table_stats(x_ref[...], weight_ref[...], links, slots, *outs)


def second_tables(x, weight, links, slots):
    points, outs = x.shape[0], weight.shape[1]
    return pl.pallas_call(
        functools.partial(second_kernel, slots),
        out_shape=[
            f32(points, outs),
            f32(points, outs),
            f32(points, outs),
            f32(points, 128),
            f32(2, outs),
        ],
        compiler_params=params(24),
        name="second_tables",
    )(x, weight, *links)


def edge_kernel(
    edges, layer, slots, first, tile, x_ref, a_ref, b_ref, stat_ref, small_ref,
    out_ref, weight_ref, inv_ref, slope_ref, moment_ref, ysum_ref, table, centre, held, bounded,
):
    points, width = a_ref.shape
    step = pl.program_id(0)
    block = 8

    @pl.when(step == 0)
    def _():
        gain = small_ref[2 * layer : 2 * layer + 1, 0:width]
        shift = small_ref[2 * layer + 1 : 2 * layer + 2, 0:width]
        scale = gain * lax.rsqrt(stat_ref[1:2, :] / edges + norm_eps) * -LOG2E
        middle = column_sum(b_ref[...]) / points
        there = (b_ref[...] - middle) * scale
        here = (a_ref[...] + (middle - stat_ref[0:1, :])) * scale - shift * LOG2E
        table[...] = two_terms(there)
        centre[...] = here
        reach = jnp.max(jnp.abs(here), axis=0, keepdims=True) + jnp.max(
            jnp.abs(there), axis=0, keepdims=True
        )
        bounded[0] = (jnp.max(reach) < 60.0).astype(jnp.int32)

    rows = pl.ds(pl.multiple_of(step * tile, tile), tile)
    columns = lax.broadcasted_iota(jnp.int32, (tile, points), 1).astype(jnp.float32)

    def gather(ids):
        pick = jnp.where(ids == columns, 1.0, 0.0).astype(jnp.bfloat16)
        return jnp.dot(pick, table[...], preferred_element_type=jnp.float32)

    def finish(at, top, totals):
        mass, slope, moment, total = totals
        out_ref[at, :] = top + jnp.log(mass)
        inv = 0.8 / mass
        inv_ref[at, :] = inv
        slope_ref[at, :] = slope * inv
        moment_ref[at, :] = moment * inv * (-1.0 / LOG2E)
        ysum_ref[at, :] = total * (-1.0 / LOG2E)

    @pl.when(bounded[0] == 1)
    def _():
        found = [gather(x_ref[rows, first + k : first + k + 1]) for k in range(slots)]
        for start in range(0, tile, block):
            at = slice(start, start + block)
            here = centre[pl.ds(pl.multiple_of(step * tile + start, block), block), :]
            totals = [jnp.zeros((block, width), jnp.float32)] * 4
            for k in range(slots):
                t = here + halves_sum(found[k][at])
                grown = 1.0 + jnp.exp2(t)
                fall = jnp.exp2((-0.2 * LOG2E) * jnp.log(grown) - t)
                share = grown * fall
                part = fall + 0.25 * share
                weight_ref[k, at, :] = part
                totals = [total + term for total, term in zip(totals, (share, part, part * t, t))]
            finish(at, 0.0, totals)

    @pl.when(bounded[0] == 0)
    def _():
        lanes = lax.broadcasted_iota(jnp.int32, (tile, x_ref.shape[1]), 1)

        def collect(k, carry):
            ids = jnp.sum(jnp.where(lanes == first + k, x_ref[rows, :], 0.0), axis=1, keepdims=True)
            held[k] = centre[rows, :] + halves_sum(gather(ids))
            return carry

        lax.fori_loop(0, slots, collect, 0)

        def rise(t):
            grown = 1.0 + jnp.exp2(jnp.minimum(t, 64.0))
            return jnp.maximum((0.8 * LOG2E) * jnp.log(grown), 0.8 * t) - t, grown

        def some(b, carry):
            at = pl.ds(pl.multiple_of(b * block, block), block)
            low = held[0, at, :]
            for k in range(1, slots):
                low = jnp.minimum(low, held[k, at, :])
            peak, _ = rise(low)
            totals = [jnp.zeros((block, width), jnp.float32)] * 4
            for k in range(slots):
                t = held[k, at, :]
                level, grown = rise(t)
                share = jnp.exp2(level - peak)
                part = share * (1.0 / grown + 0.25)
                weight_ref[k, at, :] = part
                totals = [total + term for total, term in zip(totals, (share, part, part * t, t))]
            finish(at, peak * (1.0 / LOG2E), totals)
            return carry

        lax.fori_loop(0, tile // block, some, 0)


def edge_forward(edges, layer, slots, first, tile, x, a, b, stat, small):
    points, width = a.shape
    some = pl.BlockSpec((tile, width), lambda step: (step, 0))
    return pl.pallas_call(
        functools.partial(edge_kernel, edges, layer, slots, first, tile),
        grid=(points // tile,),
        in_specs=[whole(v.shape) for v in (x, a, b, stat, small)],
        out_specs=[some, pl.BlockSpec((slots, tile, width), lambda step: (0, step, 0))] + [some] * 4,
        out_shape=[f32(points, width), in_hbm(slots, points, width)] + [f32(points, width)] * 4,
        scratch_shapes=[
            pltpu.VMEM((points, 2 * width), jnp.bfloat16),
            pltpu.VMEM((points, width), jnp.float32),
            pltpu.VMEM((slots, tile, width), jnp.float32),
            pltpu.SMEM((1,), jnp.int32),
        ],
        compiler_params=params(24),
        name="edges",
    )(x, a, b, stat, small)


def pool_kernel(me_ref, out_ref, inv_ref, slope_ref, moment_ref, gmax_ref, gmean_ref, *refs):
    count = (len(refs) - 2) // 2
    acts, parts = refs[:count], refs[count : 2 * count]
    scaled_ref, own_ref = refs[2 * count :]
    me = me_ref[0]
    points, width = out_ref.shape
    rows = points // count
    out = out_ref[...]
    top = jnp.max(out, axis=0, keepdims=True)
    pool = top + jnp.log(column_sum(jnp.exp(out - top)))
    mean = column_sum(out) / points
    to_max = gmax_ref[pl.ds(me, 1), :]
    to_mean = gmean_ref[pl.ds(me, 1), :] / points
    own_sum = moment_sum = jnp.zeros((1, width), jnp.float32)
    for m in range(count):
        here = slice(m * rows, (m + 1) * rows)
        part = out[here]
        parts[m][0:rows, :] = part
        parts[m][rows : rows + 1, :] = pool
        parts[m][rows + 1 : rows + 2, :] = mean
        parts[m][rows + 4 : rows + 8, :] = jnp.zeros((4, width), jnp.float32)
        grad = acts[m][...] + to_max * jnp.exp(part - pool) + to_mean
        own = grad * slope_ref[here, :]
        scaled_ref[here, :] = grad * inv_ref[here, :]
        own_ref[here, :] = own
        own_sum = own_sum + column_sum(own)
        moment_sum = moment_sum + column_sum(grad * moment_ref[here, :])
    for m in range(count):
        parts[m][rows + 2 : rows + 3, :] = own_sum
        parts[m][rows + 3 : rows + 4, :] = moment_sum


def pools(me, out, inv, slope, moment, grad_max, grad_mean, acts):
    points, width = out.shape
    count = len(acts)
    rows = points // count
    results = pl.pallas_call(
        pool_kernel,
        in_specs=[SMEM] + [pl.BlockSpec(memory_space=pltpu.VMEM)] * (6 + count),
        out_shape=[f32(rows + 8, width)] * count + [f32(points, width)] * 2,
        compiler_params=params(16),
        name="pools",
    )(me, out, inv, slope, moment, grad_max, grad_mean, *acts)
    return results[:count], results[count], results[count + 1]


def scatter_kernel(first, group, ids_ref, grad_ref, weight_ref, sum_ref):
    step = pl.program_id(0)
    points = grad_ref.shape[0]
    rows = lax.broadcasted_iota(jnp.int32, (points, points), 0).astype(jnp.float32)
    picks, terms = [], []
    for g in range(group):
        ids = ids_ref[pl.ds(first + step * group + g, 1), :]
        picks.append(jnp.where(ids == rows, 1.0, 0.0).astype(jnp.bfloat16))
        terms.append(two_terms(grad_ref[...] * weight_ref[g]))
    found = halves_sum(
        jnp.dot(
            jnp.concatenate(picks, axis=1),
            jnp.concatenate(terms, axis=0),
            preferred_element_type=jnp.float32,
        )
    )

    @pl.when(step == 0)
    def _():
        sum_ref[...] = found

    @pl.when(step > 0)
    def _():
        sum_ref[...] += found


def scatter(ids, first, grad, weight, start, stop, group):
    points, width = grad.shape
    edges = (stop - start) * points
    return pl.pallas_call(
        functools.partial(scatter_kernel, first + start, group),
        grid=((stop - start) // group,),
        in_specs=[
            whole(ids.shape),
            whole(grad.shape),
            pl.BlockSpec((group, points, width), lambda step: (start // group + step, 0, 0)),
        ],
        out_specs=whole((points, width)),
        out_shape=f32(points, width),
        compiler_params=params(28),
        cost_estimate=pl.CostEstimate(
            flops=4 * edges * points * width, bytes_accessed=4 * edges * width, transcendentals=0
        ),
        name="scatter",
    )(ids, grad, from_hbm(weight))


def point_grads(edges, slots, own, inward_grads, ysum, inward, degree, local, stat, sums, gain, shift):
    spread = lax.rsqrt(stat[1:2, :] / edges + norm_eps)
    scale = gain * spread
    own_all = sums[0:1, :]
    gain_all = (sums[1:2, :] - shift * own_all) / gain
    shift_part = own_all / edges
    gain_part = gain_all / edges
    leave = scale * (own - slots * shift_part - gain_part * ((ysum - slots * shift) / gain))
    normed = spread * (inward + degree * (local[0:1, :] - stat[0:1, :]))
    reach = scale * (inward_grads - degree * shift_part - gain_part * normed)
    return leave, reach, gain_all


def turned(weight):
    width = weight.shape[0] // 2
    return jnp.concatenate([weight[:width] - weight[width:], weight[width:]], axis=1)


def weight_grad(x, leave, reach):
    grads = jnp.concatenate([leave, reach - leave], axis=1)
    middle = column_sum(x) / x.shape[0]
    level = lax.dot_general(
        jnp.broadcast_to(middle, (8, x.shape[1])) * 0.125,
        jnp.broadcast_to(column_sum(grads), (8, grads.shape[1])),
        (((0,), (0,)), ((), ())),
        precision=lax.Precision.HIGHEST,
        preferred_element_type=jnp.float32,
    )
    return product(x - middle, grads, 0, 0) + level


def total_of(refs):
    total = refs[0][...]
    for ref in refs[1:]:
        total = total + ref[...]
    return total


def middle_kernel(
    edges, slots, count, me_ref, own_ref, ysum_ref, in_ref, deg_ref, local_ref, stat_ref, sums_ref,
    small_ref, x_ref, weight_ref, inv_ref, slope_ref, moment_ref, *refs,
):
    wgrad = refs[-1]
    scaled_ref, next_ref, gain_out_ref = refs[-4:-1]
    reached, parts = refs[: -4 - count], refs[-4 - count : -4]
    leave, reach, gain_all = point_grads(
        edges, slots, own_ref[...], total_of(reached), ysum_ref[...], in_ref[...], deg_ref[:, 0:1],
        local_ref[...], stat_ref[...], sums_ref[...], small_ref[2:3, :], small_ref[3:4, :],
    )
    gain_out_ref[...] = gain_all
    width, outs = x_ref.shape[1], leave.shape[1]
    both = weight_grad(x_ref[...], leave, reach)
    wgrad[0:width, :] = both[:, :outs]
    wgrad[width:, :] = both[:, outs:]
    grad = product(jnp.concatenate([leave, reach], axis=1), turned(weight_ref[...]), 1, 1)
    own = grad * slope_ref[...]
    scaled_ref[...] = grad * inv_ref[...]
    next_ref[...] = own
    own_sum = column_sum(own)
    moment_sum = column_sum(grad * moment_ref[...])
    me = me_ref[0]
    piece = 2 * width // count
    for mask, part in enumerate(parts):
        start = pl.multiple_of((me ^ mask) * piece, piece)
        part[0:piece, :] = wgrad[pl.ds(start, piece), :]
        part[piece:, :] = jnp.zeros((8, outs), jnp.float32)
        part[piece : piece + 1, 0:width] = own_sum
        part[piece + 1 : piece + 2, 0:width] = moment_sum


def middle(
    edges, slots, count, me, own, ysum, inward, degree, local, stat, sums, small, x, weight,
    inv, slope, moment, reached,
):
    points, width = x.shape
    outs = weight.shape[1]
    operands = (own, ysum, inward, degree, local, stat, sums, small, x, weight, inv, slope, moment)
    results = pl.pallas_call(
        functools.partial(middle_kernel, edges, slots, count),
        in_specs=[SMEM] + [pl.BlockSpec(memory_space=pltpu.VMEM)] * (len(operands) + len(reached)),
        out_shape=[f32(2 * width // count + 8, outs)] * count
        + [f32(points, width), f32(points, width), f32(1, outs)],
        scratch_shapes=[pltpu.VMEM((2 * width, outs), jnp.float32)],
        compiler_params=params(32),
        name="middle",
    )(me, *operands, *reached)
    return results[:count], *results[count:]


def last_kernel(
    edges, slots, count, own_ref, ysum_ref, in_ref, deg_ref, local_ref, stat_ref, joined_ref,
    small_ref, x_ref, weight_ref, *refs,
):
    reached, (gain_out_ref, wgrad_ref), parts = (
        refs[: -2 - count],
        refs[-2 - count : -count],
        refs[-count:],
    )
    width, outs = weight_ref.shape[0] // 2, weight_ref.shape[1]
    piece = joined_ref.shape[0] - 8
    leave, reach, gain_all = point_grads(
        edges, slots, own_ref[...], total_of(reached), ysum_ref[...], in_ref[...], deg_ref[:, 0:1],
        local_ref[...], stat_ref[...], joined_ref[piece : piece + 2, 0:outs],
        small_ref[0:1, 0:outs], small_ref[1:2, 0:outs],
    )
    gain_out_ref[...] = gain_all
    wgrad_ref[...] = weight_grad(x_ref[:, 0:width], leave, reach)
    grad = product(turned(weight_ref[...]), jnp.concatenate([leave, reach], axis=1), 1, 1)
    rows = grad.shape[1] // count
    for m, part in enumerate(parts):
        part[0:width, :] = grad[:, m * rows : (m + 1) * rows]
        part[width:, :] = joined_ref[0:piece, :]


def last(
    edges, slots, count, own, ysum, inward, degree, local, stat, joined, small, x, weight, reached
):
    points = x.shape[0]
    width, outs = weight.shape[0] // 2, weight.shape[1]
    lanes = points // count
    assert lanes == 2 * outs == joined.shape[1]
    results = pl.pallas_call(
        functools.partial(last_kernel, edges, slots, count),
        out_shape=[f32(1, outs), f32(width, 2 * outs)] + [f32(width + joined.shape[0] - 8, lanes)] * count,
        compiler_params=params(32),
        name="last",
    )(own, ysum, inward, degree, local, stat, joined, small, x, weight, *reached)
    return results[0], results[1], results[2:]


def body(
    features,
    neighbours_one,
    neighbours_two,
    weight_one,
    gain_one,
    shift_one,
    weight_two,
    gain_two,
    shift_two,
    grad_act,
    grad_max,
    grad_mean,
):
    clouds, rows, width = features.shape
    slots = neighbours_one.shape[1]
    count = lax.axis_size("pts")
    assert clouds == count
    points = rows * count
    local_edges = points * slots
    edges = float(local_edges * lax.axis_size(BOTH))
    me = lax.axis_index("pts").astype(jnp.int32).reshape(1)
    def to_owner(parts):
        return [parts[0]] + [exchange(part, "pts", m) for m, part in enumerate(parts) if m]

    with jax.named_scope("bring_clouds"):
        parts, small, (weight_one, weight_two) = pack(
            me, features, neighbours_one, neighbours_two,
            (gain_one, shift_one, gain_two, shift_two), (weight_one, weight_two),
        )
        parts = to_owner(parts)
        firsts = (width, width + slots)
        early = [part_links(part, firsts, slots, points) for part in parts[: count // 2]]
    with jax.named_scope("bring_cotangents"):
        acts = to_owner(split(me, grad_act))

    with jax.named_scope("layer_one"):
        x, ids, a_one, b_one, in_one, deg_one, local_one = first_tables(
            parts, [links[0] for links in early], weight_one, slots
        )
        late = [part_links(part, firsts[1:], slots, points) for part in parts[count // 2 :]]
        links = [links[-1] for links in early + late]
        stat_one = join_stats(local_one, local_edges)
        hidden, share_one, inv_one, slope_one, moment_one, ysum_one = edge_forward(
            edges, 0, slots, width, 128, x, a_one, b_one, stat_one, small
        )
    with jax.named_scope("layer_two"):
        a_two, b_two, in_two, deg_two, local_two = second_tables(hidden, weight_two, links, slots)
        stat_two = join_stats(local_two, local_edges)
        out, share_two, inv_two, slope_two, moment_two, ysum_two = edge_forward(
            edges, 1, slots, width + slots, 128, x, a_two, b_two, stat_two, small
        )
    with jax.named_scope("pools"):
        out_parts, scaled_two, own_two = pools(
            me, out, inv_two, slope_two, moment_two, grad_max, grad_mean, acts
        )
        out_parts = to_owner(out_parts)
        output, pool_max, pool_mean = unpack_output(me, out_parts)

    cut = 4 * (3 * slots // 20)
    with jax.named_scope("layer_two_back"):
        sums_two, reached = sum_beside(
            lambda received: pair_sum([part[rows + 2 : rows + 4] for part in received]),
            out_parts,
            [
                lambda ready: scatter(ids, slots, scaled_two, share_two, 0, cut, 4),
                lambda ready: scatter(ids, slots, after(scaled_two, ready), share_two, cut, slots, 4),
            ],
        )
        wgrad_parts, scaled_one, own_one, gain_grad_two = middle(
            edges, slots, count, me, own_two, ysum_two, in_two, deg_two, local_two, stat_two, sums_two,
            small, hidden, weight_two, inv_one, slope_one, moment_one, reached,
        )
    with jax.named_scope("layer_one_back"):
        joined, reached = sum_beside(
            lambda received: pair_sum(list(received)),
            to_owner(wgrad_parts),
            [
                lambda ready: scatter(ids, 0, scaled_one, share_one, 0, cut, 4),
                lambda ready: scatter(ids, 0, after(scaled_one, ready), share_one, cut, slots, 4),
            ],
        )
        gain_grad_one, wgrad_one, grad_parts = last(
            edges, slots, count, own_one, ysum_one, in_one, deg_one, local_one, stat_one, joined,
            small, x, weight_one, reached,
        )
        wgrad_one = pair_sum(to_owner([wgrad_one] * count))
        wgrad_one, *grad_parts = lax.optimization_barrier((wgrad_one, *grad_parts))
        grad_parts = to_owner(grad_parts)
        wgrad_one = sum_stages(wgrad_one, list(stages())[1:])
        wgrad_one = jnp.concatenate(jnp.split(wgrad_one, 2, axis=1), axis=0)
        grad_features, wgrad_two = unpack_grad(me, grad_parts, width)
    return (
        output,
        pool_max,
        pool_mean,
        jnp.swapaxes(grad_features, 1, 2),
        wgrad_one,
        gain_grad_one.reshape(-1),
        joined[-8, : weight_one.shape[1]],
        wgrad_two,
        gain_grad_two.reshape(-1),
        sums_two[0],
    )


def solution(mesh):
    placed = (
        P("clouds", "pts", None),
        P("clouds", None, "pts"),
        P("clouds", None, "pts"),
        P(),
        P(),
        P(),
        P(),
        P(),
        P(),
        P("clouds", "pts", None),
        P("clouds", None),
        P("clouds", None),
    )
    return jax.shard_map(
        body,
        mesh=mesh,
        in_specs=placed,
        out_specs=(
            P("clouds", "pts", None),
            P("clouds", None),
            P("clouds", None),
            P("clouds", "pts", None),
            P(),
            P(),
            P(),
            P(),
            P(),
            P(),
        ),
        check_vma=False,
    )
```

profile of v0, /device:TPU:0, one launch (start us, length us, event | category | flops | bytes accessed | tf_op | source)
XLA Modules:
  0.0 191.1 jit_solution(18414609313883809252)
XLA Ops:
  0.7 1.4 pack.1
  2.1 0.5 collective-permute-start
  2.6 2.6 %collective-permute-start.1 = (f32[104,256]{1,0:T(8,128)S(1)}, f32[104,256]{1,0:T(8,128)S(1)}, u32[]{:S(2)}, u32[]{:S(2)}) collective-permute-start(f32[104,256]{1,0:T(8,128)S(1)} %get-tuple-element.98), channel_id=1, source_target_pairs={{0,2},{1,3},{2,0},{3,1},{4,6},{5,7},{6,4},{7,5},{8,10},{9,11},{10,... | collective-permute-start | bytes 319496 | tf_op jit(solution)/shard_map/bring_clouds/ppermute | solution.py:41
  5.2 4.3 %part_links.4 = (bf16[1024,256]{1,0:T(8,128)(2,1)S(1)}, bf16[1024,256]{1,0:T(8,128)(2,1)S(1)}) custom-call(f32[104,256]{1,0:T(8,128)S(1)} %get-tuple-element.96.ids_ref.refs_0_), custom_call_target="tpu_custom_call" | custom-call | flops 1048576000 | bytes 524288 | tf_op jit(solution)/shard_map/bring_clouds/part_links/pallas_call | solution.py:276
  9.6 4.3 %part_links.5 = (bf16[1024,256]{1,0:T(8,128)(2,1)S(1)}, bf16[1024,256]{1,0:T(8,128)(2,1)S(1)}) custom-call(f32[104,256]{1,0:T(8,128)S(1)} %collective-permute-done.ids_ref.refs_1_), custom_call_target="tpu_custom_call" | custom-call | flops 1048576000 | bytes 524288 | tf_op jit(solution)/shard_map/bring_clouds/part_links/pallas_call | solution.py:276
  13.9 6.0 %first_tables.1 = (f32[1024,128]{1,0:T(8,128)S(1)}, f32[40,1024]{1,0:T(8,128)S(1)}, f32[1024,128]{1,0:T(8,128)S(1)}, f32[1024,128]{1,0:T(8,128)S(1)}, f32[1024,1...) custom-call(f32[104,256]{1,0:T(8,128)S(1)} %get-tuple-element.96.ids_ref.refs_0_, ...), custom_call_target="tpu_custom_call" | custom-call | tf_op jit(solution)/shard_map/layer_one/first_tables/pallas_call | solution.py:342
  20.0 1.7 collective-permute-start.5
  21.9 1.1 collective-permute-done.5
  23.0 2.3 %collective-permute-done.4 = f32[2,128]{1,0:T(2,128)S(1)} collective-permute-done((f32[2,128]{1,0:T(2,128)S(1)}, f32[2,128]{1,0:T(2,128)S(1)}, u32[]{:S(2)}, u32[]{:S(2)}) %collective-permute-start.4) | collective-permute-done | bytes 1056 | tf_op jit(solution)/shard_map/layer_one/ppermute | solution.py:41
  25.3 1.6 collective-permute-start.6
  26.9 2.2 %part_links.7.refs_3_ = bf16[1024,256]{1,0:T(8,128)(2,1)S(1)} custom-call(f32[104,256]{1,0:T(8,128)S(1)} %collective-permute-done.2.refs_3_.ids_ref), custom_call_target="tpu_custom_call" | custom-call | flops 524288000 | bytes 524288 | tf_op jit(solution)/shard_map/layer_one/part_links/pallas_call | solution.py:276
  29.1 3.7 %collective-permute-start.9 = (f32[2,128]{1,0:T(2,128)S(1)}, f32[2,128]{1,0:T(2,128)S(1)}, u32[]{:S(2)}, u32[]{:S(2)}) collective-permute-start(f32[2,128]{1,0:T(2,128)S(1)} %pad_maximum_fusion.5), channel_id=1, source_target_pairs={{0,24},{4,28},{8,16},{12,20},{16,8},{20,12},{24,0},{28,4},{1,25},{... | collective-permute-start | bytes 3080 | tf_op jit(solution)/shard_map/layer_one/ppermute | solution.py:41
  32.8 0.8 collective-permute-start.7
  33.5 2.2 %part_links.6.refs_2_ = bf16[1024,256]{1,0:T(8,128)(2,1)S(1)} custom-call(f32[104,256]{1,0:T(8,128)S(1)} %collective-permute-done.1.refs_2_.ids_ref), custom_call_target="tpu_custom_call" | custom-call | flops 524288000 | bytes 524288 | tf_op jit(solution)/shard_map/layer_one/part_links/pallas_call | solution.py:276
  35.7 1.5 collective-permute-done.8
  37.3 16.4 %edges.2 = (f32[1024,128]{1,0:T(8,128)S(1)}, f32[20,1024,128]{2,1,0:T(8,128)}, f32[1024,128]{1,0:T(8,128)S(1)}, f32[1024,128]{1,0:T(8,128)S(1)}, f32[1024,128]{1,0:T(8,128)S(1)}, /*index=5*/f32[1024,128]{1,0:T(8,128)S(1)}) custom-call(f32[1024,128]{1,0:T(8,128)S(1)} %get-tuple-element.103.x_ref, f32[1024,128]{1,0:T(8,128)S(1)} %get-tuple-element.104.a_ref, ...), custom_call_target="tpu_custom_call" | custom-call | tf_op jit(solution)/shard_map/layer_one/edges/pallas_call | solution.py:475
  53.7 2.6 %second_tables.1 = (f32[1024,256]{1,0:T(8,128)S(1)}, f32[1024,256]{1,0:T(8,128)S(1)}, f32[1024,256]{1,0:T(8,128)S(1)}, f32[1024,128]{1,0:T(8,128)S(1)}, f32[2,256]{1,0:T(2,128)S(1)}) custom-call(f32[1024,128]{1,0:T(8,128)S(1)} %get-tuple-element.108.x_ref, f32[256,256]{1,0:T(8,128)S(1)} %get-tuple-element.109.weight_ref, ...), custom_call_target="tpu_custom_call" | custom-call | tf_op jit(solution)/shard_map/layer_two/second_tables/pallas_call | solution.py:367
  56.4 0.6 collective-permute-start.11
  57.0 1.2 collective-permute-start.10
  58.2 1.1 collective-permute-done.12
  59.4 0.7 collective-permute-done.11
  60.0 1.5 collective-permute-start.13
  61.5 2.2 %collective-permute-done.13 = f32[2,256]{1,0:T(2,128)S(1)} collective-permute-done((f32[2,256]{1,0:T(2,128)S(1)}, f32[2,256]{1,0:T(2,128)S(1)}, u32[]{:S(2)}, u32[]{:S(2)}) %collective-permute-start.13) | collective-permute-done | bytes 2080 | tf_op jit(solution)/shard_map/layer_two/ppermute | solution.py:41
  63.7 2.2 %collective-permute-start.16 = (f32[2,256]{1,0:T(2,128)S(1)}, f32[2,256]{1,0:T(2,128)S(1)}, u32[]{:S(2)}, u32[]{:S(2)}) collective-permute-start(f32[2,256]{1,0:T(2,128)S(1)} %pad_maximum_fusion.2), channel_id=1, source_target_pairs={{0,24},{4,28},{8,16},{12,20},{16,8},{20,12},{24,0},{28,4},{1,25},{... | collective-permute-start | bytes 6152 | tf_op jit(solution)/shard_map/layer_two/ppermute | solution.py:41
  65.9 2.3 %collective-permute-start.14 = (f32[2,256]{1,0:T(2,128)S(1)}, f32[2,256]{1,0:T(2,128)S(1)}, u32[]{:S(2)}, u32[]{:S(2)}) collective-permute-start(f32[2,256]{1,0:T(2,128)S(1)} %pad_maximum_fusion.2), channel_id=1, source_target_pairs={{0,8},{4,12},{8,0},{12,4},{16,24},{20,28},{24,16},{28,20},{1,9},{5... | collective-permute-start | bytes 6152 | tf_op jit(solution)/shard_map/layer_two/ppermute | solution.py:41
  68.2 1.3 split.13
  69.6 0.6 collective-permute-start.18
  70.2 1.2 collective-permute-start.19
  71.5 30.5 %edges.3 = (f32[1024,256]{1,0:T(8,128)S(1)}, f32[20,1024,256]{2,1,0:T(8,128)}, f32[1024,256]{1,0:T(8,128)S(1)}, f32[1024,256]{1,0:T(8,128)S(1)}, f32[1024,256]{1,0:T(8,128)S(1)}, /*index=5*/f32[1024,256]{1,0:T(8,128)S(1)}) custom-call(f32[1024,128]{1,0:T(8,128)S(1)} %get-tuple-element.103.x_ref, f32[1024,256]{1,0:T(8,128)S(1)} %get-tuple-element.112.a_ref, ...), custom_call_target="tpu_custom_call" | custom-call | tf_op jit(solution)/shard_map/layer_two/edges/pallas_call | solution.py:475
  102.0 0.9 pools.1
  102.9 0.4 collective-permute-start.20
  103.3 0.6 collective-permute-start.21
  103.8 1.0 collective-permute-start.22
  104.8 16.2 %scatter.4.refs_0_ = f32[1024,256]{1,0:T(8,128)S(1)} custom-call(f32[40,1024]{1,0:T(8,128)S(1)} %get-tuple-element.134.ids_ref, f32[1024,256]{1,0:T(8,128)S(1)} %get-tuple-element.141.grad_ref, f32[20,1024,256]{2,1,0:T(8,128)} %get-tuple-element.136.weight_ref), custom_call_target="tpu_custom_call" | custom-call | flops 12884901888 | bytes 12582912 | tf_op jit(solution)/shard_map/layer_two_back/scatter/pallas_call | solution.py:567
  121.1 2.2 %collective-permute-start.25 = (f32[2,256]{1,0:T(2,128)S(1)}, f32[2,256]{1,0:T(2,128)S(1)}, u32[]{:S(2)}, u32[]{:S(2)}) collective-permute-start(f32[2,256]{1,0:T(2,128)S(1)} %add_add_fusion.5), channel_id=1, source_target_pairs={{0,24},{4,28},{8,16},{12,20},{16,8},{20,12},{24,0},{28,4},{1,25},{... | collective-permute-start | bytes 6152 | tf_op jit(solution)/shard_map/layer_two_back/ppermute | solution.py:41
  123.3 2.3 %collective-permute-start.23 = (f32[2,256]{1,0:T(2,128)S(1)}, f32[2,256]{1,0:T(2,128)S(1)}, u32[]{:S(2)}, u32[]{:S(2)}) collective-permute-start(f32[2,256]{1,0:T(2,128)S(1)} %add_add_fusion.5), channel_id=1, source_target_pairs={{0,8},{4,12},{8,0},{12,4},{16,24},{20,28},{24,16},{28,20},{1,9},{5... | collective-permute-start | bytes 6152 | tf_op jit(solution)/shard_map/layer_two_back/ppermute | solution.py:41
  125.6 11.5 %scatter.5.refs_1_ = f32[1024,256]{1,0:T(8,128)S(1)} custom-call(f32[40,1024]{1,0:T(8,128)S(1)} %get-tuple-element.134.ids_ref, f32[1024,256]{1,0:T(8,128)S(1)} %get-tuple-element.141.grad_ref, f32[20,1024,256]{2,1,0:T(8,128)} %get-tuple-element.136.weight_ref), custom_call_target="tpu_custom_call" | custom-call | flops 8589934592 | bytes 8388608 | tf_op jit(solution)/shard_map/layer_two_back/scatter/pallas_call | solution.py:567
  137.2 1.5 collective-permute-start.26
  138.6 2.2 %collective-permute-done.26 = f32[2,256]{1,0:T(2,128)S(1)} collective-permute-done((f32[2,256]{1,0:T(2,128)S(1)}, f32[2,256]{1,0:T(2,128)S(1)}, u32[]{:S(2)}, u32[]{:S(2)}) %collective-permute-start.26) | collective-permute-done | bytes 2080 | tf_op jit(solution)/shard_map/layer_two_back/ppermute | solution.py:41
  140.8 2.9 %middle.1 = (f32[72,256]{1,0:T(8,128)S(1)}, f32[72,256]{1,0:T(8,128)S(1)}, f32[72,256]{1,0:T(8,128)S(1)}, f32[72,256]{1,0:T(8,128)S(1)}, f32[1024,128]{1,0:T(8,1...) custom-call(s32[1]{0:T(128)} %bitcast.me_ref, f32[1024,256]{1,0:T(8,128)S(1)} %get-tuple-element.130.own_ref, ...), custom_call_target="tpu_custom_call" | custom-call | tf_op jit(solution)/shard_map/layer_two_back/middle/pallas_call | solution.py:662
  143.7 0.5 collective-permute-start.28
  144.3 1.3 collective-permute-start.29
  145.6 8.8 %scatter.6.refs_0_ = f32[1024,128]{1,0:T(8,128)S(1)} custom-call(f32[40,1024]{1,0:T(8,128)S(1)} %get-tuple-element.134.ids_ref, f32[1024,128]{1,0:T(8,128)S(1)} %get-tuple-element.163.grad_ref, f32[20,1024,128]{2,1,0:T(8,128)} %get-tuple-element.158.weight_ref), custom_call_target="tpu_custom_call" | custom-call | flops 6442450944 | bytes 6291456 | tf_op jit(solution)/shard_map/layer_one_back/scatter/pallas_call | solution.py:567
  154.5 2.2 %collective-permute-start.32 = (f32[72,256]{1,0:T(8,128)S(1)}, f32[72,256]{1,0:T(8,128)S(1)}, u32[]{:S(2)}, u32[]{:S(2)}) collective-permute-start(f32[72,256]{1,0:T(8,128)S(1)} %add_add_fusion.1), channel_id=1, source_target_pairs={{0,24},{4,28},{8,16},{12,20},{16,8},{20,12},{24,0},{28,4},{1,25},{... | collective-permute-start | bytes 221192 | tf_op jit(solution)/shard_map/layer_one_back/ppermute | solution.py:41
  156.7 2.3 %collective-permute-start.30 = (f32[72,256]{1,0:T(8,128)S(1)}, f32[72,256]{1,0:T(8,128)S(1)}, u32[]{:S(2)}, u32[]{:S(2)}) collective-permute-start(f32[72,256]{1,0:T(8,128)S(1)} %add_add_fusion.1), channel_id=1, source_target_pairs={{0,8},{4,12},{8,0},{12,4},{16,24},{20,28},{24,16},{28,20},{1,9},{5... | collective-permute-start | bytes 221192 | tf_op jit(solution)/shard_map/layer_one_back/ppermute | solution.py:41
  158.9 6.4 %scatter.7.refs_1_ = f32[1024,128]{1,0:T(8,128)S(1)} custom-call(f32[40,1024]{1,0:T(8,128)S(1)} %get-tuple-element.134.ids_ref, f32[1024,128]{1,0:T(8,128)S(1)} %get-tuple-element.163.grad_ref, f32[20,1024,128]{2,1,0:T(8,128)} %get-tuple-element.158.weight_ref), custom_call_target="tpu_custom_call" | custom-call | flops 4294967296 | bytes 4194304 | tf_op jit(solution)/shard_map/layer_one_back/scatter/pallas_call | solution.py:567
  165.4 1.5 collective-permute-start.33
  166.9 3.0 %collective-permute-done.33 = f32[72,256]{1,0:T(8,128)S(1)} collective-permute-done((f32[72,256]{1,0:T(8,128)S(1)}, f32[72,256]{1,0:T(8,128)S(1)}, u32[]{:S(2)}, u32[]{:S(2)}) %collective-permute-start.33) | collective-permute-done | bytes 73760 | tf_op jit(solution)/shard_map/layer_one_back/ppermute | solution.py:41
  169.9 1.6 last.1
  171.4 0.6 collective-permute-start.35
  172.0 1.3 collective-permute-start.34
  173.3 2.0 %collective-permute-done.36 = f32[64,256]{1,0:T(8,128)S(1)} collective-permute-done((f32[64,256]{1,0:T(8,128)S(1)}, f32[64,256]{1,0:T(8,128)S(1)}, u32[]{:S(2)}, u32[]{:S(2)}) %collective-permute-start.36) | collective-permute-done | bytes 65568 | tf_op jit(solution)/shard_map/layer_one_back/ppermute | solution.py:41
  175.3 1.1 collective-permute-done.35
  176.6 1.4 collective-permute-start.40
  178.0 1.0 unpack_output.1
  179.0 0.6 slice.183
  179.6 1.3 collective-permute-start.38
  181.1 2.2 %collective-permute-start.43 = (f32[64,256]{1,0:T(8,128)S(1)}, f32[64,256]{1,0:T(8,128)S(1)}, u32[]{:S(2)}, u32[]{:S(2)}) collective-permute-start(f32[64,256]{1,0:T(8,128)S(1)} %add.272), channel_id=1, source_target_pairs={{0,24},{4,28},{8,16},{12,20},{16,8},{20,12},{24,0},{28,4},{1,25},{... | collective-permute-start | bytes 196616 | tf_op jit(solution)/shard_map/layer_one_back/ppermute | solution.py:41
  183.2 2.3 %collective-permute-start.41 = (f32[64,256]{1,0:T(8,128)S(1)}, f32[64,256]{1,0:T(8,128)S(1)}, u32[]{:S(2)}, u32[]{:S(2)}) collective-permute-start(f32[64,256]{1,0:T(8,128)S(1)} %add.272), channel_id=1, source_target_pairs={{0,8},{4,12},{8,0},{12,4},{16,24},{20,28},{24,16},{28,20},{1,9},{5... | collective-permute-start | bytes 196616 | tf_op jit(solution)/shard_map/layer_one_back/ppermute | solution.py:41
  185.5 0.5 slice_bitcast_fusion
  186.0 1.0 collective-permute-done.39.refs_3_
  187.0 0.8 unpack_grad.1
  188.0 2.5 %collective-permute-done.42 = f32[64,256]{1,0:T(8,128)S(1)} collective-permute-done((f32[64,256]{1,0:T(8,128)S(1)}, f32[64,256]{1,0:T(8,128)S(1)}, u32[]{:S(2)}, u32[]{:S(2)}) %collective-permute-start.42) | collective-permute-done | bytes 65568 | tf_op jit(solution)/shard_map/layer_one_back/ppermute | solution.py:41
  190.5 0.6 pad_maximum_fusion
  (72 shorter events, 1.2 us)
Async XLA Ops:
  0.6 101.3 %copy-start.1 = (f32[4,256]{1,0:T(4,128)S(1)}, f32[4,256]{1,0:T(4,128)}, u32[]{:S(2)}) copy-start(f32[4,256]{1,0:T(4,128)} %gmean_ref.1) | copy-start | bytes 12292
  0.7 101.3 %copy-start = (f32[4,256]{1,0:T(4,128)S(1)}, f32[4,256]{1,0:T(4,128)}, u32[]{:S(2)}) copy-start(f32[4,256]{1,0:T(4,128)} %gmax_ref.1) | copy-start | bytes 12292
  2.1 7.5 %collective-permute-start = (f32[104,256]{1,0:T(8,128)S(1)}, f32[104,256]{1,0:T(8,128)S(1)}, u32[]{:S(2)}, u32[]{:S(2)}) collective-permute-start(f32[104,256]{1,0:T(8,128)S(1)} %get-tuple-element.97), channel_id=1, source_target_pairs={{0,1},{1,0},{2,3},{3,2},{4,5},{5,4},{6,7},{7,6},{8,9},{9,8},{10,11... | collective-permute-start | bytes 319496 | tf_op jit(solution)/shard_map/bring_clouds/ppermute | solution.py:41
  2.6 11.3 %collective-permute-start.1 = (f32[104,256]{1,0:T(8,128)S(1)}, f32[104,256]{1,0:T(8,128)S(1)}, u32[]{:S(2)}, u32[]{:S(2)}) collective-permute-start(f32[104,256]{1,0:T(8,128)S(1)} %get-tuple-element.98), channel_id=1, source_target_pairs={{0,2},{1,3},{2,0},{3,1},{4,6},{5,7},{6,4},{7,5},{8,10},{9,11},{10,... | collective-permute-start | bytes 319496 | tf_op jit(solution)/shard_map/bring_clouds/ppermute | solution.py:41
  5.2 8.7 %collective-permute-start.2 = (f32[104,256]{1,0:T(8,128)S(1)}, f32[104,256]{1,0:T(8,128)S(1)}, u32[]{:S(2)}, u32[]{:S(2)}) collective-permute-start(f32[104,256]{1,0:T(8,128)S(1)} %get-tuple-element.99), channel_id=1, source_target_pairs={{0,3},{1,2},{2,1},{3,0},{4,7},{5,6},{6,5},{7,4},{8,11},{9,10},{10,... | collective-permute-start | bytes 319496 | tf_op jit(solution)/shard_map/bring_clouds/ppermute | solution.py:41
  20.0 3.1 %collective-permute-start.5 = (f32[2,128]{1,0:T(2,128)S(1)}, f32[2,128]{1,0:T(2,128)S(1)}, u32[]{:S(2)}, u32[]{:S(2)}) collective-permute-start(f32[2,128]{1,0:T(2,128)S(1)} %get-tuple-element.106.local_ref), channel_id=1, source_target_pairs={{0,3},{1,2},{2,1},{3,0},{4,7},{5,6},{6,5},{7,4},{8,11},{9,10},{10,... | collective-permute-start | bytes 3080 | tf_op jit(solution)/shard_map/layer_one/ppermute | solution.py:41
  21.7 3.6 %collective-permute-start.4 = (f32[2,128]{1,0:T(2,128)S(1)}, f32[2,128]{1,0:T(2,128)S(1)}, u32[]{:S(2)}, u32[]{:S(2)}) collective-permute-start(f32[2,128]{1,0:T(2,128)S(1)} %get-tuple-element.106.local_ref), channel_id=1, source_target_pairs={{0,2},{1,3},{2,0},{3,1},{4,6},{5,7},{6,4},{7,5},{8,10},{9,11},{10,... | collective-permute-start | bytes 3080 | tf_op jit(solution)/shard_map/layer_one/ppermute | solution.py:41
  21.8 3.4 %collective-permute-start.3 = (f32[2,128]{1,0:T(2,128)S(1)}, f32[2,128]{1,0:T(2,128)S(1)}, u32[]{:S(2)}, u32[]{:S(2)}) collective-permute-start(f32[2,128]{1,0:T(2,128)S(1)} %get-tuple-element.106.local_ref), channel_id=1, source_target_pairs={{0,1},{1,0},{2,3},{3,2},{4,5},{5,4},{6,7},{7,6},{8,9},{9,8},{10,11... | collective-permute-start | bytes 3080 | tf_op jit(solution)/shard_map/layer_one/ppermute | solution.py:41
  25.3 3.7 %collective-permute-start.6 = (f32[2,128]{1,0:T(2,128)S(1)}, f32[2,128]{1,0:T(2,128)S(1)}, u32[]{:S(2)}, u32[]{:S(2)}) collective-permute-start(f32[2,128]{1,0:T(2,128)S(1)} %pad_maximum_fusion.4), channel_id=1, source_target_pairs={{0,4},{4,0},{8,12},{12,8},{16,20},{20,16},{24,28},{28,24},{1,5},{5... | collective-permute-start | bytes 3080 | tf_op jit(solution)/shard_map/layer_one/ppermute | solution.py:41
  29.1 6.6 %collective-permute-start.9 = (f32[2,128]{1,0:T(2,128)S(1)}, f32[2,128]{1,0:T(2,128)S(1)}, u32[]{:S(2)}, u32[]{:S(2)}) collective-permute-start(f32[2,128]{1,0:T(2,128)S(1)} %pad_maximum_fusion.5), channel_id=1, source_target_pairs={{0,24},{4,28},{8,16},{12,20},{16,8},{20,12},{24,0},{28,4},{1,25},{... | collective-permute-start | bytes 3080 | tf_op jit(solution)/shard_map/layer_one/ppermute | solution.py:41
  32.8 4.5 %collective-permute-start.8 = (f32[2,128]{1,0:T(2,128)S(1)}, f32[2,128]{1,0:T(2,128)S(1)}, u32[]{:S(2)}, u32[]{:S(2)}) collective-permute-start(f32[2,128]{1,0:T(2,128)S(1)} %pad_maximum_fusion.5), channel_id=1, source_target_pairs={{0,16},{4,20},{8,24},{12,28},{16,0},{20,4},{24,8},{28,12},{1,17},{... | collective-permute-start | bytes 3080 | tf_op jit(solution)/shard_map/layer_one/ppermute | solution.py:41
  32.8 4.5 %collective-permute-start.7 = (f32[2,128]{1,0:T(2,128)S(1)}, f32[2,128]{1,0:T(2,128)S(1)}, u32[]{:S(2)}, u32[]{:S(2)}) collective-permute-start(f32[2,128]{1,0:T(2,128)S(1)} %pad_maximum_fusion.5), channel_id=1, source_target_pairs={{0,8},{4,12},{8,0},{12,4},{16,24},{20,28},{24,16},{28,20},{1,9},{5... | collective-permute-start | bytes 3080 | tf_op jit(solution)/shard_map/layer_one/ppermute | solution.py:41
  56.3 3.1 %collective-permute-start.12 = (f32[2,256]{1,0:T(2,128)S(1)}, f32[2,256]{1,0:T(2,128)S(1)}, u32[]{:S(2)}, u32[]{:S(2)}) collective-permute-start(f32[2,256]{1,0:T(2,128)S(1)} %get-tuple-element.114.local_ref), channel_id=1, source_target_pairs={{0,3},{1,2},{2,1},{3,0},{4,7},{5,6},{6,5},{7,4},{8,11},{9,10},{10,... | collective-permute-start | bytes 6152 | tf_op jit(solution)/shard_map/layer_two/ppermute | solution.py:41
  56.4 3.7 %collective-permute-start.11 = (f32[2,256]{1,0:T(2,128)S(1)}, f32[2,256]{1,0:T(2,128)S(1)}, u32[]{:S(2)}, u32[]{:S(2)}) collective-permute-start(f32[2,256]{1,0:T(2,128)S(1)} %get-tuple-element.114.local_ref), channel_id=1, source_target_pairs={{0,2},{1,3},{2,0},{3,1},{4,6},{5,7},{6,4},{7,5},{8,10},{9,11},{10,... | collective-permute-start | bytes 6152 | tf_op jit(solution)/shard_map/layer_two/ppermute | solution.py:41
  57.0 3.1 %collective-permute-start.10 = (f32[2,256]{1,0:T(2,128)S(1)}, f32[2,256]{1,0:T(2,128)S(1)}, u32[]{:S(2)}, u32[]{:S(2)}) collective-permute-start(f32[2,256]{1,0:T(2,128)S(1)} %get-tuple-element.114.local_ref), channel_id=1, source_target_pairs={{0,1},{1,0},{2,3},{3,2},{4,5},{5,4},{6,7},{7,6},{8,9},{9,8},{10,11... | collective-permute-start | bytes 6152 | tf_op jit(solution)/shard_map/layer_two/ppermute | solution.py:41
  60.0 3.7 %collective-permute-start.13 = (f32[2,256]{1,0:T(2,128)S(1)}, f32[2,256]{1,0:T(2,128)S(1)}, u32[]{:S(2)}, u32[]{:S(2)}) collective-permute-start(f32[2,256]{1,0:T(2,128)S(1)} %pad_maximum_fusion.1), channel_id=1, source_target_pairs={{0,4},{4,0},{8,12},{12,8},{16,20},{20,16},{24,28},{28,24},{1,5},{5... | collective-permute-start | bytes 6152 | tf_op jit(solution)/shard_map/layer_two/ppermute | solution.py:41
  63.7 6.4 %collective-permute-start.16 = (f32[2,256]{1,0:T(2,128)S(1)}, f32[2,256]{1,0:T(2,128)S(1)}, u32[]{:S(2)}, u32[]{:S(2)}) collective-permute-start(f32[2,256]{1,0:T(2,128)S(1)} %pad_maximum_fusion.2), channel_id=1, source_target_pairs={{0,24},{4,28},{8,16},{12,20},{16,8},{20,12},{24,0},{28,4},{1,25},{... | collective-permute-start | bytes 6152 | tf_op jit(solution)/shard_map/layer_two/ppermute | solution.py:41
  65.9 5.5 %collective-permute-start.15 = (f32[2,256]{1,0:T(2,128)S(1)}, f32[2,256]{1,0:T(2,128)S(1)}, u32[]{:S(2)}, u32[]{:S(2)}) collective-permute-start(f32[2,256]{1,0:T(2,128)S(1)} %pad_maximum_fusion.2), channel_id=1, source_target_pairs={{0,16},{4,20},{8,24},{12,28},{16,0},{20,4},{24,8},{28,12},{1,17},{... | collective-permute-start | bytes 6152 | tf_op jit(solution)/shard_map/layer_two/ppermute | solution.py:41
  65.9 5.5 %collective-permute-start.14 = (f32[2,256]{1,0:T(2,128)S(1)}, f32[2,256]{1,0:T(2,128)S(1)}, u32[]{:S(2)}, u32[]{:S(2)}) collective-permute-start(f32[2,256]{1,0:T(2,128)S(1)} %pad_maximum_fusion.2), channel_id=1, source_target_pairs={{0,8},{4,12},{8,0},{12,4},{16,24},{20,28},{24,16},{28,20},{1,9},{5... | collective-permute-start | bytes 6152 | tf_op jit(solution)/shard_map/layer_two/ppermute | solution.py:41
  69.5 32.5 %collective-permute-start.17 = (f32[256,256]{1,0:T(8,128)S(1)}, f32[256,256]{1,0:T(8,128)S(1)}, u32[]{:S(2)}, u32[]{:S(2)}) collective-permute-start(f32[256,256]{1,0:T(8,128)S(1)} %get-tuple-element.120), channel_id=1, source_target_pairs={{0,1},{1,0},{2,3},{3,2},{4,5},{5,4},{6,7},{7,6},{8,9},{9,8},{10,11... | collective-permute-start | bytes 786440 | tf_op jit(solution)/shard_map/bring_cotangents/ppermute | solution.py:41
  69.6 32.4 %collective-permute-start.18 = (f32[256,256]{1,0:T(8,128)S(1)}, f32[256,256]{1,0:T(8,128)S(1)}, u32[]{:S(2)}, u32[]{:S(2)}) collective-permute-start(f32[256,256]{1,0:T(8,128)S(1)} %get-tuple-element.121), channel_id=1, source_target_pairs={{0,2},{1,3},{2,0},{3,1},{4,6},{5,7},{6,4},{7,5},{8,10},{9,11},{10,... | collective-permute-start | bytes 786440 | tf_op jit(solution)/shard_map/bring_cotangents/ppermute | solution.py:41
  70.2 31.8 %collective-permute-start.19 = (f32[256,256]{1,0:T(8,128)S(1)}, f32[256,256]{1,0:T(8,128)S(1)}, u32[]{:S(2)}, u32[]{:S(2)}) collective-permute-start(f32[256,256]{1,0:T(8,128)S(1)} %get-tuple-element.122), channel_id=1, source_target_pairs={{0,3},{1,2},{2,1},{3,0},{4,7},{5,6},{6,5},{7,4},{8,11},{9,10},{10,... | collective-permute-start | bytes 786440 | tf_op jit(solution)/shard_map/bring_cotangents/ppermute | solution.py:41
  102.9 18.2 %collective-permute-start.20 = (f32[264,256]{1,0:T(8,128)S(1)}, f32[264,256]{1,0:T(8,128)S(1)}, u32[]{:S(2)}, u32[]{:S(2)}) collective-permute-start(f32[264,256]{1,0:T(8,128)S(1)} %get-tuple-element.124), channel_id=1, source_target_pairs={{0,1},{1,0},{2,3},{3,2},{4,5},{5,4},{6,7},{7,6},{8,9},{9,8},{10,11... | collective-permute-start | bytes 811016 | tf_op jit(solution)/shard_map/pools/ppermute | solution.py:41
  103.3 17.8 %collective-permute-start.21 = (f32[264,256]{1,0:T(8,128)S(1)}, f32[264,256]{1,0:T(8,128)S(1)}, u32[]{:S(2)}, u32[]{:S(2)}) collective-permute-start(f32[264,256]{1,0:T(8,128)S(1)} %get-tuple-element.125), channel_id=1, source_target_pairs={{0,2},{1,3},{2,0},{3,1},{4,6},{5,7},{6,4},{7,5},{8,10},{9,11},{10,... | collective-permute-start | bytes 811016 | tf_op jit(solution)/shard_map/pools/ppermute | solution.py:41
  103.8 17.2 %collective-permute-start.22 = (f32[264,256]{1,0:T(8,128)S(1)}, f32[264,256]{1,0:T(8,128)S(1)}, u32[]{:S(2)}, u32[]{:S(2)}) collective-permute-start(f32[264,256]{1,0:T(8,128)S(1)} %get-tuple-element.126), channel_id=1, source_target_pairs={{0,3},{1,2},{2,1},{3,0},{4,7},{5,6},{6,5},{7,4},{8,11},{9,10},{10,... | collective-permute-start | bytes 811016 | tf_op jit(solution)/shard_map/pools/ppermute | solution.py:41
  121.1 16.0 %collective-permute-start.25 = (f32[2,256]{1,0:T(2,128)S(1)}, f32[2,256]{1,0:T(2,128)S(1)}, u32[]{:S(2)}, u32[]{:S(2)}) collective-permute-start(f32[2,256]{1,0:T(2,128)S(1)} %add_add_fusion.5), channel_id=1, source_target_pairs={{0,24},{4,28},{8,16},{12,20},{16,8},{20,12},{24,0},{28,4},{1,25},{... | collective-permute-start | bytes 6152 | tf_op jit(solution)/shard_map/layer_two_back/ppermute | solution.py:41
  123.3 13.8 %collective-permute-start.24 = (f32[2,256]{1,0:T(2,128)S(1)}, f32[2,256]{1,0:T(2,128)S(1)}, u32[]{:S(2)}, u32[]{:S(2)}) collective-permute-start(f32[2,256]{1,0:T(2,128)S(1)} %add_add_fusion.5), channel_id=1, source_target_pairs={{0,16},{4,20},{8,24},{12,28},{16,0},{20,4},{24,8},{28,12},{1,17},{... | collective-permute-start | bytes 6152 | tf_op jit(solution)/shard_map/layer_two_back/ppermute | solution.py:41
  123.3 13.8 %collective-permute-start.23 = (f32[2,256]{1,0:T(2,128)S(1)}, f32[2,256]{1,0:T(2,128)S(1)}, u32[]{:S(2)}, u32[]{:S(2)}) collective-permute-start(f32[2,256]{1,0:T(2,128)S(1)} %add_add_fusion.5), channel_id=1, source_target_pairs={{0,8},{4,12},{8,0},{12,4},{16,24},{20,28},{24,16},{28,20},{1,9},{5... | collective-permute-start | bytes 6152 | tf_op jit(solution)/shard_map/layer_two_back/ppermute | solution.py:41
  137.2 3.7 %collective-permute-start.26 = (f32[2,256]{1,0:T(2,128)S(1)}, f32[2,256]{1,0:T(2,128)S(1)}, u32[]{:S(2)}, u32[]{:S(2)}) collective-permute-start(f32[2,256]{1,0:T(2,128)S(1)} %add_add_fusion.4), channel_id=1, source_target_pairs={{0,4},{4,0},{8,12},{12,8},{16,20},{20,16},{24,28},{28,24},{1,5},{5... | collective-permute-start | bytes 6152 | tf_op jit(solution)/shard_map/layer_two_back/ppermute | solution.py:41
  143.7 10.7 %collective-permute-start.27 = (f32[72,256]{1,0:T(8,128)S(1)}, f32[72,256]{1,0:T(8,128)S(1)}, u32[]{:S(2)}, u32[]{:S(2)}) collective-permute-start(f32[72,256]{1,0:T(8,128)S(1)} %get-tuple-element.154), channel_id=1, source_target_pairs={{0,1},{1,0},{2,3},{3,2},{4,5},{5,4},{6,7},{7,6},{8,9},{9,8},{10,11... | collective-permute-start | bytes 221192 | tf_op jit(solution)/shard_map/layer_one_back/ppermute | solution.py:41
  143.7 10.7 %collective-permute-start.28 = (f32[72,256]{1,0:T(8,128)S(1)}, f32[72,256]{1,0:T(8,128)S(1)}, u32[]{:S(2)}, u32[]{:S(2)}) collective-permute-start(f32[72,256]{1,0:T(8,128)S(1)} %get-tuple-element.155), channel_id=1, source_target_pairs={{0,2},{1,3},{2,0},{3,1},{4,6},{5,7},{6,4},{7,5},{8,10},{9,11},{10,... | collective-permute-start | bytes 221192 | tf_op jit(solution)/shard_map/layer_one_back/ppermute | solution.py:41
  144.3 10.2 %collective-permute-start.29 = (f32[72,256]{1,0:T(8,128)S(1)}, f32[72,256]{1,0:T(8,128)S(1)}, u32[]{:S(2)}, u32[]{:S(2)}) collective-permute-start(f32[72,256]{1,0:T(8,128)S(1)} %get-tuple-element.156), channel_id=1, source_target_pairs={{0,3},{1,2},{2,1},{3,0},{4,7},{5,6},{6,5},{7,4},{8,11},{9,10},{10,... | collective-permute-start | bytes 221192 | tf_op jit(solution)/shard_map/layer_one_back/ppermute | solution.py:41
  154.5 10.9 %collective-permute-start.32 = (f32[72,256]{1,0:T(8,128)S(1)}, f32[72,256]{1,0:T(8,128)S(1)}, u32[]{:S(2)}, u32[]{:S(2)}) collective-permute-start(f32[72,256]{1,0:T(8,128)S(1)} %add_add_fusion.1), channel_id=1, source_target_pairs={{0,24},{4,28},{8,16},{12,20},{16,8},{20,12},{24,0},{28,4},{1,25},{... | collective-permute-start | bytes 221192 | tf_op jit(solution)/shard_map/layer_one_back/ppermute | solution.py:41
  156.7 8.7 %collective-permute-start.31 = (f32[72,256]{1,0:T(8,128)S(1)}, f32[72,256]{1,0:T(8,128)S(1)}, u32[]{:S(2)}, u32[]{:S(2)}) collective-permute-start(f32[72,256]{1,0:T(8,128)S(1)} %add_add_fusion.1), channel_id=1, source_target_pairs={{0,16},{4,20},{8,24},{12,28},{16,0},{20,4},{24,8},{28,12},{1,17},{... | collective-permute-start | bytes 221192 | tf_op jit(solution)/shard_map/layer_one_back/ppermute | solution.py:41
  156.7 8.7 %collective-permute-start.30 = (f32[72,256]{1,0:T(8,128)S(1)}, f32[72,256]{1,0:T(8,128)S(1)}, u32[]{:S(2)}, u32[]{:S(2)}) collective-permute-start(f32[72,256]{1,0:T(8,128)S(1)} %add_add_fusion.1), channel_id=1, source_target_pairs={{0,8},{4,12},{8,0},{12,4},{16,24},{20,28},{24,16},{28,20},{1,9},{5... | collective-permute-start | bytes 221192 | tf_op jit(solution)/shard_map/layer_one_back/ppermute | solution.py:41
  165.4 4.4 %collective-permute-start.33 = (f32[72,256]{1,0:T(8,128)S(1)}, f32[72,256]{1,0:T(8,128)S(1)}, u32[]{:S(2)}, u32[]{:S(2)}) collective-permute-start(f32[72,256]{1,0:T(8,128)S(1)} %add_add_fusion), channel_id=1, source_target_pairs={{0,4},{4,0},{8,12},{12,8},{16,20},{20,16},{24,28},{28,24},{1,5},{5... | collective-permute-start | bytes 221192 | tf_op jit(solution)/shard_map/layer_one_back/ppermute | solution.py:41
  171.4 3.8 %collective-permute-start.36 = (f32[64,256]{1,0:T(8,128)S(1)}, f32[64,256]{1,0:T(8,128)S(1)}, u32[]{:S(2)}, u32[]{:S(2)}) collective-permute-start(f32[64,256]{1,0:T(8,128)S(1)} %get-tuple-element.168), channel_id=1, source_target_pairs={{0,3},{1,2},{2,1},{3,0},{4,7},{5,6},{6,5},{7,4},{8,11},{9,10},{10,... | collective-permute-start | bytes 196616 | tf_op jit(solution)/shard_map/layer_one_back/ppermute | solution.py:41
  171.4 4.9 %collective-permute-start.35 = (f32[64,256]{1,0:T(8,128)S(1)}, f32[64,256]{1,0:T(8,128)S(1)}, u32[]{:S(2)}, u32[]{:S(2)}) collective-permute-start(f32[64,256]{1,0:T(8,128)S(1)} %get-tuple-element.168), channel_id=1, source_target_pairs={{0,2},{1,3},{2,0},{3,1},{4,6},{5,7},{6,4},{7,5},{8,10},{9,11},{10,... | collective-permute-start | bytes 196616 | tf_op jit(solution)/shard_map/layer_one_back/ppermute | solution.py:41
  172.0 4.4 %collective-permute-start.34 = (f32[64,256]{1,0:T(8,128)S(1)}, f32[64,256]{1,0:T(8,128)S(1)}, u32[]{:S(2)}, u32[]{:S(2)}) collective-permute-start(f32[64,256]{1,0:T(8,128)S(1)} %get-tuple-element.168), channel_id=1, source_target_pairs={{0,1},{1,0},{2,3},{3,2},{4,5},{5,4},{6,7},{7,6},{8,9},{9,8},{10,11... | collective-permute-start | bytes 196616 | tf_op jit(solution)/shard_map/layer_one_back/ppermute | solution.py:41
  176.4 6.8 %collective-permute-start.37 = (f32[128,256]{1,0:T(8,128)S(1)}, f32[128,256]{1,0:T(8,128)S(1)}, u32[]{:S(2)}, u32[]{:S(2)}) collective-permute-start(f32[128,256]{1,0:T(8,128)S(1)} %get-tuple-element.174), channel_id=1, source_target_pairs={{0,1},{1,0},{2,3},{3,2},{4,5},{5,4},{6,7},{7,6},{8,9},{9,8},{10,11... | collective-permute-start | bytes 393224 | tf_op jit(solution)/shard_map/layer_one_back/ppermute | solution.py:41
  176.6 4.5 %collective-permute-start.40 = (f32[64,256]{1,0:T(8,128)S(1)}, f32[64,256]{1,0:T(8,128)S(1)}, u32[]{:S(2)}, u32[]{:S(2)}) collective-permute-start(f32[64,256]{1,0:T(8,128)S(1)} %add_add_fusion.3), channel_id=1, source_target_pairs={{0,4},{4,0},{8,12},{12,8},{16,20},{20,16},{24,28},{28,24},{1,5},{5... | collective-permute-start | bytes 196616 | tf_op jit(solution)/shard_map/layer_one_back/ppermute | solution.py:41
  179.6 6.4 %collective-permute-start.38 = (f32[128,256]{1,0:T(8,128)S(1)}, f32[128,256]{1,0:T(8,128)S(1)}, u32[]{:S(2)}, u32[]{:S(2)}) collective-permute-start(f32[128,256]{1,0:T(8,128)S(1)} %get-tuple-element.175), channel_id=1, source_target_pairs={{0,2},{1,3},{2,0},{3,1},{4,6},{5,7},{6,4},{7,5},{8,10},{9,11},{10,... | collective-permute-start | bytes 393224 | tf_op jit(solution)/shard_map/layer_one_back/ppermute | solution.py:41
  180.9 6.1 %collective-permute-start.39 = (f32[128,256]{1,0:T(8,128)S(1)}, f32[128,256]{1,0:T(8,128)S(1)}, u32[]{:S(2)}, u32[]{:S(2)}) collective-permute-start(f32[128,256]{1,0:T(8,128)S(1)} %get-tuple-element.176), channel_id=1, source_target_pairs={{0,3},{1,2},{2,1},{3,0},{4,7},{5,6},{6,5},{7,4},{8,11},{9,10},{10,... | collective-permute-start | bytes 393224 | tf_op jit(solution)/shard_map/layer_one_back/ppermute | solution.py:41
  181.1 6.9 %collective-permute-start.43 = (f32[64,256]{1,0:T(8,128)S(1)}, f32[64,256]{1,0:T(8,128)S(1)}, u32[]{:S(2)}, u32[]{:S(2)}) collective-permute-start(f32[64,256]{1,0:T(8,128)S(1)} %add.272), channel_id=1, source_target_pairs={{0,24},{4,28},{8,16},{12,20},{16,8},{20,12},{24,0},{28,4},{1,25},{... | collective-permute-start | bytes 196616 | tf_op jit(solution)/shard_map/layer_one_back/ppermute | solution.py:41
  183.2 7.2 %collective-permute-start.42 = (f32[64,256]{1,0:T(8,128)S(1)}, f32[64,256]{1,0:T(8,128)S(1)}, u32[]{:S(2)}, u32[]{:S(2)}) collective-permute-start(f32[64,256]{1,0:T(8,128)S(1)} %add.272), channel_id=1, source_target_pairs={{0,16},{4,20},{8,24},{12,28},{16,0},{20,4},{24,8},{28,12},{1,17},{... | collective-permute-start | bytes 196616 | tf_op jit(solution)/shard_map/layer_one_back/ppermute | solution.py:41
  183.2 7.2 %collective-permute-start.41 = (f32[64,256]{1,0:T(8,128)S(1)}, f32[64,256]{1,0:T(8,128)S(1)}, u32[]{:S(2)}, u32[]{:S(2)}) collective-permute-start(f32[64,256]{1,0:T(8,128)S(1)} %add.272), channel_id=1, source_target_pairs={{0,8},{4,12},{8,0},{12,4},{16,24},{20,28},{24,16},{28,20},{1,9},{5... | collective-permute-start | bytes 196616 | tf_op jit(solution)/shard_map/layer_one_back/ppermute | solution.py:41
where the time goes:
time: 191 us
  Pallas kernels  121 us (63%)
  starting transfers between devices  45.9 us (24%)
  waiting for transfers between devices  20.8 us (11%)
    pallas_call x2, Pallas kernels, edge_forward(): pl.pallas_call(functools.partial(edge_kernel, edges, layer, slots, first,...  46.9 us
    ppermute x44, starting transfers between devices, exchange(): return lax.ppermute(x, axes, [(i, i ^ mask) for i in range(size)])  45.9 us
    pallas_call x4, Pallas kernels, scatter(): pl.pallas_call(functools.partial(scatter_kernel, first + start, group), g...  43 us
    ppermute x44, waiting for transfers between devices, exchange(): return lax.ppermute(x, axes, [(i, i ^ mask) for i in range(size)])  20.8 us
    pallas_call x4, Pallas kernels, part_links(): pl.pallas_call(functools.partial(links_kernel, firsts, slots), out_shape=...  13 us
    pallas_call x1, Pallas kernels, first_tables(): pl.pallas_call(functools.partial(first_kernel, slots, width, count), out_...  6.04 us
  transfers between devices with their start and end apart: 44, of which 13 were waited for; matrix products, arithmetic and copies ran while one was open for 1% of the time, Pallas kernels for 47%

commit v1 on v0

--- a/solution.py
+++ b/solution.py
@@ -243,25 +243,30 @@
 
 def count_links(ids_ref, first, slots, wide, links):
     points, columns = links.shape
-    block = 256
-    here = lax.broadcasted_iota(jnp.int32, (16, columns), 0).astype(jnp.bfloat16)
-    one = jnp.ones((16, columns), jnp.bfloat16)
-    zero = jnp.zeros((16, columns), jnp.bfloat16)
+    block, rows, groups = 256, 16, 4
+    here = lax.broadcasted_iota(jnp.int32, (rows, columns), 0).astype(jnp.bfloat16)
+    one = jnp.ones((rows, columns), jnp.bfloat16)
+    zero = jnp.zeros((rows, columns), jnp.bfloat16)
     for start in range(0, points, block):
         for k in range(slots):
             local = ids_ref[first + k : first + k + 1, :] - float(start)
-            local = jnp.where((local >= 0) & (local < block), local, -1.0)
-            wide[k] = jnp.broadcast_to(local, (16, columns)).astype(jnp.bfloat16)
-
-        def sixteen(step, carry):
-            row = here + (step * 16).astype(jnp.float32).astype(jnp.bfloat16)
-            total = zero
+            wide[k] = jnp.broadcast_to(local, (rows, columns)).astype(jnp.bfloat16)
+
+        def some(step, carry):
+            base = step * (rows * groups)
+            names = [here + (base + g * rows).astype(jnp.float32).astype(jnp.bfloat16) for g in range(groups)]
+            totals = [zero] * groups
             for k in range(slots):
-                total = total + jnp.where(wide[k] == row, one, zero)
-            links[pl.ds(pl.multiple_of(start + step * 16, 16), 16), :] = total
+                ids = wide[k]
+                totals = [
+                    total + jnp.where(ids == name, one, zero) for total, name in zip(totals, names)
+                ]
+            for g in range(groups):
+                at = pl.ds(pl.multiple_of(start + base + g * rows, rows), rows)
+                links[at, :] = totals[g]
             return carry
 
-        lax.fori_loop(0, block // 16, sixteen, 0)
+        lax.fori_loop(0, block // (rows * groups), some, 0)
 
 
 def links_kernel(firsts, slots, ids_ref, *refs):

time: 191 us -> 186 us (0.974)
  Pallas kernels: 121 us -> 115 us
    pallas_call x4, Pallas kernels: 13 us -> 7.93 us  [part_links(): pl.pallas_call(functools.partial(links_kernel, firsts, slots), out_shape=...]
  transfers between devices with their start and end apart: 44 -> 44, of which waited for: 13 -> 15; matrix products, arithmetic and copies ran while one was open for 1% -> 1% of each run, Pallas kernels for 47% -> 45%
where the time goes in v1:
time: 186 us
  Pallas kernels  115 us (62%)
  starting transfers between devices  46.4 us (25%)
  waiting for transfers between devices  21.9 us (12%)
    pallas_call x2, Pallas kernels, edge_forward(): pl.pallas_call(functools.partial(edge_kernel, edges, layer, slots, first,...  46.9 us
    ppermute x44, starting transfers between devices, exchange(): return lax.ppermute(x, axes, [(i, i ^ mask) for i in range(size)])  46.4 us
    pallas_call x4, Pallas kernels, scatter(): pl.pallas_call(functools.partial(scatter_kernel, first + start, group), g...  43 us
    ppermute x44, waiting for transfers between devices, exchange(): return lax.ppermute(x, axes, [(i, i ^ mask) for i in range(size)])  21.9 us
    pallas_call x4, Pallas kernels, part_links(): pl.pallas_call(functools.partial(links_kernel, firsts, slots), out_shape=...  7.93 us
    pallas_call x1, Pallas kernels, first_tables(): pl.pallas_call(functools.partial(first_kernel, slots, width, count), out_...  4.37 us
  transfers between devices with their start and end apart: 44, of which 15 were waited for; matrix products, arithmetic and copies ran while one was open for 1% of the time, Pallas kernels for 45%

profile of v1, /device:TPU:0, one launch (start us, length us, event | category | flops | bytes accessed | tf_op | source)
XLA Modules:
  0.0 186.1 jit_solution(14622591770014339116)
XLA Ops:
  0.7 1.4 pack.1
  2.1 0.5 collective-permute-start
  2.6 2.6 %collective-permute-start.1 = (f32[104,256]{1,0:T(8,128)S(1)}, f32[104,256]{1,0:T(8,128)S(1)}, u32[]{:S(2)}, u32[]{:S(2)}) collective-permute-start(f32[104,256]{1,0:T(8,128)S(1)} %get-tuple-element.98), channel_id=1, source_target_pairs={{0,2},{1,3},{2,0},{3,1},{4,6},{5,7},{6,4},{7,5},{8,10},{9,11},{10,... | collective-permute-start | bytes 319496 | tf_op jit(solution)/shard_map/bring_clouds/ppermute | solution.py:41
  5.2 2.6 %part_links.4 = (bf16[1024,256]{1,0:T(8,128)(2,1)S(1)}, bf16[1024,256]{1,0:T(8,128)(2,1)S(1)}) custom-call(f32[104,256]{1,0:T(8,128)S(1)} %get-tuple-element.96.ids_ref.refs_0_), custom_call_target="tpu_custom_call" | custom-call | flops 1048576000 | bytes 524288 | tf_op jit(solution)/shard_map/bring_clouds/part_links/pallas_call | solution.py:281
  7.9 2.6 %part_links.5 = (bf16[1024,256]{1,0:T(8,128)(2,1)S(1)}, bf16[1024,256]{1,0:T(8,128)(2,1)S(1)}) custom-call(f32[104,256]{1,0:T(8,128)S(1)} %collective-permute-done.ids_ref.refs_1_), custom_call_target="tpu_custom_call" | custom-call | flops 1048576000 | bytes 524288 | tf_op jit(solution)/shard_map/bring_clouds/part_links/pallas_call | solution.py:281
  10.8 4.4 %first_tables.1 = (f32[1024,128]{1,0:T(8,128)S(1)}, f32[40,1024]{1,0:T(8,128)S(1)}, f32[1024,128]{1,0:T(8,128)S(1)}, f32[1024,128]{1,0:T(8,128)S(1)}, f32[1024,1...) custom-call(f32[104,256]{1,0:T(8,128)S(1)} %get-tuple-element.96.ids_ref.refs_0_, ...), custom_call_target="tpu_custom_call" | custom-call | tf_op jit(solution)/shard_map/layer_one/first_tables/pallas_call | solution.py:347
  15.1 1.6 collective-permute-start.5
  17.1 1.1 collective-permute-done.5
  18.2 2.1 %collective-permute-done.4 = f32[2,128]{1,0:T(2,128)S(1)} collective-permute-done((f32[2,128]{1,0:T(2,128)S(1)}, f32[2,128]{1,0:T(2,128)S(1)}, u32[]{:S(2)}, u32[]{:S(2)}) %collective-permute-start.4) | collective-permute-done | bytes 1056 | tf_op jit(solution)/shard_map/layer_one/ppermute | solution.py:41
  20.3 1.6 collective-permute-start.6
  21.9 1.3 part_links.7.refs_3_
  23.2 0.7 collective-permute-done.6
  24.0 3.7 %collective-permute-start.9 = (f32[2,128]{1,0:T(2,128)S(1)}, f32[2,128]{1,0:T(2,128)S(1)}, u32[]{:S(2)}, u32[]{:S(2)}) collective-permute-start(f32[2,128]{1,0:T(2,128)S(1)} %pad_maximum_fusion.5), channel_id=1, source_target_pairs={{0,24},{4,28},{8,16},{12,20},{16,8},{20,12},{24,0},{28,4},{1,25},{... | collective-permute-start | bytes 3080 | tf_op jit(solution)/shard_map/layer_one/ppermute | solution.py:41
  27.6 0.8 collective-permute-start.7
  28.4 1.3 part_links.6.refs_2_
  29.7 2.3 %collective-permute-done.8 = f32[2,128]{1,0:T(2,128)S(1)} collective-permute-done((f32[2,128]{1,0:T(2,128)S(1)}, f32[2,128]{1,0:T(2,128)S(1)}, u32[]{:S(2)}, u32[]{:S(2)}) %collective-permute-start.8) | collective-permute-done | bytes 1056 | tf_op jit(solution)/shard_map/layer_one/ppermute | solution.py:41
  32.1 16.4 %edges.2 = (f32[1024,128]{1,0:T(8,128)S(1)}, f32[20,1024,128]{2,1,0:T(8,128)}, f32[1024,128]{1,0:T(8,128)S(1)}, f32[1024,128]{1,0:T(8,128)S(1)}, f32[1024,128]{1,0:T(8,128)S(1)}, /*index=5*/f32[1024,128]{1,0:T(8,128)S(1)}) custom-call(f32[1024,128]{1,0:T(8,128)S(1)} %get-tuple-element.103.x_ref, f32[1024,128]{1,0:T(8,128)S(1)} %get-tuple-element.104.a_ref, ...), custom_call_target="tpu_custom_call" | custom-call | tf_op jit(solution)/shard_map/layer_one/edges/pallas_call | solution.py:480
  48.5 2.6 %second_tables.1 = (f32[1024,256]{1,0:T(8,128)S(1)}, f32[1024,256]{1,0:T(8,128)S(1)}, f32[1024,256]{1,0:T(8,128)S(1)}, f32[1024,128]{1,0:T(8,128)S(1)}, f32[2,256]{1,0:T(2,128)S(1)}) custom-call(f32[1024,128]{1,0:T(8,128)S(1)} %get-tuple-element.108.x_ref, f32[256,256]{1,0:T(8,128)S(1)} %get-tuple-element.109.weight_ref, ...), custom_call_target="tpu_custom_call" | custom-call | tf_op jit(solution)/shard_map/layer_two/second_tables/pallas_call | solution.py:372
  51.2 0.6 collective-permute-start.11
  51.8 1.2 collective-permute-start.10
  53.1 1.1 collective-permute-done.12
  54.2 0.7 collective-permute-done.11
  54.9 1.6 collective-permute-start.13
  56.5 2.1 %collective-permute-done.13 = f32[2,256]{1,0:T(2,128)S(1)} collective-permute-done((f32[2,256]{1,0:T(2,128)S(1)}, f32[2,256]{1,0:T(2,128)S(1)}, u32[]{:S(2)}, u32[]{:S(2)}) %collective-permute-start.13) | collective-permute-done | bytes 2080 | tf_op jit(solution)/shard_map/layer_two/ppermute | solution.py:41
  58.6 1.5 collective-permute-start.16
  60.1 0.6 collective-permute-start.15
  60.8 2.3 %collective-permute-start.14 = (f32[2,256]{1,0:T(2,128)S(1)}, f32[2,256]{1,0:T(2,128)S(1)}, u32[]{:S(2)}, u32[]{:S(2)}) collective-permute-start(f32[2,256]{1,0:T(2,128)S(1)} %pad_maximum_fusion.2), channel_id=1, source_target_pairs={{0,8},{4,12},{8,0},{12,4},{16,24},{20,28},{24,16},{28,20},{1,9},{5... | collective-permute-start | bytes 6152 | tf_op jit(solution)/shard_map/layer_two/ppermute | solution.py:41
  63.0 1.3 split.13
  64.4 0.6 collective-permute-start.18
  65.0 1.2 collective-permute-start.19
  66.3 30.5 %edges.3 = (f32[1024,256]{1,0:T(8,128)S(1)}, f32[20,1024,256]{2,1,0:T(8,128)}, f32[1024,256]{1,0:T(8,128)S(1)}, f32[1024,256]{1,0:T(8,128)S(1)}, f32[1024,256]{1,0:T(8,128)S(1)}, /*index=5*/f32[1024,256]{1,0:T(8,128)S(1)}) custom-call(f32[1024,128]{1,0:T(8,128)S(1)} %get-tuple-element.103.x_ref, f32[1024,256]{1,0:T(8,128)S(1)} %get-tuple-element.112.a_ref, ...), custom_call_target="tpu_custom_call" | custom-call | tf_op jit(solution)/shard_map/layer_two/edges/pallas_call | solution.py:480
  96.8 0.9 pools.1
  98.1 0.6 collective-permute-start.21
  98.7 1.0 collective-permute-start.22
  99.7 16.2 %scatter.4.refs_0_ = f32[1024,256]{1,0:T(8,128)S(1)} custom-call(f32[40,1024]{1,0:T(8,128)S(1)} %get-tuple-element.134.ids_ref, f32[1024,256]{1,0:T(8,128)S(1)} %get-tuple-element.141.grad_ref, f32[20,1024,256]{2,1,0:T(8,128)} %get-tuple-element.136.weight_ref), custom_call_target="tpu_custom_call" | custom-call | flops 12884901888 | bytes 12582912 | tf_op jit(solution)/shard_map/layer_two_back/scatter/pallas_call | solution.py:572
  116.0 1.5 collective-permute-start.25
  117.8 2.6 %collective-permute-start.23 = (f32[2,256]{1,0:T(2,128)S(1)}, f32[2,256]{1,0:T(2,128)S(1)}, u32[]{:S(2)}, u32[]{:S(2)}) collective-permute-start(f32[2,256]{1,0:T(2,128)S(1)} %add_add_fusion.5), channel_id=1, source_target_pairs={{0,8},{4,12},{8,0},{12,4},{16,24},{20,28},{24,16},{28,20},{1,9},{5... | collective-permute-start | bytes 6152 | tf_op jit(solution)/shard_map/layer_two_back/ppermute | solution.py:41
  120.4 11.5 %scatter.5.refs_1_ = f32[1024,256]{1,0:T(8,128)S(1)} custom-call(f32[40,1024]{1,0:T(8,128)S(1)} %get-tuple-element.134.ids_ref, f32[1024,256]{1,0:T(8,128)S(1)} %get-tuple-element.141.grad_ref, f32[20,1024,256]{2,1,0:T(8,128)} %get-tuple-element.136.weight_ref), custom_call_target="tpu_custom_call" | custom-call | flops 8589934592 | bytes 8388608 | tf_op jit(solution)/shard_map/layer_two_back/scatter/pallas_call | solution.py:572
  132.0 1.6 collective-permute-start.26
  133.6 2.1 %collective-permute-done.26 = f32[2,256]{1,0:T(2,128)S(1)} collective-permute-done((f32[2,256]{1,0:T(2,128)S(1)}, f32[2,256]{1,0:T(2,128)S(1)}, u32[]{:S(2)}, u32[]{:S(2)}) %collective-permute-start.26) | collective-permute-done | bytes 2080 | tf_op jit(solution)/shard_map/layer_two_back/ppermute | solution.py:41
  135.7 2.9 %middle.1 = (f32[72,256]{1,0:T(8,128)S(1)}, f32[72,256]{1,0:T(8,128)S(1)}, f32[72,256]{1,0:T(8,128)S(1)}, f32[72,256]{1,0:T(8,128)S(1)}, f32[1024,128]{1,0:T(8,1...) custom-call(s32[1]{0:T(128)} %bitcast.me_ref, f32[1024,256]{1,0:T(8,128)S(1)} %get-tuple-element.130.own_ref, ...), custom_call_target="tpu_custom_call" | custom-call | tf_op jit(solution)/shard_map/layer_two_back/middle/pallas_call | solution.py:667
  138.6 0.5 collective-permute-start.28
  139.1 1.3 collective-permute-start.29
  140.4 8.8 %scatter.6.refs_0_ = f32[1024,128]{1,0:T(8,128)S(1)} custom-call(f32[40,1024]{1,0:T(8,128)S(1)} %get-tuple-element.134.ids_ref, f32[1024,128]{1,0:T(8,128)S(1)} %get-tuple-element.163.grad_ref, f32[20,1024,128]{2,1,0:T(8,128)} %get-tuple-element.158.weight_ref), custom_call_target="tpu_custom_call" | custom-call | flops 6442450944 | bytes 6291456 | tf_op jit(solution)/shard_map/layer_one_back/scatter/pallas_call | solution.py:572
  149.4 1.5 collective-permute-start.32
  150.9 2.9 %collective-permute-start.30 = (f32[72,256]{1,0:T(8,128)S(1)}, f32[72,256]{1,0:T(8,128)S(1)}, u32[]{:S(2)}, u32[]{:S(2)}) collective-permute-start(f32[72,256]{1,0:T(8,128)S(1)} %add_add_fusion.1), channel_id=1, source_target_pairs={{0,8},{4,12},{8,0},{12,4},{16,24},{20,28},{24,16},{28,20},{1,9},{5... | collective-permute-start | bytes 221192 | tf_op jit(solution)/shard_map/layer_one_back/ppermute | solution.py:41
  153.8 6.4 %scatter.7.refs_1_ = f32[1024,128]{1,0:T(8,128)S(1)} custom-call(f32[40,1024]{1,0:T(8,128)S(1)} %get-tuple-element.134.ids_ref, f32[1024,128]{1,0:T(8,128)S(1)} %get-tuple-element.163.grad_ref, f32[20,1024,128]{2,1,0:T(8,128)} %get-tuple-element.158.weight_ref), custom_call_target="tpu_custom_call" | custom-call | flops 4294967296 | bytes 4194304 | tf_op jit(solution)/shard_map/layer_one_back/scatter/pallas_call | solution.py:572
  160.3 1.6 collective-permute-start.33
  161.9 2.8 %collective-permute-done.33 = f32[72,256]{1,0:T(8,128)S(1)} collective-permute-done((f32[72,256]{1,0:T(8,128)S(1)}, f32[72,256]{1,0:T(8,128)S(1)}, u32[]{:S(2)}, u32[]{:S(2)}) %collective-permute-start.33) | collective-permute-done | bytes 73760 | tf_op jit(solution)/shard_map/layer_one_back/ppermute | solution.py:41
  164.7 1.6 last.1
  166.3 0.6 collective-permute-start.35
  166.9 1.3 collective-permute-start.34
  168.2 2.0 %collective-permute-done.36 = f32[64,256]{1,0:T(8,128)S(1)} collective-permute-done((f32[64,256]{1,0:T(8,128)S(1)}, f32[64,256]{1,0:T(8,128)S(1)}, u32[]{:S(2)}, u32[]{:S(2)}) %collective-permute-start.36) | collective-permute-done | bytes 65568 | tf_op jit(solution)/shard_map/layer_one_back/ppermute | solution.py:41
  170.1 1.1 collective-permute-done.35
  171.4 1.6 collective-permute-start.40
  173.0 1.0 unpack_output.1
  174.0 0.6 slice.183
  174.6 1.3 collective-permute-start.38
  176.0 1.5 collective-permute-start.43
  177.6 2.9 %collective-permute-start.41 = (f32[64,256]{1,0:T(8,128)S(1)}, f32[64,256]{1,0:T(8,128)S(1)}, u32[]{:S(2)}, u32[]{:S(2)}) collective-permute-start(f32[64,256]{1,0:T(8,128)S(1)} %add.272), channel_id=1, source_target_pairs={{0,8},{4,12},{8,0},{12,4},{16,24},{20,28},{24,16},{28,20},{1,9},{5... | collective-permute-start | bytes 196616 | tf_op jit(solution)/shard_map/layer_one_back/ppermute | solution.py:41
  181.0 1.0 collective-permute-done.39.refs_3_
  182.0 0.8 unpack_grad.1
  183.0 2.5 %collective-permute-done.42 = f32[64,256]{1,0:T(8,128)S(1)} collective-permute-done((f32[64,256]{1,0:T(8,128)S(1)}, f32[64,256]{1,0:T(8,128)S(1)}, u32[]{:S(2)}, u32[]{:S(2)}) %collective-permute-start.42) | collective-permute-done | bytes 65568 | tf_op jit(solution)/shard_map/layer_one_back/ppermute | solution.py:41
  185.5 0.6 pad_maximum_fusion
  (72 shorter events, 2.8 us)
Async XLA Ops:
  0.6 96.2 %copy-start.1 = (f32[4,256]{1,0:T(4,128)S(1)}, f32[4,256]{1,0:T(4,128)}, u32[]{:S(2)}) copy-start(f32[4,256]{1,0:T(4,128)} %gmean_ref.1) | copy-start | bytes 12292
  0.7 96.2 %copy-start = (f32[4,256]{1,0:T(4,128)S(1)}, f32[4,256]{1,0:T(4,128)}, u32[]{:S(2)}) copy-start(f32[4,256]{1,0:T(4,128)} %gmax_ref.1) | copy-start | bytes 12292
  2.1 5.8 %collective-permute-start = (f32[104,256]{1,0:T(8,128)S(1)}, f32[104,256]{1,0:T(8,128)S(1)}, u32[]{:S(2)}, u32[]{:S(2)}) collective-permute-start(f32[104,256]{1,0:T(8,128)S(1)} %get-tuple-element.97), channel_id=1, source_target_pairs={{0,1},{1,0},{2,3},{3,2},{4,5},{5,4},{6,7},{7,6},{8,9},{9,8},{10,11... | collective-permute-start | bytes 319496 | tf_op jit(solution)/shard_map/bring_clouds/ppermute | solution.py:41
  2.6 8.0 %collective-permute-start.1 = (f32[104,256]{1,0:T(8,128)S(1)}, f32[104,256]{1,0:T(8,128)S(1)}, u32[]{:S(2)}, u32[]{:S(2)}) collective-permute-start(f32[104,256]{1,0:T(8,128)S(1)} %get-tuple-element.98), channel_id=1, source_target_pairs={{0,2},{1,3},{2,0},{3,1},{4,6},{5,7},{6,4},{7,5},{8,10},{9,11},{10,... | collective-permute-start | bytes 319496 | tf_op jit(solution)/shard_map/bring_clouds/ppermute | solution.py:41
  5.2 5.6 %collective-permute-start.2 = (f32[104,256]{1,0:T(8,128)S(1)}, f32[104,256]{1,0:T(8,128)S(1)}, u32[]{:S(2)}, u32[]{:S(2)}) collective-permute-start(f32[104,256]{1,0:T(8,128)S(1)} %get-tuple-element.99), channel_id=1, source_target_pairs={{0,3},{1,2},{2,1},{3,0},{4,7},{5,6},{6,5},{7,4},{8,11},{9,10},{10,... | collective-permute-start | bytes 319496 | tf_op jit(solution)/shard_map/bring_clouds/ppermute | solution.py:41
  15.1 3.1 %collective-permute-start.5 = (f32[2,128]{1,0:T(2,128)S(1)}, f32[2,128]{1,0:T(2,128)S(1)}, u32[]{:S(2)}, u32[]{:S(2)}) collective-permute-start(f32[2,128]{1,0:T(2,128)S(1)} %get-tuple-element.106.local_ref), channel_id=1, source_target_pairs={{0,3},{1,2},{2,1},{3,0},{4,7},{5,6},{6,5},{7,4},{8,11},{9,10},{10,... | collective-permute-start | bytes 3080 | tf_op jit(solution)/shard_map/layer_one/ppermute | solution.py:41
  16.7 3.6 %collective-permute-start.4 = (f32[2,128]{1,0:T(2,128)S(1)}, f32[2,128]{1,0:T(2,128)S(1)}, u32[]{:S(2)}, u32[]{:S(2)}) collective-permute-start(f32[2,128]{1,0:T(2,128)S(1)} %get-tuple-element.106.local_ref), channel_id=1, source_target_pairs={{0,2},{1,3},{2,0},{3,1},{4,6},{5,7},{6,4},{7,5},{8,10},{9,11},{10,... | collective-permute-start | bytes 3080 | tf_op jit(solution)/shard_map/layer_one/ppermute | solution.py:41
  16.9 3.3 %collective-permute-start.3 = (f32[2,128]{1,0:T(2,128)S(1)}, f32[2,128]{1,0:T(2,128)S(1)}, u32[]{:S(2)}, u32[]{:S(2)}) collective-permute-start(f32[2,128]{1,0:T(2,128)S(1)} %get-tuple-element.106.local_ref), channel_id=1, source_target_pairs={{0,1},{1,0},{2,3},{3,2},{4,5},{5,4},{6,7},{7,6},{8,9},{9,8},{10,11... | collective-permute-start | bytes 3080 | tf_op jit(solution)/shard_map/layer_one/ppermute | solution.py:41
  20.3 3.6 %collective-permute-start.6 = (f32[2,128]{1,0:T(2,128)S(1)}, f32[2,128]{1,0:T(2,128)S(1)}, u32[]{:S(2)}, u32[]{:S(2)}) collective-permute-start(f32[2,128]{1,0:T(2,128)S(1)} %pad_maximum_fusion.4), channel_id=1, source_target_pairs={{0,4},{4,0},{8,12},{12,8},{16,20},{20,16},{24,28},{28,24},{1,5},{5... | collective-permute-start | bytes 3080 | tf_op jit(solution)/shard_map/layer_one/ppermute | solution.py:41
  24.0 5.8 %collective-permute-start.9 = (f32[2,128]{1,0:T(2,128)S(1)}, f32[2,128]{1,0:T(2,128)S(1)}, u32[]{:S(2)}, u32[]{:S(2)}) collective-permute-start(f32[2,128]{1,0:T(2,128)S(1)} %pad_maximum_fusion.5), channel_id=1, source_target_pairs={{0,24},{4,28},{8,16},{12,20},{16,8},{20,12},{24,0},{28,4},{1,25},{... | collective-permute-start | bytes 3080 | tf_op jit(solution)/shard_map/layer_one/ppermute | solution.py:41
  27.6 4.5 %collective-permute-start.8 = (f32[2,128]{1,0:T(2,128)S(1)}, f32[2,128]{1,0:T(2,128)S(1)}, u32[]{:S(2)}, u32[]{:S(2)}) collective-permute-start(f32[2,128]{1,0:T(2,128)S(1)} %pad_maximum_fusion.5), channel_id=1, source_target_pairs={{0,16},{4,20},{8,24},{12,28},{16,0},{20,4},{24,8},{28,12},{1,17},{... | collective-permute-start | bytes 3080 | tf_op jit(solution)/shard_map/layer_one/ppermute | solution.py:41
  27.6 4.5 %collective-permute-start.7 = (f32[2,128]{1,0:T(2,128)S(1)}, f32[2,128]{1,0:T(2,128)S(1)}, u32[]{:S(2)}, u32[]{:S(2)}) collective-permute-start(f32[2,128]{1,0:T(2,128)S(1)} %pad_maximum_fusion.5), channel_id=1, source_target_pairs={{0,8},{4,12},{8,0},{12,4},{16,24},{20,28},{24,16},{28,20},{1,9},{5... | collective-permute-start | bytes 3080 | tf_op jit(solution)/shard_map/layer_one/ppermute | solution.py:41
  51.1 3.1 %collective-permute-start.12 = (f32[2,256]{1,0:T(2,128)S(1)}, f32[2,256]{1,0:T(2,128)S(1)}, u32[]{:S(2)}, u32[]{:S(2)}) collective-permute-start(f32[2,256]{1,0:T(2,128)S(1)} %get-tuple-element.114.local_ref), channel_id=1, source_target_pairs={{0,3},{1,2},{2,1},{3,0},{4,7},{5,6},{6,5},{7,4},{8,11},{9,10},{10,... | collective-permute-start | bytes 6152 | tf_op jit(solution)/shard_map/layer_two/ppermute | solution.py:41
  51.2 3.7 %collective-permute-start.11 = (f32[2,256]{1,0:T(2,128)S(1)}, f32[2,256]{1,0:T(2,128)S(1)}, u32[]{:S(2)}, u32[]{:S(2)}) collective-permute-start(f32[2,256]{1,0:T(2,128)S(1)} %get-tuple-element.114.local_ref), channel_id=1, source_target_pairs={{0,2},{1,3},{2,0},{3,1},{4,6},{5,7},{6,4},{7,5},{8,10},{9,11},{10,... | collective-permute-start | bytes 6152 | tf_op jit(solution)/shard_map/layer_two/ppermute | solution.py:41
  51.8 3.1 %collective-permute-start.10 = (f32[2,256]{1,0:T(2,128)S(1)}, f32[2,256]{1,0:T(2,128)S(1)}, u32[]{:S(2)}, u32[]{:S(2)}) collective-permute-start(f32[2,256]{1,0:T(2,128)S(1)} %get-tuple-element.114.local_ref), channel_id=1, source_target_pairs={{0,1},{1,0},{2,3},{3,2},{4,5},{5,4},{6,7},{7,6},{8,9},{9,8},{10,11... | collective-permute-start | bytes 6152 | tf_op jit(solution)/shard_map/layer_two/ppermute | solution.py:41
  54.9 3.7 %collective-permute-start.13 = (f32[2,256]{1,0:T(2,128)S(1)}, f32[2,256]{1,0:T(2,128)S(1)}, u32[]{:S(2)}, u32[]{:S(2)}) collective-permute-start(f32[2,256]{1,0:T(2,128)S(1)} %pad_maximum_fusion.1), channel_id=1, source_target_pairs={{0,4},{4,0},{8,12},{12,8},{16,20},{20,16},{24,28},{28,24},{1,5},{5... | collective-permute-start | bytes 6152 | tf_op jit(solution)/shard_map/layer_two/ppermute | solution.py:41
  58.6 6.4 %collective-permute-start.16 = (f32[2,256]{1,0:T(2,128)S(1)}, f32[2,256]{1,0:T(2,128)S(1)}, u32[]{:S(2)}, u32[]{:S(2)}) collective-permute-start(f32[2,256]{1,0:T(2,128)S(1)} %pad_maximum_fusion.2), channel_id=1, source_target_pairs={{0,24},{4,28},{8,16},{12,20},{16,8},{20,12},{24,0},{28,4},{1,25},{... | collective-permute-start | bytes 6152 | tf_op jit(solution)/shard_map/layer_two/ppermute | solution.py:41
  60.1 6.2 %collective-permute-start.15 = (f32[2,256]{1,0:T(2,128)S(1)}, f32[2,256]{1,0:T(2,128)S(1)}, u32[]{:S(2)}, u32[]{:S(2)}) collective-permute-start(f32[2,256]{1,0:T(2,128)S(1)} %pad_maximum_fusion.2), channel_id=1, source_target_pairs={{0,16},{4,20},{8,24},{12,28},{16,0},{20,4},{24,8},{28,12},{1,17},{... | collective-permute-start | bytes 6152 | tf_op jit(solution)/shard_map/layer_two/ppermute | solution.py:41
  60.8 5.5 %collective-permute-start.14 = (f32[2,256]{1,0:T(2,128)S(1)}, f32[2,256]{1,0:T(2,128)S(1)}, u32[]{:S(2)}, u32[]{:S(2)}) collective-permute-start(f32[2,256]{1,0:T(2,128)S(1)} %pad_maximum_fusion.2), channel_id=1, source_target_pairs={{0,8},{4,12},{8,0},{12,4},{16,24},{20,28},{24,16},{28,20},{1,9},{5... | collective-permute-start | bytes 6152 | tf_op jit(solution)/shard_map/layer_two/ppermute | solution.py:41
  64.3 32.5 %collective-permute-start.17 = (f32[256,256]{1,0:T(8,128)S(1)}, f32[256,256]{1,0:T(8,128)S(1)}, u32[]{:S(2)}, u32[]{:S(2)}) collective-permute-start(f32[256,256]{1,0:T(8,128)S(1)} %get-tuple-element.120), channel_id=1, source_target_pairs={{0,1},{1,0},{2,3},{3,2},{4,5},{5,4},{6,7},{7,6},{8,9},{9,8},{10,11... | collective-permute-start | bytes 786440 | tf_op jit(solution)/shard_map/bring_cotangents/ppermute | solution.py:41
  64.4 32.4 %collective-permute-start.18 = (f32[256,256]{1,0:T(8,128)S(1)}, f32[256,256]{1,0:T(8,128)S(1)}, u32[]{:S(2)}, u32[]{:S(2)}) collective-permute-start(f32[256,256]{1,0:T(8,128)S(1)} %get-tuple-element.121), channel_id=1, source_target_pairs={{0,2},{1,3},{2,0},{3,1},{4,6},{5,7},{6,4},{7,5},{8,10},{9,11},{10,... | collective-permute-start | bytes 786440 | tf_op jit(solution)/shard_map/bring_cotangents/ppermute | solution.py:41
  65.0 31.8 %collective-permute-start.19 = (f32[256,256]{1,0:T(8,128)S(1)}, f32[256,256]{1,0:T(8,128)S(1)}, u32[]{:S(2)}, u32[]{:S(2)}) collective-permute-start(f32[256,256]{1,0:T(8,128)S(1)} %get-tuple-element.122), channel_id=1, source_target_pairs={{0,3},{1,2},{2,1},{3,0},{4,7},{5,6},{6,5},{7,4},{8,11},{9,10},{10,... | collective-permute-start | bytes 786440 | tf_op jit(solution)/shard_map/bring_cotangents/ppermute | solution.py:41
  97.7 18.2 %collective-permute-start.20 = (f32[264,256]{1,0:T(8,128)S(1)}, f32[264,256]{1,0:T(8,128)S(1)}, u32[]{:S(2)}, u32[]{:S(2)}) collective-permute-start(f32[264,256]{1,0:T(8,128)S(1)} %get-tuple-element.124), channel_id=1, source_target_pairs={{0,1},{1,0},{2,3},{3,2},{4,5},{5,4},{6,7},{7,6},{8,9},{9,8},{10,11... | collective-permute-start | bytes 811016 | tf_op jit(solution)/shard_map/pools/ppermute | solution.py:41
  98.1 17.8 %collective-permute-start.21 = (f32[264,256]{1,0:T(8,128)S(1)}, f32[264,256]{1,0:T(8,128)S(1)}, u32[]{:S(2)}, u32[]{:S(2)}) collective-permute-start(f32[264,256]{1,0:T(8,128)S(1)} %get-tuple-element.125), channel_id=1, source_target_pairs={{0,2},{1,3},{2,0},{3,1},{4,6},{5,7},{6,4},{7,5},{8,10},{9,11},{10,... | collective-permute-start | bytes 811016 | tf_op jit(solution)/shard_map/pools/ppermute | solution.py:41
  98.7 17.2 %collective-permute-start.22 = (f32[264,256]{1,0:T(8,128)S(1)}, f32[264,256]{1,0:T(8,128)S(1)}, u32[]{:S(2)}, u32[]{:S(2)}) collective-permute-start(f32[264,256]{1,0:T(8,128)S(1)} %get-tuple-element.126), channel_id=1, source_target_pairs={{0,3},{1,2},{2,1},{3,0},{4,7},{5,6},{6,5},{7,4},{8,11},{9,10},{10,... | collective-permute-start | bytes 811016 | tf_op jit(solution)/shard_map/pools/ppermute | solution.py:41
  116.0 16.0 %collective-permute-start.25 = (f32[2,256]{1,0:T(2,128)S(1)}, f32[2,256]{1,0:T(2,128)S(1)}, u32[]{:S(2)}, u32[]{:S(2)}) collective-permute-start(f32[2,256]{1,0:T(2,128)S(1)} %add_add_fusion.5), channel_id=1, source_target_pairs={{0,24},{4,28},{8,16},{12,20},{16,8},{20,12},{24,0},{28,4},{1,25},{... | collective-permute-start | bytes 6152 | tf_op jit(solution)/shard_map/layer_two_back/ppermute | solution.py:41
  117.5 14.5 %collective-permute-start.24 = (f32[2,256]{1,0:T(2,128)S(1)}, f32[2,256]{1,0:T(2,128)S(1)}, u32[]{:S(2)}, u32[]{:S(2)}) collective-permute-start(f32[2,256]{1,0:T(2,128)S(1)} %add_add_fusion.5), channel_id=1, source_target_pairs={{0,16},{4,20},{8,24},{12,28},{16,0},{20,4},{24,8},{28,12},{1,17},{... | collective-permute-start | bytes 6152 | tf_op jit(solution)/shard_map/layer_two_back/ppermute | solution.py:41
  117.8 14.2 %collective-permute-start.23 = (f32[2,256]{1,0:T(2,128)S(1)}, f32[2,256]{1,0:T(2,128)S(1)}, u32[]{:S(2)}, u32[]{:S(2)}) collective-permute-start(f32[2,256]{1,0:T(2,128)S(1)} %add_add_fusion.5), channel_id=1, source_target_pairs={{0,8},{4,12},{8,0},{12,4},{16,24},{20,28},{24,16},{28,20},{1,9},{5... | collective-permute-start | bytes 6152 | tf_op jit(solution)/shard_map/layer_two_back/ppermute | solution.py:41
  132.0 3.7 %collective-permute-start.26 = (f32[2,256]{1,0:T(2,128)S(1)}, f32[2,256]{1,0:T(2,128)S(1)}, u32[]{:S(2)}, u32[]{:S(2)}) collective-permute-start(f32[2,256]{1,0:T(2,128)S(1)} %add_add_fusion.4), channel_id=1, source_target_pairs={{0,4},{4,0},{8,12},{12,8},{16,20},{20,16},{24,28},{28,24},{1,5},{5... | collective-permute-start | bytes 6152 | tf_op jit(solution)/shard_map/layer_two_back/ppermute | solution.py:41
  138.6 10.7 %collective-permute-start.27 = (f32[72,256]{1,0:T(8,128)S(1)}, f32[72,256]{1,0:T(8,128)S(1)}, u32[]{:S(2)}, u32[]{:S(2)}) collective-permute-start(f32[72,256]{1,0:T(8,128)S(1)} %get-tuple-element.154), channel_id=1, source_target_pairs={{0,1},{1,0},{2,3},{3,2},{4,5},{5,4},{6,7},{7,6},{8,9},{9,8},{10,11... | collective-permute-start | bytes 221192 | tf_op jit(solution)/shard_map/layer_one_back/ppermute | solution.py:41
  138.6 10.7 %collective-permute-start.28 = (f32[72,256]{1,0:T(8,128)S(1)}, f32[72,256]{1,0:T(8,128)S(1)}, u32[]{:S(2)}, u32[]{:S(2)}) collective-permute-start(f32[72,256]{1,0:T(8,128)S(1)} %get-tuple-element.155), channel_id=1, source_target_pairs={{0,2},{1,3},{2,0},{3,1},{4,6},{5,7},{6,4},{7,5},{8,10},{9,11},{10,... | collective-permute-start | bytes 221192 | tf_op jit(solution)/shard_map/layer_one_back/ppermute | solution.py:41
  139.1 10.2 %collective-permute-start.29 = (f32[72,256]{1,0:T(8,128)S(1)}, f32[72,256]{1,0:T(8,128)S(1)}, u32[]{:S(2)}, u32[]{:S(2)}) collective-permute-start(f32[72,256]{1,0:T(8,128)S(1)} %get-tuple-element.156), channel_id=1, source_target_pairs={{0,3},{1,2},{2,1},{3,0},{4,7},{5,6},{6,5},{7,4},{8,11},{9,10},{10,... | collective-permute-start | bytes 221192 | tf_op jit(solution)/shard_map/layer_one_back/ppermute | solution.py:41
  149.4 10.9 %collective-permute-start.32 = (f32[72,256]{1,0:T(8,128)S(1)}, f32[72,256]{1,0:T(8,128)S(1)}, u32[]{:S(2)}, u32[]{:S(2)}) collective-permute-start(f32[72,256]{1,0:T(8,128)S(1)} %add_add_fusion.1), channel_id=1, source_target_pairs={{0,24},{4,28},{8,16},{12,20},{16,8},{20,12},{24,0},{28,4},{1,25},{... | collective-permute-start | bytes 221192 | tf_op jit(solution)/shard_map/layer_one_back/ppermute | solution.py:41
  150.9 9.4 %collective-permute-start.31 = (f32[72,256]{1,0:T(8,128)S(1)}, f32[72,256]{1,0:T(8,128)S(1)}, u32[]{:S(2)}, u32[]{:S(2)}) collective-permute-start(f32[72,256]{1,0:T(8,128)S(1)} %add_add_fusion.1), channel_id=1, source_target_pairs={{0,16},{4,20},{8,24},{12,28},{16,0},{20,4},{24,8},{28,12},{1,17},{... | collective-permute-start | bytes 221192 | tf_op jit(solution)/shard_map/layer_one_back/ppermute | solution.py:41
  150.9 9.4 %collective-permute-start.30 = (f32[72,256]{1,0:T(8,128)S(1)}, f32[72,256]{1,0:T(8,128)S(1)}, u32[]{:S(2)}, u32[]{:S(2)}) collective-permute-start(f32[72,256]{1,0:T(8,128)S(1)} %add_add_fusion.1), channel_id=1, source_target_pairs={{0,8},{4,12},{8,0},{12,4},{16,24},{20,28},{24,16},{28,20},{1,9},{5... | collective-permute-start | bytes 221192 | tf_op jit(solution)/shard_map/layer_one_back/ppermute | solution.py:41
  160.3 4.4 %collective-permute-start.33 = (f32[72,256]{1,0:T(8,128)S(1)}, f32[72,256]{1,0:T(8,128)S(1)}, u32[]{:S(2)}, u32[]{:S(2)}) collective-permute-start(f32[72,256]{1,0:T(8,128)S(1)} %add_add_fusion), channel_id=1, source_target_pairs={{0,4},{4,0},{8,12},{12,8},{16,20},{20,16},{24,28},{28,24},{1,5},{5... | collective-permute-start | bytes 221192 | tf_op jit(solution)/shard_map/layer_one_back/ppermute | solution.py:41
  166.3 3.8 %collective-permute-start.36 = (f32[64,256]{1,0:T(8,128)S(1)}, f32[64,256]{1,0:T(8,128)S(1)}, u32[]{:S(2)}, u32[]{:S(2)}) collective-permute-start(f32[64,256]{1,0:T(8,128)S(1)} %get-tuple-element.168), channel_id=1, source_target_pairs={{0,3},{1,2},{2,1},{3,0},{4,7},{5,6},{6,5},{7,4},{8,11},{9,10},{10,... | collective-permute-start | bytes 196616 | tf_op jit(solution)/shard_map/layer_one_back/ppermute | solution.py:41
  166.3 4.9 %collective-permute-start.35 = (f32[64,256]{1,0:T(8,128)S(1)}, f32[64,256]{1,0:T(8,128)S(1)}, u32[]{:S(2)}, u32[]{:S(2)}) collective-permute-start(f32[64,256]{1,0:T(8,128)S(1)} %get-tuple-element.168), channel_id=1, source_target_pairs={{0,2},{1,3},{2,0},{3,1},{4,6},{5,7},{6,4},{7,5},{8,10},{9,11},{10,... | collective-permute-start | bytes 196616 | tf_op jit(solution)/shard_map/layer_one_back/ppermute | solution.py:41
  166.9 4.4 %collective-permute-start.34 = (f32[64,256]{1,0:T(8,128)S(1)}, f32[64,256]{1,0:T(8,128)S(1)}, u32[]{:S(2)}, u32[]{:S(2)}) collective-permute-start(f32[64,256]{1,0:T(8,128)S(1)} %get-tuple-element.168), channel_id=1, source_target_pairs={{0,1},{1,0},{2,3},{3,2},{4,5},{5,4},{6,7},{7,6},{8,9},{9,8},{10,11... | collective-permute-start | bytes 196616 | tf_op jit(solution)/shard_map/layer_one_back/ppermute | solution.py:41
  171.3 6.3 %collective-permute-start.37 = (f32[128,256]{1,0:T(8,128)S(1)}, f32[128,256]{1,0:T(8,128)S(1)}, u32[]{:S(2)}, u32[]{:S(2)}) collective-permute-start(f32[128,256]{1,0:T(8,128)S(1)} %get-tuple-element.174), channel_id=1, source_target_pairs={{0,1},{1,0},{2,3},{3,2},{4,5},{5,4},{6,7},{7,6},{8,9},{9,8},{10,11... | collective-permute-start | bytes 393224 | tf_op jit(solution)/shard_map/layer_one_back/ppermute | solution.py:41
  171.4 4.6 %collective-permute-start.40 = (f32[64,256]{1,0:T(8,128)S(1)}, f32[64,256]{1,0:T(8,128)S(1)}, u32[]{:S(2)}, u32[]{:S(2)}) collective-permute-start(f32[64,256]{1,0:T(8,128)S(1)} %add_add_fusion.3), channel_id=1, source_target_pairs={{0,4},{4,0},{8,12},{12,8},{16,20},{20,16},{24,28},{28,24},{1,5},{5... | collective-permute-start | bytes 196616 | tf_op jit(solution)/shard_map/layer_one_back/ppermute | solution.py:41
  174.6 6.4 %collective-permute-start.38 = (f32[128,256]{1,0:T(8,128)S(1)}, f32[128,256]{1,0:T(8,128)S(1)}, u32[]{:S(2)}, u32[]{:S(2)}) collective-permute-start(f32[128,256]{1,0:T(8,128)S(1)} %get-tuple-element.175), channel_id=1, source_target_pairs={{0,2},{1,3},{2,0},{3,1},{4,6},{5,7},{6,4},{7,5},{8,10},{9,11},{10,... | collective-permute-start | bytes 393224 | tf_op jit(solution)/shard_map/layer_one_back/ppermute | solution.py:41
  175.9 6.1 %collective-permute-start.39 = (f32[128,256]{1,0:T(8,128)S(1)}, f32[128,256]{1,0:T(8,128)S(1)}, u32[]{:S(2)}, u32[]{:S(2)}) collective-permute-start(f32[128,256]{1,0:T(8,128)S(1)} %get-tuple-element.176), channel_id=1, source_target_pairs={{0,3},{1,2},{2,1},{3,0},{4,7},{5,6},{6,5},{7,4},{8,11},{9,10},{10,... | collective-permute-start | bytes 393224 | tf_op jit(solution)/shard_map/layer_one_back/ppermute | solution.py:41
  176.0 6.9 %collective-permute-start.43 = (f32[64,256]{1,0:T(8,128)S(1)}, f32[64,256]{1,0:T(8,128)S(1)}, u32[]{:S(2)}, u32[]{:S(2)}) collective-permute-start(f32[64,256]{1,0:T(8,128)S(1)} %add.272), channel_id=1, source_target_pairs={{0,24},{4,28},{8,16},{12,20},{16,8},{20,12},{24,0},{28,4},{1,25},{... | collective-permute-start | bytes 196616 | tf_op jit(solution)/shard_map/layer_one_back/ppermute | solution.py:41
  177.6 7.9 %collective-permute-start.42 = (f32[64,256]{1,0:T(8,128)S(1)}, f32[64,256]{1,0:T(8,128)S(1)}, u32[]{:S(2)}, u32[]{:S(2)}) collective-permute-start(f32[64,256]{1,0:T(8,128)S(1)} %add.272), channel_id=1, source_target_pairs={{0,16},{4,20},{8,24},{12,28},{16,0},{20,4},{24,8},{28,12},{1,17},{... | collective-permute-start | bytes 196616 | tf_op jit(solution)/shard_map/layer_one_back/ppermute | solution.py:41
  177.6 7.8 %collective-permute-start.41 = (f32[64,256]{1,0:T(8,128)S(1)}, f32[64,256]{1,0:T(8,128)S(1)}, u32[]{:S(2)}, u32[]{:S(2)}) collective-permute-start(f32[64,256]{1,0:T(8,128)S(1)} %add.272), channel_id=1, source_target_pairs={{0,8},{4,12},{8,0},{12,4},{16,24},{20,28},{24,16},{28,20},{1,9},{5... | collective-permute-start | bytes 196616 | tf_op jit(solution)/shard_map/layer_one_back/ppermute | solution.py:41

commit v2 on v1

--- a/solution.py
+++ b/solution.py
@@ -11,6 +11,7 @@
 LOG2E = 1.4426950408889634
 BOTH = ("clouds", "pts")
 MIB = 2**20
+SMALL = jnp.float8_e4m3fn
 
 
 def f32(*shape):
@@ -29,11 +30,8 @@
     return pltpu.CompilerParams(vmem_limit_bytes=mib * MIB)
 
 
-def whole(shape):
-    return pl.BlockSpec(shape, lambda *step: (0,) * len(shape))
-
-
 SMEM = pl.BlockSpec(memory_space=pltpu.SMEM)
+VMEM = pl.BlockSpec(memory_space=pltpu.VMEM)
 
 
 def exchange(x, axes, mask):
@@ -162,7 +160,7 @@
     clouds, rows, width = x.shape
     return pl.pallas_call(
         split_kernel,
-        in_specs=[SMEM, pl.BlockSpec(memory_space=pltpu.VMEM)],
+        in_specs=[SMEM, VMEM],
         out_shape=[f32(rows, width)] * clouds,
         compiler_params=params(16),
         name="split",
@@ -184,7 +182,7 @@
     rows = parts[0].shape[0] - 8
     return pl.pallas_call(
         functools.partial(unpack_output_kernel, rows),
-        in_specs=[SMEM] + [pl.BlockSpec(memory_space=pltpu.VMEM)] * clouds,
+        in_specs=[SMEM] + [VMEM] * clouds,
         out_shape=[f32(clouds, rows, width), f32(clouds, width), f32(clouds, width)],
         compiler_params=params(16),
         name="unpack_output",
@@ -207,7 +205,7 @@
     count = len(parts)
     return pl.pallas_call(
         unpack_grad_kernel,
-        in_specs=[SMEM] + [pl.BlockSpec(memory_space=pltpu.VMEM)] * count,
+        in_specs=[SMEM] + [VMEM] * count,
         out_shape=[f32(count, width, lanes), f32(count * (rows - width), lanes)],
         compiler_params=params(16),
         name="unpack_grad",
@@ -480,7 +478,7 @@
     return pl.pallas_call(
         functools.partial(edge_kernel, edges, layer, slots, first, tile),
         grid=(points // tile,),
-        in_specs=[whole(v.shape) for v in (x, a, b, stat, small)],
+        in_specs=[VMEM] * 5,
         out_specs=[some, pl.BlockSpec((slots, tile, width), lambda step: (0, step, 0))] + [some] * 4,
         out_shape=[f32(points, width), in_hbm(slots, points, width)] + [f32(points, width)] * 4,
         scratch_shapes=[
@@ -495,9 +493,9 @@
 
 
 def pool_kernel(me_ref, out_ref, inv_ref, slope_ref, moment_ref, gmax_ref, gmean_ref, *refs):
-    count = (len(refs) - 2) // 2
+    count = (len(refs) - 3) // 2
     acts, parts = refs[:count], refs[count : 2 * count]
-    scaled_ref, own_ref = refs[2 * count :]
+    scaled_ref, own_ref, largest_ref = refs[2 * count :]
     me = me_ref[0]
     points, width = out_ref.shape
     rows = points // count
@@ -507,7 +505,7 @@
     mean = column_sum(out) / points
     to_max = gmax_ref[pl.ds(me, 1), :]
     to_mean = gmean_ref[pl.ds(me, 1), :] / points
-    own_sum = moment_sum = jnp.zeros((1, width), jnp.float32)
+    own_sum = moment_sum = largest = jnp.zeros((1, width), jnp.float32)
     for m in range(count):
         here = slice(m * rows, (m + 1) * rows)
         part = out[here]
@@ -521,6 +519,8 @@
         own_ref[here, :] = own
         own_sum = own_sum + column_sum(own)
         moment_sum = moment_sum + column_sum(grad * moment_ref[here, :])
+        largest = jnp.maximum(largest, jnp.max(jnp.abs(grad), axis=0, keepdims=True))
+    largest_ref[...] = largest
     for m in range(count):
         parts[m][rows + 2 : rows + 3, :] = own_sum
         parts[m][rows + 3 : rows + 4, :] = moment_sum
@@ -532,62 +532,77 @@
     rows = points // count
     results = pl.pallas_call(
         pool_kernel,
-        in_specs=[SMEM] + [pl.BlockSpec(memory_space=pltpu.VMEM)] * (6 + count),
-        out_shape=[f32(rows + 8, width)] * count + [f32(points, width)] * 2,
+        in_specs=[SMEM] + [VMEM] * (6 + count),
+        out_shape=[f32(rows + 8, width)] * count + [f32(points, width)] * 2 + [f32(1, width)],
         compiler_params=params(16),
         name="pools",
     )(me, out, inv, slope, moment, grad_max, grad_mean, *acts)
-    return results[:count], results[count], results[count + 1]
-
-
-def scatter_kernel(first, group, ids_ref, grad_ref, weight_ref, sum_ref):
+    return results[:count], *results[count:]
+
+
+def scatter_kernel(first, group, small_rest, ids_ref, grad_ref, largest_ref, weight_ref, sum_ref):
     step = pl.program_id(0)
-    points = grad_ref.shape[0]
+    points, width = grad_ref.shape
     rows = lax.broadcasted_iota(jnp.int32, (points, points), 0).astype(jnp.float32)
-    picks, terms = [], []
+    scale = 2.0**16 / jnp.maximum(largest_ref[...], 1e-30)
+    picks, small_picks, terms, rests = [], [], [], []
     for g in range(group):
-        ids = ids_ref[pl.ds(first + step * group + g, 1), :]
-        picks.append(jnp.where(ids == rows, 1.0, 0.0).astype(jnp.bfloat16))
-        terms.append(two_terms(grad_ref[...] * weight_ref[g]))
-    found = halves_sum(
-        jnp.dot(
+        here = ids_ref[pl.ds(first + step * group + g, 1), :] == rows
+        value = grad_ref[...] * weight_ref[g]
+        picks.append(jnp.where(here, 1.0, 0.0).astype(jnp.bfloat16))
+        if small_rest:
+            high = value.astype(jnp.bfloat16)
+            terms.append(high)
+            small_picks.append(jnp.where(here, SMALL(1), SMALL(0)))
+            rests.append(((value - high.astype(jnp.float32)) * scale).astype(SMALL))
+        else:
+            terms.append(two_terms(value))
+
+    def found(picks, terms):
+        return jnp.dot(
             jnp.concatenate(picks, axis=1),
             jnp.concatenate(terms, axis=0),
             preferred_element_type=jnp.float32,
         )
-    )
+
+    if small_rest:
+        total = found(picks, terms) + found(small_picks, rests) * (1.0 / scale)
+    else:
+        total = halves_sum(found(picks, terms))
 
     @pl.when(step == 0)
     def _():
-        sum_ref[...] = found
+        sum_ref[...] = total
 
     @pl.when(step > 0)
     def _():
-        sum_ref[...] += found
-
-
-def scatter(ids, first, grad, weight, start, stop, group):
+        sum_ref[...] += total
+
+
+def scatter(ids, first, grad, largest, weight, start, stop, group):
     points, width = grad.shape
     edges = (stop - start) * points
     return pl.pallas_call(
-        functools.partial(scatter_kernel, first + start, group),
+        functools.partial(scatter_kernel, first + start, group, width >= 256),
         grid=((stop - start) // group,),
         in_specs=[
-            whole(ids.shape),
-            whole(grad.shape),
+            VMEM,
+            VMEM,
+            VMEM,
             pl.BlockSpec((group, points, width), lambda step: (start // group + step, 0, 0)),
         ],
-        out_specs=whole((points, width)),
+        out_specs=VMEM,
         out_shape=f32(points, width),
-        compiler_params=params(28),
+        compiler_params=params(36),
         cost_estimate=pl.CostEstimate(
             flops=4 * edges * points * width, bytes_accessed=4 * edges * width, transcendentals=0
         ),
         name="scatter",
-    )(ids, grad, from_hbm(weight))
+    )(ids, grad, largest, from_hbm(weight))
 
 
 def point_grads(edges, slots, own, inward_grads, ysum, inward, degree, local, stat, sums, gain, shift):
+    inward_grads = inward_grads + (column_sum(own) - column_sum(inward_grads)) / own.shape[0]
     spread = lax.rsqrt(stat[1:2, :] / edges + norm_eps)
     scale = gain * spread
     own_all = sums[0:1, :]
@@ -606,16 +621,16 @@
 
 
 def weight_grad(x, leave, reach):
-    grads = jnp.concatenate([leave, reach - leave], axis=1)
     middle = column_sum(x) / x.shape[0]
     level = lax.dot_general(
         jnp.broadcast_to(middle, (8, x.shape[1])) * 0.125,
-        jnp.broadcast_to(column_sum(grads), (8, grads.shape[1])),
+        jnp.broadcast_to(column_sum(leave), (8, leave.shape[1])),
         (((0,), (0,)), ((), ())),
         precision=lax.Precision.HIGHEST,
         preferred_element_type=jnp.float32,
     )
-    return product(x - middle, grads, 0, 0) + level
+    level = jnp.concatenate([level, jnp.zeros_like(level)], axis=1)
+    return product(x - middle, jnp.concatenate([leave, reach - leave], axis=1), 0, 0) + level
 
 
 def total_of(refs):
@@ -666,7 +681,7 @@
     operands = (own, ysum, inward, degree, local, stat, sums, small, x, weight, inv, slope, moment)
     results = pl.pallas_call(
         functools.partial(middle_kernel, edges, slots, count),
-        in_specs=[SMEM] + [pl.BlockSpec(memory_space=pltpu.VMEM)] * (len(operands) + len(reached)),
+        in_specs=[SMEM] + [VMEM] * (len(operands) + len(reached)),
         out_shape=[f32(2 * width // count + 8, outs)] * count
         + [f32(points, width), f32(points, width), f32(1, outs)],
         scratch_shapes=[pltpu.VMEM((2 * width, outs), jnp.float32)],
@@ -770,7 +785,7 @@
             edges, 1, slots, width + slots, 128, x, a_two, b_two, stat_two, small
         )
     with jax.named_scope("pools"):
-        out_parts, scaled_two, own_two = pools(
+        out_parts, scaled_two, own_two, largest_two = pools(
             me, out, inv_two, slope_two, moment_two, grad_max, grad_mean, acts
         )
         out_parts = to_owner(out_parts)
@@ -782,8 +797,8 @@
             lambda received: pair_sum([part[rows + 2 : rows + 4] for part in received]),
             out_parts,
             [
-                lambda ready: scatter(ids, slots, scaled_two, share_two, 0, cut, 4),
-                lambda ready: scatter(ids, slots, after(scaled_two, ready), share_two, cut, slots, 4),
+                lambda ready: scatter(ids, slots, scaled_two, largest_two, share_two, 0, cut, 4),
+                lambda ready: scatter(ids, slots, after(scaled_two, ready), largest_two, share_two, cut, slots, 4),
             ],
         )
         wgrad_parts, scaled_one, own_one, gain_grad_two = middle(
@@ -795,8 +810,8 @@
             lambda received: pair_sum(list(received)),
             to_owner(wgrad_parts),
             [
-                lambda ready: scatter(ids, 0, scaled_one, share_one, 0, cut, 4),
-                lambda ready: scatter(ids, 0, after(scaled_one, ready), share_one, cut, slots, 4),
+                lambda ready: scatter(ids, 0, scaled_one, scaled_one[:1], share_one, 0, cut, 4),
+                lambda ready: scatter(ids, 0, after(scaled_one, ready), scaled_one[:1], share_one, cut, slots, 4),
             ],
         )
         gain_grad_one, wgrad_one, grad_parts = last(

time: 186 us -> 182 us (0.978)
  Pallas kernels: 115 us -> 110 us
    pallas_call x7, Pallas kernels: 46.1 us -> 41.4 us  [the longest x4 38.4 us: scatter(): pl.pallas_call(functools.partial(scatter_kernel, first + start, group, wi...]
  transfers between devices with their start and end apart: 44 -> 44, of which waited for: 15 -> 15; matrix products, arithmetic and copies ran while one was open for 1% -> 1% of each run, Pallas kernels for 45% -> 44%
where the time goes in v2:
time: 182 us
  Pallas kernels  110 us (60%)
  starting transfers between devices  46.4 us (25%)
  waiting for transfers between devices  22 us (12%)
    pallas_call x2, Pallas kernels, edge_forward(): pl.pallas_call(functools.partial(edge_kernel, edges, layer, slots, first,...  46.9 us
    ppermute x44, starting transfers between devices, exchange(): return lax.ppermute(x, axes, [(i, i ^ mask) for i in range(size)])  46.4 us
    pallas_call x4, Pallas kernels, scatter(): pl.pallas_call(functools.partial(scatter_kernel, first + start, group, wi...  38.4 us
    ppermute x44, waiting for transfers between devices, exchange(): return lax.ppermute(x, axes, [(i, i ^ mask) for i in range(size)])  22 us
    pallas_call x4, Pallas kernels, part_links(): pl.pallas_call(functools.partial(links_kernel, firsts, slots), out_shape=...  7.93 us
    pallas_call x1, Pallas kernels, first_tables(): pl.pallas_call(functools.partial(first_kernel, slots, width, count), out_...  4.37 us
  transfers between devices with their start and end apart: 44, of which 15 were waited for; matrix products, arithmetic and copies ran while one was open for 1% of the time, Pallas kernels for 44%

profile of v2, /device:TPU:0, one launch (start us, length us, event | category | flops | bytes accessed | tf_op | source)
XLA Modules:
  0.0 181.8 jit_solution(3434424842530032869)
XLA Ops:
  0.7 1.4 pack.1
  2.1 0.5 collective-permute-start
  2.6 2.6 %collective-permute-start.1 = (f32[104,256]{1,0:T(8,128)S(1)}, f32[104,256]{1,0:T(8,128)S(1)}, u32[]{:S(2)}, u32[]{:S(2)}) collective-permute-start(f32[104,256]{1,0:T(8,128)S(1)} %get-tuple-element.99), channel_id=1, source_target_pairs={{0,2},{1,3},{2,0},{3,1},{4,6},{5,7},{6,4},{7,5},{8,10},{9,11},{10,... | collective-permute-start | bytes 319496 | tf_op jit(solution)/shard_map/bring_clouds/ppermute | solution.py:39
  5.2 2.6 %part_links.4 = (bf16[1024,256]{1,0:T(8,128)(2,1)S(1)}, bf16[1024,256]{1,0:T(8,128)(2,1)S(1)}) custom-call(f32[104,256]{1,0:T(8,128)S(1)} %get-tuple-element.97.ids_ref.refs_0_), custom_call_target="tpu_custom_call" | custom-call | flops 1048576000 | bytes 524288 | tf_op jit(solution)/shard_map/bring_clouds/part_links/pallas_call | solution.py:279
  7.9 2.6 %part_links.5 = (bf16[1024,256]{1,0:T(8,128)(2,1)S(1)}, bf16[1024,256]{1,0:T(8,128)(2,1)S(1)}) custom-call(f32[104,256]{1,0:T(8,128)S(1)} %collective-permute-done.ids_ref.refs_1_), custom_call_target="tpu_custom_call" | custom-call | flops 1048576000 | bytes 524288 | tf_op jit(solution)/shard_map/bring_clouds/part_links/pallas_call | solution.py:279
  10.8 4.4 %first_tables.1 = (f32[1024,128]{1,0:T(8,128)S(1)}, f32[40,1024]{1,0:T(8,128)S(1)}, f32[1024,128]{1,0:T(8,128)S(1)}, f32[1024,128]{1,0:T(8,128)S(1)}, f32[1024,1...) custom-call(f32[104,256]{1,0:T(8,128)S(1)} %get-tuple-element.97.ids_ref.refs_0_, ...), custom_call_target="tpu_custom_call" | custom-call | tf_op jit(solution)/shard_map/layer_one/first_tables/pallas_call | solution.py:345
  15.1 1.6 collective-permute-start.5
  17.1 1.1 collective-permute-done.5
  18.2 2.1 %collective-permute-done.4 = f32[2,128]{1,0:T(2,128)S(1)} collective-permute-done((f32[2,128]{1,0:T(2,128)S(1)}, f32[2,128]{1,0:T(2,128)S(1)}, u32[]{:S(2)}, u32[]{:S(2)}) %collective-permute-start.4) | collective-permute-done | bytes 1056 | tf_op jit(solution)/shard_map/layer_one/ppermute | solution.py:39
  20.3 1.6 collective-permute-start.6
  21.9 1.3 part_links.7.refs_3_
  23.2 0.7 collective-permute-done.6
  24.0 3.7 %collective-permute-start.9 = (f32[2,128]{1,0:T(2,128)S(1)}, f32[2,128]{1,0:T(2,128)S(1)}, u32[]{:S(2)}, u32[]{:S(2)}) collective-permute-start(f32[2,128]{1,0:T(2,128)S(1)} %pad_maximum_fusion.5), channel_id=1, source_target_pairs={{0,24},{4,28},{8,16},{12,20},{16,8},{20,12},{24,0},{28,4},{1,25},{... | collective-permute-start | bytes 3080 | tf_op jit(solution)/shard_map/layer_one/ppermute | solution.py:39
  27.6 0.8 collective-permute-start.7
  28.4 1.3 part_links.6.refs_2_
  29.7 2.3 %collective-permute-done.8 = f32[2,128]{1,0:T(2,128)S(1)} collective-permute-done((f32[2,128]{1,0:T(2,128)S(1)}, f32[2,128]{1,0:T(2,128)S(1)}, u32[]{:S(2)}, u32[]{:S(2)}) %collective-permute-start.8) | collective-permute-done | bytes 1056 | tf_op jit(solution)/shard_map/layer_one/ppermute | solution.py:39
  32.1 16.4 %edges.2 = (f32[1024,128]{1,0:T(8,128)S(1)}, f32[20,1024,128]{2,1,0:T(8,128)}, f32[1024,128]{1,0:T(8,128)S(1)}, f32[1024,128]{1,0:T(8,128)S(1)}, f32[1024,128]{1,0:T(8,128)S(1)}, /*index=5*/f32[1024,128]{1,0:T(8,128)S(1)}) custom-call(f32[1024,128]{1,0:T(8,128)S(1)} %get-tuple-element.104.x_ref, f32[1024,128]{1,0:T(8,128)S(1)} %get-tuple-element.105.a_ref, ...), custom_call_target="tpu_custom_call" | custom-call | tf_op jit(solution)/shard_map/layer_one/edges/pallas_call | solution.py:478
  48.5 2.6 %second_tables.1 = (f32[1024,256]{1,0:T(8,128)S(1)}, f32[1024,256]{1,0:T(8,128)S(1)}, f32[1024,256]{1,0:T(8,128)S(1)}, f32[1024,128]{1,0:T(8,128)S(1)}, f32[2,256]{1,0:T(2,128)S(1)}) custom-call(f32[1024,128]{1,0:T(8,128)S(1)} %get-tuple-element.109.x_ref, f32[256,256]{1,0:T(8,128)S(1)} %get-tuple-element.110.weight_ref, ...), custom_call_target="tpu_custom_call" | custom-call | tf_op jit(solution)/shard_map/layer_two/second_tables/pallas_call | solution.py:370
  51.2 0.6 collective-permute-start.11
  51.8 1.2 collective-permute-start.10
  53.1 1.1 collective-permute-done.12
  54.2 0.7 collective-permute-done.11
  54.9 1.6 collective-permute-start.13
  56.5 2.1 %collective-permute-done.13 = f32[2,256]{1,0:T(2,128)S(1)} collective-permute-done((f32[2,256]{1,0:T(2,128)S(1)}, f32[2,256]{1,0:T(2,128)S(1)}, u32[]{:S(2)}, u32[]{:S(2)}) %collective-permute-start.13) | collective-permute-done | bytes 2080 | tf_op jit(solution)/shard_map/layer_two/ppermute | solution.py:39
  58.6 1.5 collective-permute-start.16
  60.1 0.6 collective-permute-start.15
  60.8 2.3 %collective-permute-start.14 = (f32[2,256]{1,0:T(2,128)S(1)}, f32[2,256]{1,0:T(2,128)S(1)}, u32[]{:S(2)}, u32[]{:S(2)}) collective-permute-start(f32[2,256]{1,0:T(2,128)S(1)} %pad_maximum_fusion.2), channel_id=1, source_target_pairs={{0,8},{4,12},{8,0},{12,4},{16,24},{20,28},{24,16},{28,20},{1,9},{5... | collective-permute-start | bytes 6152 | tf_op jit(solution)/shard_map/layer_two/ppermute | solution.py:39
  63.1 1.3 split.13
  64.4 0.6 collective-permute-start.18
  65.0 1.2 collective-permute-start.19
  66.3 30.5 %edges.3 = (f32[1024,256]{1,0:T(8,128)S(1)}, f32[20,1024,256]{2,1,0:T(8,128)}, f32[1024,256]{1,0:T(8,128)S(1)}, f32[1024,256]{1,0:T(8,128)S(1)}, f32[1024,256]{1,0:T(8,128)S(1)}, /*index=5*/f32[1024,256]{1,0:T(8,128)S(1)}) custom-call(f32[1024,128]{1,0:T(8,128)S(1)} %get-tuple-element.104.x_ref, f32[1024,256]{1,0:T(8,128)S(1)} %get-tuple-element.113.a_ref, ...), custom_call_target="tpu_custom_call" | custom-call | tf_op jit(solution)/shard_map/layer_two/edges/pallas_call | solution.py:478
  96.8 0.9 pools.1
  98.1 0.6 collective-permute-start.21
  98.7 1.0 collective-permute-start.22
  99.6 13.5 %scatter.4.refs_0_ = f32[1024,256]{1,0:T(8,128)S(1)} custom-call(f32[40,1024]{1,0:T(8,128)S(1)} %get-tuple-element.135.ids_ref, f32[1024,256]{1,0:T(8,128)S(1)} %get-tuple-element.143.grad_ref, f32[1,256]{1,0:T(1,128)S(1)} %get-tuple-element.137.largest_ref, f32[20,1024,256]{2,1,0:T(8,128)} %get-tuple-element.138.weight_ref), custom_call_target="tpu_custom_call" | custom-call | flops 12884901888 | bytes 12582912 | tf_op jit(solution)/shard_map/layer_two_back/scatter/pallas_call | solution.py:585
  113.2 1.5 collective-permute-start.25
  115.1 2.6 %collective-permute-start.23 = (f32[2,256]{1,0:T(2,128)S(1)}, f32[2,256]{1,0:T(2,128)S(1)}, u32[]{:S(2)}, u32[]{:S(2)}) collective-permute-start(f32[2,256]{1,0:T(2,128)S(1)} %add_add_fusion.5), channel_id=1, source_target_pairs={{0,8},{4,12},{8,0},{12,4},{16,24},{20,28},{24,16},{28,20},{1,9},{5... | collective-permute-start | bytes 6152 | tf_op jit(solution)/shard_map/layer_two_back/ppermute | solution.py:39
  117.6 9.7 %scatter.5.refs_1_ = f32[1024,256]{1,0:T(8,128)S(1)} custom-call(f32[40,1024]{1,0:T(8,128)S(1)} %get-tuple-element.135.ids_ref, f32[1024,256]{1,0:T(8,128)S(1)} %get-tuple-element.143.grad_ref, f32[1,256]{1,0:T(1,128)S(1)} %get-tuple-element.137.largest_ref, f32[20,1024,256]{2,1,0:T(8,128)} %get-tuple-element.138.weight_ref), custom_call_target="tpu_custom_call" | custom-call | flops 8589934592 | bytes 8388608 | tf_op jit(solution)/shard_map/layer_two_back/scatter/pallas_call | solution.py:585
  127.4 1.6 collective-permute-start.26
  129.0 2.1 %collective-permute-done.26 = f32[2,256]{1,0:T(2,128)S(1)} collective-permute-done((f32[2,256]{1,0:T(2,128)S(1)}, f32[2,256]{1,0:T(2,128)S(1)}, u32[]{:S(2)}, u32[]{:S(2)}) %collective-permute-start.26) | collective-permute-done | bytes 2080 | tf_op jit(solution)/shard_map/layer_two_back/ppermute | solution.py:39
  131.0 3.2 %middle.1 = (f32[72,256]{1,0:T(8,128)S(1)}, f32[72,256]{1,0:T(8,128)S(1)}, f32[72,256]{1,0:T(8,128)S(1)}, f32[72,256]{1,0:T(8,128)S(1)}, f32[1024,128]{1,0:T(8,1...) custom-call(s32[1]{0:T(128)} %bitcast.me_ref, f32[1024,256]{1,0:T(8,128)S(1)} %get-tuple-element.131.own_ref, ...), custom_call_target="tpu_custom_call" | custom-call | tf_op jit(solution)/shard_map/layer_two_back/middle/pallas_call | solution.py:682
  134.2 0.6 collective-permute-start.28
  134.8 1.3 collective-permute-start.29
  136.1 8.8 %scatter.6.refs_0_ = f32[1024,128]{1,0:T(8,128)S(1)} custom-call(f32[40,1024]{1,0:T(8,128)S(1)} %get-tuple-element.135.ids_ref, f32[1024,128]{1,0:T(8,128)S(1)} %get-tuple-element.165.grad_ref, f32[1,128]{1,0:T(1,128)S(1)} %slice.170.largest_ref, f32[20,1024,128]{2,1,0:T(8,128)} %get-tuple-element.160.weight_ref), custom_call_target="tpu_custom_call" | custom-call | flops 6442450944 | bytes 6291456 | tf_op jit(solution)/shard_map/layer_one_back/scatter/pallas_call | solution.py:585
  145.0 1.5 collective-permute-start.32
  146.5 2.9 %collective-permute-start.30 = (f32[72,256]{1,0:T(8,128)S(1)}, f32[72,256]{1,0:T(8,128)S(1)}, u32[]{:S(2)}, u32[]{:S(2)}) collective-permute-start(f32[72,256]{1,0:T(8,128)S(1)} %add_add_fusion.1), channel_id=1, source_target_pairs={{0,8},{4,12},{8,0},{12,4},{16,24},{20,28},{24,16},{28,20},{1,9},{5... | collective-permute-start | bytes 221192 | tf_op jit(solution)/shard_map/layer_one_back/ppermute | solution.py:39
  149.4 6.4 %scatter.7.refs_1_ = f32[1024,128]{1,0:T(8,128)S(1)} custom-call(f32[40,1024]{1,0:T(8,128)S(1)} %get-tuple-element.135.ids_ref, f32[1024,128]{1,0:T(8,128)S(1)} %get-tuple-element.165.grad_ref, f32[1,128]{1,0:T(1,128)S(1)} %slice.170.largest_ref, f32[20,1024,128]{2,1,0:T(8,128)} %get-tuple-element.160.weight_ref), custom_call_target="tpu_custom_call" | custom-call | flops 4294967296 | bytes 4194304 | tf_op jit(solution)/shard_map/layer_one_back/scatter/pallas_call | solution.py:585
  155.9 1.6 collective-permute-start.33
  157.5 2.8 %collective-permute-done.33 = f32[72,256]{1,0:T(8,128)S(1)} collective-permute-done((f32[72,256]{1,0:T(8,128)S(1)}, f32[72,256]{1,0:T(8,128)S(1)}, u32[]{:S(2)}, u32[]{:S(2)}) %collective-permute-start.33) | collective-permute-done | bytes 73760 | tf_op jit(solution)/shard_map/layer_one_back/ppermute | solution.py:39
  160.3 1.6 last.1
  161.9 0.6 collective-permute-start.35
  162.6 1.2 collective-permute-start.34
  163.8 1.9 %collective-permute-done.36 = f32[64,256]{1,0:T(8,128)S(1)} collective-permute-done((f32[64,256]{1,0:T(8,128)S(1)}, f32[64,256]{1,0:T(8,128)S(1)}, u32[]{:S(2)}, u32[]{:S(2)}) %collective-permute-start.36) | collective-permute-done | bytes 65568 | tf_op jit(solution)/shard_map/layer_one_back/ppermute | solution.py:39
  165.7 1.2 collective-permute-done.35
  167.1 1.6 collective-permute-start.40
  168.7 1.0 unpack_output.1
  169.7 0.6 slice.188
  170.3 1.3 collective-permute-start.38
  171.7 1.5 collective-permute-start.43
  173.3 2.9 %collective-permute-start.41 = (f32[64,256]{1,0:T(8,128)S(1)}, f32[64,256]{1,0:T(8,128)S(1)}, u32[]{:S(2)}, u32[]{:S(2)}) collective-permute-start(f32[64,256]{1,0:T(8,128)S(1)} %add.272), channel_id=1, source_target_pairs={{0,8},{4,12},{8,0},{12,4},{16,24},{20,28},{24,16},{28,20},{1,9},{5... | collective-permute-start | bytes 196616 | tf_op jit(solution)/shard_map/layer_one_back/ppermute | solution.py:39
  176.7 1.0 collective-permute-done.39.refs_3_
  177.7 0.8 unpack_grad.1
  178.7 2.5 %collective-permute-done.42 = f32[64,256]{1,0:T(8,128)S(1)} collective-permute-done((f32[64,256]{1,0:T(8,128)S(1)}, f32[64,256]{1,0:T(8,128)S(1)}, u32[]{:S(2)}, u32[]{:S(2)}) %collective-permute-start.42) | collective-permute-done | bytes 65568 | tf_op jit(solution)/shard_map/layer_one_back/ppermute | solution.py:39
  181.1 0.6 pad_maximum_fusion
  (73 shorter events, 2.9 us)
Async XLA Ops:
  0.6 96.2 %copy-start.1 = (f32[4,256]{1,0:T(4,128)S(1)}, f32[4,256]{1,0:T(4,128)}, u32[]{:S(2)}) copy-start(f32[4,256]{1,0:T(4,128)} %gmean_ref.1) | copy-start | bytes 12292
  0.7 96.2 %copy-start = (f32[4,256]{1,0:T(4,128)S(1)}, f32[4,256]{1,0:T(4,128)}, u32[]{:S(2)}) copy-start(f32[4,256]{1,0:T(4,128)} %gmax_ref.1) | copy-start | bytes 12292
  2.1 5.8 %collective-permute-start = (f32[104,256]{1,0:T(8,128)S(1)}, f32[104,256]{1,0:T(8,128)S(1)}, u32[]{:S(2)}, u32[]{:S(2)}) collective-permute-start(f32[104,256]{1,0:T(8,128)S(1)} %get-tuple-element.98), channel_id=1, source_target_pairs={{0,1},{1,0},{2,3},{3,2},{4,5},{5,4},{6,7},{7,6},{8,9},{9,8},{10,11... | collective-permute-start | bytes 319496 | tf_op jit(solution)/shard_map/bring_clouds/ppermute | solution.py:39
  2.6 8.0 %collective-permute-start.1 = (f32[104,256]{1,0:T(8,128)S(1)}, f32[104,256]{1,0:T(8,128)S(1)}, u32[]{:S(2)}, u32[]{:S(2)}) collective-permute-start(f32[104,256]{1,0:T(8,128)S(1)} %get-tuple-element.99), channel_id=1, source_target_pairs={{0,2},{1,3},{2,0},{3,1},{4,6},{5,7},{6,4},{7,5},{8,10},{9,11},{10,... | collective-permute-start | bytes 319496 | tf_op jit(solution)/shard_map/bring_clouds/ppermute | solution.py:39
  5.2 5.6 %collective-permute-start.2 = (f32[104,256]{1,0:T(8,128)S(1)}, f32[104,256]{1,0:T(8,128)S(1)}, u32[]{:S(2)}, u32[]{:S(2)}) collective-permute-start(f32[104,256]{1,0:T(8,128)S(1)} %get-tuple-element.100), channel_id=1, source_target_pairs={{0,3},{1,2},{2,1},{3,0},{4,7},{5,6},{6,5},{7,4},{8,11},{9,10},{10,... | collective-permute-start | bytes 319496 | tf_op jit(solution)/shard_map/bring_clouds/ppermute | solution.py:39
  15.1 3.1 %collective-permute-start.5 = (f32[2,128]{1,0:T(2,128)S(1)}, f32[2,128]{1,0:T(2,128)S(1)}, u32[]{:S(2)}, u32[]{:S(2)}) collective-permute-start(f32[2,128]{1,0:T(2,128)S(1)} %get-tuple-element.107.local_ref), channel_id=1, source_target_pairs={{0,3},{1,2},{2,1},{3,0},{4,7},{5,6},{6,5},{7,4},{8,11},{9,10},{10,... | collective-permute-start | bytes 3080 | tf_op jit(solution)/shard_map/layer_one/ppermute | solution.py:39
  16.7 3.6 %collective-permute-start.4 = (f32[2,128]{1,0:T(2,128)S(1)}, f32[2,128]{1,0:T(2,128)S(1)}, u32[]{:S(2)}, u32[]{:S(2)}) collective-permute-start(f32[2,128]{1,0:T(2,128)S(1)} %get-tuple-element.107.local_ref), channel_id=1, source_target_pairs={{0,2},{1,3},{2,0},{3,1},{4,6},{5,7},{6,4},{7,5},{8,10},{9,11},{10,... | collective-permute-start | bytes 3080 | tf_op jit(solution)/shard_map/layer_one/ppermute | solution.py:39
  16.9 3.3 %collective-permute-start.3 = (f32[2,128]{1,0:T(2,128)S(1)}, f32[2,128]{1,0:T(2,128)S(1)}, u32[]{:S(2)}, u32[]{:S(2)}) collective-permute-start(f32[2,128]{1,0:T(2,128)S(1)} %get-tuple-element.107.local_ref), channel_id=1, source_target_pairs={{0,1},{1,0},{2,3},{3,2},{4,5},{5,4},{6,7},{7,6},{8,9},{9,8},{10,11... | collective-permute-start | bytes 3080 | tf_op jit(solution)/shard_map/layer_one/ppermute | solution.py:39
  20.3 3.6 %collective-permute-start.6 = (f32[2,128]{1,0:T(2,128)S(1)}, f32[2,128]{1,0:T(2,128)S(1)}, u32[]{:S(2)}, u32[]{:S(2)}) collective-permute-start(f32[2,128]{1,0:T(2,128)S(1)} %pad_maximum_fusion.4), channel_id=1, source_target_pairs={{0,4},{4,0},{8,12},{12,8},{16,20},{20,16},{24,28},{28,24},{1,5},{5... | collective-permute-start | bytes 3080 | tf_op jit(solution)/shard_map/layer_one/ppermute | solution.py:39
  24.0 5.8 %collective-permute-start.9 = (f32[2,128]{1,0:T(2,128)S(1)}, f32[2,128]{1,0:T(2,128)S(1)}, u32[]{:S(2)}, u32[]{:S(2)}) collective-permute-start(f32[2,128]{1,0:T(2,128)S(1)} %pad_maximum_fusion.5), channel_id=1, source_target_pairs={{0,24},{4,28},{8,16},{12,20},{16,8},{20,12},{24,0},{28,4},{1,25},{... | collective-permute-start | bytes 3080 | tf_op jit(solution)/shard_map/layer_one/ppermute | solution.py:39
  27.6 4.5 %collective-permute-start.8 = (f32[2,128]{1,0:T(2,128)S(1)}, f32[2,128]{1,0:T(2,128)S(1)}, u32[]{:S(2)}, u32[]{:S(2)}) collective-permute-start(f32[2,128]{1,0:T(2,128)S(1)} %pad_maximum_fusion.5), channel_id=1, source_target_pairs={{0,16},{4,20},{8,24},{12,28},{16,0},{20,4},{24,8},{28,12},{1,17},{... | collective-permute-start | bytes 3080 | tf_op jit(solution)/shard_map/layer_one/ppermute | solution.py:39
  27.6 4.5 %collective-permute-start.7 = (f32[2,128]{1,0:T(2,128)S(1)}, f32[2,128]{1,0:T(2,128)S(1)}, u32[]{:S(2)}, u32[]{:S(2)}) collective-permute-start(f32[2,128]{1,0:T(2,128)S(1)} %pad_maximum_fusion.5), channel_id=1, source_target_pairs={{0,8},{4,12},{8,0},{12,4},{16,24},{20,28},{24,16},{28,20},{1,9},{5... | collective-permute-start | bytes 3080 | tf_op jit(solution)/shard_map/layer_one/ppermute | solution.py:39
  51.2 3.1 %collective-permute-start.12 = (f32[2,256]{1,0:T(2,128)S(1)}, f32[2,256]{1,0:T(2,128)S(1)}, u32[]{:S(2)}, u32[]{:S(2)}) collective-permute-start(f32[2,256]{1,0:T(2,128)S(1)} %get-tuple-element.115.local_ref), channel_id=1, source_target_pairs={{0,3},{1,2},{2,1},{3,0},{4,7},{5,6},{6,5},{7,4},{8,11},{9,10},{10,... | collective-permute-start | bytes 6152 | tf_op jit(solution)/shard_map/layer_two/ppermute | solution.py:39
  51.2 3.7 %collective-permute-start.11 = (f32[2,256]{1,0:T(2,128)S(1)}, f32[2,256]{1,0:T(2,128)S(1)}, u32[]{:S(2)}, u32[]{:S(2)}) collective-permute-start(f32[2,256]{1,0:T(2,128)S(1)} %get-tuple-element.115.local_ref), channel_id=1, source_target_pairs={{0,2},{1,3},{2,0},{3,1},{4,6},{5,7},{6,4},{7,5},{8,10},{9,11},{10,... | collective-permute-start | bytes 6152 | tf_op jit(solution)/shard_map/layer_two/ppermute | solution.py:39
  51.8 3.1 %collective-permute-start.10 = (f32[2,256]{1,0:T(2,128)S(1)}, f32[2,256]{1,0:T(2,128)S(1)}, u32[]{:S(2)}, u32[]{:S(2)}) collective-permute-start(f32[2,256]{1,0:T(2,128)S(1)} %get-tuple-element.115.local_ref), channel_id=1, source_target_pairs={{0,1},{1,0},{2,3},{3,2},{4,5},{5,4},{6,7},{7,6},{8,9},{9,8},{10,11... | collective-permute-start | bytes 6152 | tf_op jit(solution)/shard_map/layer_two/ppermute | solution.py:39
  54.9 3.7 %collective-permute-start.13 = (f32[2,256]{1,0:T(2,128)S(1)}, f32[2,256]{1,0:T(2,128)S(1)}, u32[]{:S(2)}, u32[]{:S(2)}) collective-permute-start(f32[2,256]{1,0:T(2,128)S(1)} %pad_maximum_fusion.1), channel_id=1, source_target_pairs={{0,4},{4,0},{8,12},{12,8},{16,20},{20,16},{24,28},{28,24},{1,5},{5... | collective-permute-start | bytes 6152 | tf_op jit(solution)/shard_map/layer_two/ppermute | solution.py:39
  58.6 6.4 %collective-permute-start.16 = (f32[2,256]{1,0:T(2,128)S(1)}, f32[2,256]{1,0:T(2,128)S(1)}, u32[]{:S(2)}, u32[]{:S(2)}) collective-permute-start(f32[2,256]{1,0:T(2,128)S(1)} %pad_maximum_fusion.2), channel_id=1, source_target_pairs={{0,24},{4,28},{8,16},{12,20},{16,8},{20,12},{24,0},{28,4},{1,25},{... | collective-permute-start | bytes 6152 | tf_op jit(solution)/shard_map/layer_two/ppermute | solution.py:39
  60.1 6.2 %collective-permute-start.15 = (f32[2,256]{1,0:T(2,128)S(1)}, f32[2,256]{1,0:T(2,128)S(1)}, u32[]{:S(2)}, u32[]{:S(2)}) collective-permute-start(f32[2,256]{1,0:T(2,128)S(1)} %pad_maximum_fusion.2), channel_id=1, source_target_pairs={{0,16},{4,20},{8,24},{12,28},{16,0},{20,4},{24,8},{28,12},{1,17},{... | collective-permute-start | bytes 6152 | tf_op jit(solution)/shard_map/layer_two/ppermute | solution.py:39
  60.8 5.5 %collective-permute-start.14 = (f32[2,256]{1,0:T(2,128)S(1)}, f32[2,256]{1,0:T(2,128)S(1)}, u32[]{:S(2)}, u32[]{:S(2)}) collective-permute-start(f32[2,256]{1,0:T(2,128)S(1)} %pad_maximum_fusion.2), channel_id=1, source_target_pairs={{0,8},{4,12},{8,0},{12,4},{16,24},{20,28},{24,16},{28,20},{1,9},{5... | collective-permute-start | bytes 6152 | tf_op jit(solution)/shard_map/layer_two/ppermute | solution.py:39
  64.4 32.5 %collective-permute-start.17 = (f32[256,256]{1,0:T(8,128)S(1)}, f32[256,256]{1,0:T(8,128)S(1)}, u32[]{:S(2)}, u32[]{:S(2)}) collective-permute-start(f32[256,256]{1,0:T(8,128)S(1)} %get-tuple-element.121), channel_id=1, source_target_pairs={{0,1},{1,0},{2,3},{3,2},{4,5},{5,4},{6,7},{7,6},{8,9},{9,8},{10,11... | collective-permute-start | bytes 786440 | tf_op jit(solution)/shard_map/bring_cotangents/ppermute | solution.py:39
  64.4 32.4 %collective-permute-start.18 = (f32[256,256]{1,0:T(8,128)S(1)}, f32[256,256]{1,0:T(8,128)S(1)}, u32[]{:S(2)}, u32[]{:S(2)}) collective-permute-start(f32[256,256]{1,0:T(8,128)S(1)} %get-tuple-element.122), channel_id=1, source_target_pairs={{0,2},{1,3},{2,0},{3,1},{4,6},{5,7},{6,4},{7,5},{8,10},{9,11},{10,... | collective-permute-start | bytes 786440 | tf_op jit(solution)/shard_map/bring_cotangents/ppermute | solution.py:39
  65.0 31.8 %collective-permute-start.19 = (f32[256,256]{1,0:T(8,128)S(1)}, f32[256,256]{1,0:T(8,128)S(1)}, u32[]{:S(2)}, u32[]{:S(2)}) collective-permute-start(f32[256,256]{1,0:T(8,128)S(1)} %get-tuple-element.123), channel_id=1, source_target_pairs={{0,3},{1,2},{2,1},{3,0},{4,7},{5,6},{6,5},{7,4},{8,11},{9,10},{10,... | collective-permute-start | bytes 786440 | tf_op jit(solution)/shard_map/bring_cotangents/ppermute | solution.py:39
  97.7 15.4 %collective-permute-start.20 = (f32[264,256]{1,0:T(8,128)S(1)}, f32[264,256]{1,0:T(8,128)S(1)}, u32[]{:S(2)}, u32[]{:S(2)}) collective-permute-start(f32[264,256]{1,0:T(8,128)S(1)} %get-tuple-element.125), channel_id=1, source_target_pairs={{0,1},{1,0},{2,3},{3,2},{4,5},{5,4},{6,7},{7,6},{8,9},{9,8},{10,11... | collective-permute-start | bytes 811016 | tf_op jit(solution)/shard_map/pools/ppermute | solution.py:39
  98.1 15.0 %collective-permute-start.21 = (f32[264,256]{1,0:T(8,128)S(1)}, f32[264,256]{1,0:T(8,128)S(1)}, u32[]{:S(2)}, u32[]{:S(2)}) collective-permute-start(f32[264,256]{1,0:T(8,128)S(1)} %get-tuple-element.126), channel_id=1, source_target_pairs={{0,2},{1,3},{2,0},{3,1},{4,6},{5,7},{6,4},{7,5},{8,10},{9,11},{10,... | collective-permute-start | bytes 811016 | tf_op jit(solution)/shard_map/pools/ppermute | solution.py:39
  98.7 14.5 %collective-permute-start.22 = (f32[264,256]{1,0:T(8,128)S(1)}, f32[264,256]{1,0:T(8,128)S(1)}, u32[]{:S(2)}, u32[]{:S(2)}) collective-permute-start(f32[264,256]{1,0:T(8,128)S(1)} %get-tuple-element.127), channel_id=1, source_target_pairs={{0,3},{1,2},{2,1},{3,0},{4,7},{5,6},{6,5},{7,4},{8,11},{9,10},{10,... | collective-permute-start | bytes 811016 | tf_op jit(solution)/shard_map/pools/ppermute | solution.py:39
  113.2 14.2 %collective-permute-start.25 = (f32[2,256]{1,0:T(2,128)S(1)}, f32[2,256]{1,0:T(2,128)S(1)}, u32[]{:S(2)}, u32[]{:S(2)}) collective-permute-start(f32[2,256]{1,0:T(2,128)S(1)} %add_add_fusion.5), channel_id=1, source_target_pairs={{0,24},{4,28},{8,16},{12,20},{16,8},{20,12},{24,0},{28,4},{1,25},{... | collective-permute-start | bytes 6152 | tf_op jit(solution)/shard_map/layer_two_back/ppermute | solution.py:39
  114.7 12.6 %collective-permute-start.24 = (f32[2,256]{1,0:T(2,128)S(1)}, f32[2,256]{1,0:T(2,128)S(1)}, u32[]{:S(2)}, u32[]{:S(2)}) collective-permute-start(f32[2,256]{1,0:T(2,128)S(1)} %add_add_fusion.5), channel_id=1, source_target_pairs={{0,16},{4,20},{8,24},{12,28},{16,0},{20,4},{24,8},{28,12},{1,17},{... | collective-permute-start | bytes 6152 | tf_op jit(solution)/shard_map/layer_two_back/ppermute | solution.py:39
  115.1 12.3 %collective-permute-start.23 = (f32[2,256]{1,0:T(2,128)S(1)}, f32[2,256]{1,0:T(2,128)S(1)}, u32[]{:S(2)}, u32[]{:S(2)}) collective-permute-start(f32[2,256]{1,0:T(2,128)S(1)} %add_add_fusion.5), channel_id=1, source_target_pairs={{0,8},{4,12},{8,0},{12,4},{16,24},{20,28},{24,16},{28,20},{1,9},{5... | collective-permute-start | bytes 6152 | tf_op jit(solution)/shard_map/layer_two_back/ppermute | solution.py:39
  127.4 3.7 %collective-permute-start.26 = (f32[2,256]{1,0:T(2,128)S(1)}, f32[2,256]{1,0:T(2,128)S(1)}, u32[]{:S(2)}, u32[]{:S(2)}) collective-permute-start(f32[2,256]{1,0:T(2,128)S(1)} %add_add_fusion.4), channel_id=1, source_target_pairs={{0,4},{4,0},{8,12},{12,8},{16,20},{20,16},{24,28},{28,24},{1,5},{5... | collective-permute-start | bytes 6152 | tf_op jit(solution)/shard_map/layer_two_back/ppermute | solution.py:39
  134.2 10.7 %collective-permute-start.27 = (f32[72,256]{1,0:T(8,128)S(1)}, f32[72,256]{1,0:T(8,128)S(1)}, u32[]{:S(2)}, u32[]{:S(2)}) collective-permute-start(f32[72,256]{1,0:T(8,128)S(1)} %get-tuple-element.156), channel_id=1, source_target_pairs={{0,1},{1,0},{2,3},{3,2},{4,5},{5,4},{6,7},{7,6},{8,9},{9,8},{10,11... | collective-permute-start | bytes 221192 | tf_op jit(solution)/shard_map/layer_one_back/ppermute | solution.py:39
  134.2 10.7 %collective-permute-start.28 = (f32[72,256]{1,0:T(8,128)S(1)}, f32[72,256]{1,0:T(8,128)S(1)}, u32[]{:S(2)}, u32[]{:S(2)}) collective-permute-start(f32[72,256]{1,0:T(8,128)S(1)} %get-tuple-element.157), channel_id=1, source_target_pairs={{0,2},{1,3},{2,0},{3,1},{4,6},{5,7},{6,4},{7,5},{8,10},{9,11},{10,... | collective-permute-start | bytes 221192 | tf_op jit(solution)/shard_map/layer_one_back/ppermute | solution.py:39
  134.8 10.2 %collective-permute-start.29 = (f32[72,256]{1,0:T(8,128)S(1)}, f32[72,256]{1,0:T(8,128)S(1)}, u32[]{:S(2)}, u32[]{:S(2)}) collective-permute-start(f32[72,256]{1,0:T(8,128)S(1)} %get-tuple-element.158), channel_id=1, source_target_pairs={{0,3},{1,2},{2,1},{3,0},{4,7},{5,6},{6,5},{7,4},{8,11},{9,10},{10,... | collective-permute-start | bytes 221192 | tf_op jit(solution)/shard_map/layer_one_back/ppermute | solution.py:39
  145.0 10.9 %collective-permute-start.32 = (f32[72,256]{1,0:T(8,128)S(1)}, f32[72,256]{1,0:T(8,128)S(1)}, u32[]{:S(2)}, u32[]{:S(2)}) collective-permute-start(f32[72,256]{1,0:T(8,128)S(1)} %add_add_fusion.1), channel_id=1, source_target_pairs={{0,24},{4,28},{8,16},{12,20},{16,8},{20,12},{24,0},{28,4},{1,25},{... | collective-permute-start | bytes 221192 | tf_op jit(solution)/shard_map/layer_one_back/ppermute | solution.py:39
  146.5 9.4 %collective-permute-start.31 = (f32[72,256]{1,0:T(8,128)S(1)}, f32[72,256]{1,0:T(8,128)S(1)}, u32[]{:S(2)}, u32[]{:S(2)}) collective-permute-start(f32[72,256]{1,0:T(8,128)S(1)} %add_add_fusion.1), channel_id=1, source_target_pairs={{0,16},{4,20},{8,24},{12,28},{16,0},{20,4},{24,8},{28,12},{1,17},{... | collective-permute-start | bytes 221192 | tf_op jit(solution)/shard_map/layer_one_back/ppermute | solution.py:39
  146.5 9.4 %collective-permute-start.30 = (f32[72,256]{1,0:T(8,128)S(1)}, f32[72,256]{1,0:T(8,128)S(1)}, u32[]{:S(2)}, u32[]{:S(2)}) collective-permute-start(f32[72,256]{1,0:T(8,128)S(1)} %add_add_fusion.1), channel_id=1, source_target_pairs={{0,8},{4,12},{8,0},{12,4},{16,24},{20,28},{24,16},{28,20},{1,9},{5... | collective-permute-start | bytes 221192 | tf_op jit(solution)/shard_map/layer_one_back/ppermute | solution.py:39
  155.9 4.4 %collective-permute-start.33 = (f32[72,256]{1,0:T(8,128)S(1)}, f32[72,256]{1,0:T(8,128)S(1)}, u32[]{:S(2)}, u32[]{:S(2)}) collective-permute-start(f32[72,256]{1,0:T(8,128)S(1)} %add_add_fusion), channel_id=1, source_target_pairs={{0,4},{4,0},{8,12},{12,8},{16,20},{20,16},{24,28},{28,24},{1,5},{5... | collective-permute-start | bytes 221192 | tf_op jit(solution)/shard_map/layer_one_back/ppermute | solution.py:39
  161.9 3.8 %collective-permute-start.36 = (f32[64,256]{1,0:T(8,128)S(1)}, f32[64,256]{1,0:T(8,128)S(1)}, u32[]{:S(2)}, u32[]{:S(2)}) collective-permute-start(f32[64,256]{1,0:T(8,128)S(1)} %get-tuple-element.170), channel_id=1, source_target_pairs={{0,3},{1,2},{2,1},{3,0},{4,7},{5,6},{6,5},{7,4},{8,11},{9,10},{10,... | collective-permute-start | bytes 196616 | tf_op jit(solution)/shard_map/layer_one_back/ppermute | solution.py:39
  161.9 5.0 %collective-permute-start.35 = (f32[64,256]{1,0:T(8,128)S(1)}, f32[64,256]{1,0:T(8,128)S(1)}, u32[]{:S(2)}, u32[]{:S(2)}) collective-permute-start(f32[64,256]{1,0:T(8,128)S(1)} %get-tuple-element.170), channel_id=1, source_target_pairs={{0,2},{1,3},{2,0},{3,1},{4,6},{5,7},{6,4},{7,5},{8,10},{9,11},{10,... | collective-permute-start | bytes 196616 | tf_op jit(solution)/shard_map/layer_one_back/ppermute | solution.py:39
  162.6 4.4 %collective-permute-start.34 = (f32[64,256]{1,0:T(8,128)S(1)}, f32[64,256]{1,0:T(8,128)S(1)}, u32[]{:S(2)}, u32[]{:S(2)}) collective-permute-start(f32[64,256]{1,0:T(8,128)S(1)} %get-tuple-element.170), channel_id=1, source_target_pairs={{0,1},{1,0},{2,3},{3,2},{4,5},{5,4},{6,7},{7,6},{8,9},{9,8},{10,11... | collective-permute-start | bytes 196616 | tf_op jit(solution)/shard_map/layer_one_back/ppermute | solution.py:39
  166.9 6.3 %collective-permute-start.37 = (f32[128,256]{1,0:T(8,128)S(1)}, f32[128,256]{1,0:T(8,128)S(1)}, u32[]{:S(2)}, u32[]{:S(2)}) collective-permute-start(f32[128,256]{1,0:T(8,128)S(1)} %get-tuple-element.176), channel_id=1, source_target_pairs={{0,1},{1,0},{2,3},{3,2},{4,5},{5,4},{6,7},{7,6},{8,9},{9,8},{10,11... | collective-permute-start | bytes 393224 | tf_op jit(solution)/shard_map/layer_one_back/ppermute | solution.py:39
  167.1 4.6 %collective-permute-start.40 = (f32[64,256]{1,0:T(8,128)S(1)}, f32[64,256]{1,0:T(8,128)S(1)}, u32[]{:S(2)}, u32[]{:S(2)}) collective-permute-start(f32[64,256]{1,0:T(8,128)S(1)} %add_add_fusion.3), channel_id=1, source_target_pairs={{0,4},{4,0},{8,12},{12,8},{16,20},{20,16},{24,28},{28,24},{1,5},{5... | collective-permute-start | bytes 196616 | tf_op jit(solution)/shard_map/layer_one_back/ppermute | solution.py:39
  170.3 6.4 %collective-permute-start.38 = (f32[128,256]{1,0:T(8,128)S(1)}, f32[128,256]{1,0:T(8,128)S(1)}, u32[]{:S(2)}, u32[]{:S(2)}) collective-permute-start(f32[128,256]{1,0:T(8,128)S(1)} %get-tuple-element.177), channel_id=1, source_target_pairs={{0,2},{1,3},{2,0},{3,1},{4,6},{5,7},{6,4},{7,5},{8,10},{9,11},{10,... | collective-permute-start | bytes 393224 | tf_op jit(solution)/shard_map/layer_one_back/ppermute | solution.py:39
  171.6 6.1 %collective-permute-start.39 = (f32[128,256]{1,0:T(8,128)S(1)}, f32[128,256]{1,0:T(8,128)S(1)}, u32[]{:S(2)}, u32[]{:S(2)}) collective-permute-start(f32[128,256]{1,0:T(8,128)S(1)} %get-tuple-element.178), channel_id=1, source_target_pairs={{0,3},{1,2},{2,1},{3,0},{4,7},{5,6},{6,5},{7,4},{8,11},{9,10},{10,... | collective-permute-start | bytes 393224 | tf_op jit(solution)/shard_map/layer_one_back/ppermute | solution.py:39
  171.7 6.9 %collective-permute-start.43 = (f32[64,256]{1,0:T(8,128)S(1)}, f32[64,256]{1,0:T(8,128)S(1)}, u32[]{:S(2)}, u32[]{:S(2)}) collective-permute-start(f32[64,256]{1,0:T(8,128)S(1)} %add.272), channel_id=1, source_target_pairs={{0,24},{4,28},{8,16},{12,20},{16,8},{20,12},{24,0},{28,4},{1,25},{... | collective-permute-start | bytes 196616 | tf_op jit(solution)/shard_map/layer_one_back/ppermute | solution.py:39
  173.3 7.8 %collective-permute-start.42 = (f32[64,256]{1,0:T(8,128)S(1)}, f32[64,256]{1,0:T(8,128)S(1)}, u32[]{:S(2)}, u32[]{:S(2)}) collective-permute-start(f32[64,256]{1,0:T(8,128)S(1)} %add.272), channel_id=1, source_target_pairs={{0,16},{4,20},{8,24},{12,28},{16,0},{20,4},{24,8},{28,12},{1,17},{... | collective-permute-start | bytes 196616 | tf_op jit(solution)/shard_map/layer_one_back/ppermute | solution.py:39
  173.3 7.8 %collective-permute-start.41 = (f32[64,256]{1,0:T(8,128)S(1)}, f32[64,256]{1,0:T(8,128)S(1)}, u32[]{:S(2)}, u32[]{:S(2)}) collective-permute-start(f32[64,256]{1,0:T(8,128)S(1)} %add.272), channel_id=1, source_target_pairs={{0,8},{4,12},{8,0},{12,4},{16,24},{20,28},{24,16},{28,20},{1,9},{5... | collective-permute-start | bytes 196616 | tf_op jit(solution)/shard_map/layer_one_back/ppermute | solution.py:39

commit v3 on v2

--- a/solution.py
+++ b/solution.py
@@ -79,13 +79,14 @@
 
 
 def sum_beside(message, received, work):
-    (axis, masks), *rest = list(stages())[:0:-1]
-    first = work[0](None)
-    total = message(lax.optimization_barrier((*received, first))[:-1])
-    moving = swap(total, axis, masks)
-    second = work[1](total)
-    total = pair_sum(list(lax.optimization_barrier((*moving, second))[:-1]))
-    return sum_stages(total, rest), [first, second]
+    cloud_stages = list(stages())[:0:-1]
+    done = [work[0](None)]
+    total = message(lax.optimization_barrier((*received, done[0]))[:-1])
+    for piece, (axis, masks) in zip(work[1:], cloud_stages):
+        moving = swap(total, axis, masks)
+        done.append(piece(total))
+        total = pair_sum(list(lax.optimization_barrier((*moving, done[-1]))[:-1]))
+    return sum_stages(total, cloud_stages[len(work) - 1 :]), done
 
 
 def join_stats(stat, count):
@@ -223,16 +224,23 @@
     return x[:, :half] + x[:, half:]
 
 
-def product(x, y, on_x, on_y):
-    x_high, y_high = x.astype(jnp.bfloat16), y.astype(jnp.bfloat16)
-    x_low = (x - x_high.astype(jnp.float32)).astype(jnp.bfloat16)
-    y_low = (y - y_high.astype(jnp.float32)).astype(jnp.bfloat16)
+def terms_of(x):
+    high = x.astype(jnp.bfloat16)
+    return high, (x - high.astype(jnp.float32)).astype(jnp.bfloat16)
+
+
+def term_product(x_terms, y_terms, on_x, on_y):
+    (x_high, x_low), (y_high, y_low) = x_terms, y_terms
     return lax.dot_general(
         jnp.concatenate([x_high, x_low, x_high], axis=on_x),
         jnp.concatenate([y_high, y_high, y_low], axis=on_y),
         (((on_x,), (on_y,)), ((), ())),
         preferred_element_type=jnp.float32,
     )
+
+
+def product(x, y, on_x, on_y):
+    return term_product(terms_of(x), terms_of(y), on_x, on_y)
 
 
 def column_sum(x):
@@ -620,7 +628,7 @@
     return jnp.concatenate([weight[:width] - weight[width:], weight[width:]], axis=1)
 
 
-def weight_grad(x, leave, reach):
+def weight_grad(x, leave, pair_terms):
     middle = column_sum(x) / x.shape[0]
     level = lax.dot_general(
         jnp.broadcast_to(middle, (8, x.shape[1])) * 0.125,
@@ -629,8 +637,9 @@
         precision=lax.Precision.HIGHEST,
         preferred_element_type=jnp.float32,
     )
-    level = jnp.concatenate([level, jnp.zeros_like(level)], axis=1)
-    return product(x - middle, jnp.concatenate([leave, reach - leave], axis=1), 0, 0) + level
+    both = term_product(terms_of(x - middle), pair_terms, 0, 0)
+    outs = leave.shape[1]
+    return both[:, :outs] + level, both[:, outs:] - both[:, :outs]
 
 
 def total_of(refs):
@@ -653,10 +662,9 @@
     )
     gain_out_ref[...] = gain_all
     width, outs = x_ref.shape[1], leave.shape[1]
-    both = weight_grad(x_ref[...], leave, reach)
-    wgrad[0:width, :] = both[:, :outs]
-    wgrad[width:, :] = both[:, outs:]
-    grad = product(jnp.concatenate([leave, reach], axis=1), turned(weight_ref[...]), 1, 1)
+    pair_terms = terms_of(jnp.concatenate([leave, reach], axis=1))
+    wgrad[0:width, :], wgrad[width:, :] = weight_grad(x_ref[...], leave, pair_terms)
+    grad = term_product(pair_terms, terms_of(turned(weight_ref[...])), 1, 1)
     own = grad * slope_ref[...]
     scaled_ref[...] = grad * inv_ref[...]
     next_ref[...] = own
@@ -708,8 +716,9 @@
         small_ref[0:1, 0:outs], small_ref[1:2, 0:outs],
     )
     gain_out_ref[...] = gain_all
-    wgrad_ref[...] = weight_grad(x_ref[:, 0:width], leave, reach)
-    grad = product(turned(weight_ref[...]), jnp.concatenate([leave, reach], axis=1), 1, 1)
+    pair_terms = terms_of(jnp.concatenate([leave, reach], axis=1))
+    wgrad_ref[:, :outs], wgrad_ref[:, outs:] = weight_grad(x_ref[:, 0:width], leave, pair_terms)
+    grad = term_product(terms_of(turned(weight_ref[...])), pair_terms, 1, 1)
     rows = grad.shape[1] // count
     for m, part in enumerate(parts):
         part[0:width, :] = grad[:, m * rows : (m + 1) * rows]
@@ -791,15 +800,19 @@
         out_parts = to_owner(out_parts)
         output, pool_max, pool_mean = unpack_output(me, out_parts)
 
-    cut = 4 * (3 * slots // 20)
+    def pieces(first, scaled, largest, share, *cuts):
+        def piece(start, stop):
+            return lambda ready: scatter(
+                ids, first, scaled if ready is None else after(scaled, ready), largest, share, start, stop, 4
+            )
+
+        return [piece(*cut) for cut in zip((0, *cuts), (*cuts, slots))]
+
     with jax.named_scope("layer_two_back"):
         sums_two, reached = sum_beside(
             lambda received: pair_sum([part[rows + 2 : rows + 4] for part in received]),
             out_parts,
-            [
-                lambda ready: scatter(ids, slots, scaled_two, largest_two, share_two, 0, cut, 4),
-                lambda ready: scatter(ids, slots, after(scaled_two, ready), largest_two, share_two, cut, slots, 4),
-            ],
+            pieces(slots, scaled_two, largest_two, share_two, slots - 8),
         )
         wgrad_parts, scaled_one, own_one, gain_grad_two = middle(
             edges, slots, count, me, own_two, ysum_two, in_two, deg_two, local_two, stat_two, sums_two,
@@ -809,10 +822,7 @@
         joined, reached = sum_beside(
             lambda received: pair_sum(list(received)),
             to_owner(wgrad_parts),
-            [
-                lambda ready: scatter(ids, 0, scaled_one, scaled_one[:1], share_one, 0, cut, 4),
-                lambda ready: scatter(ids, 0, after(scaled_one, ready), scaled_one[:1], share_one, cut, slots, 4),
-            ],
+            pieces(0, scaled_one, scaled_one[:1], share_one, slots - 12, slots - 4),
         )
         gain_grad_one, wgrad_one, grad_parts = last(
             edges, slots, count, own_one, ysum_one, in_one, deg_one, local_one, stat_one, joined,

time: 182 us -> 180 us (0.989)
  waiting for transfers between devices: 22 us -> 19.2 us
  Pallas kernels: 110 us -> 112 us
    ppermute x44, waiting for transfers between devices: 22 us -> 19.2 us  [exchange(): return lax.ppermute(x, axes, [(i, i ^ mask) for i in range(size)])]
    pallas_call x4 -> x5, Pallas kernels: 38.4 us -> 40.2 us  [scatter(): pl.pallas_call(functools.partial(scatter_kernel, first + start, group, wi...]
  transfers between devices with their start and end apart: 44 -> 44, of which waited for: 15 -> 15; matrix products, arithmetic and copies ran while one was open for 1% -> 1% of each run, Pallas kernels for 44% -> 46%
where the time goes in v3:
time: 180 us
  Pallas kernels  112 us (62%)
  starting transfers between devices  45.4 us (25%)
  waiting for transfers between devices  19.2 us (11%)
    pallas_call x2, Pallas kernels, edge_forward(): pl.pallas_call(functools.partial(edge_kernel, edges, layer, slots, first,...  46.9 us
    ppermute x44, starting transfers between devices, exchange(): return lax.ppermute(x, axes, [(i, i ^ mask) for i in range(size)])  45.4 us
    pallas_call x5, Pallas kernels, scatter(): pl.pallas_call(functools.partial(scatter_kernel, first + start, group, wi...  40.2 us
    ppermute x44, waiting for transfers between devices, exchange(): return lax.ppermute(x, axes, [(i, i ^ mask) for i in range(size)])  19.2 us
    pallas_call x4, Pallas kernels, part_links(): pl.pallas_call(functools.partial(links_kernel, firsts, slots), out_shape=...  7.93 us
    pallas_call x1, Pallas kernels, first_tables(): pl.pallas_call(functools.partial(first_kernel, slots, width, count), out_...  4.37 us
  transfers between devices with their start and end apart: 44, of which 15 were waited for; matrix products, arithmetic and copies ran while one was open for 1% of the time, Pallas kernels for 46%

profile of v3, /device:TPU:0, one launch (start us, length us, event | category | flops | bytes accessed | tf_op | source)
XLA Modules:
  0.0 179.6 jit_solution(15813352150914185210)
XLA Ops:
  0.7 1.4 pack.1
  2.6 2.6 %collective-permute-start.1 = (f32[104,256]{1,0:T(8,128)S(1)}, f32[104,256]{1,0:T(8,128)S(1)}, u32[]{:S(2)}, u32[]{:S(2)}) collective-permute-start(f32[104,256]{1,0:T(8,128)S(1)} %get-tuple-element.102), channel_id=1, source_target_pairs={{0,2},{1,3},{2,0},{3,1},{4,6},{5,7},{6,4},{7,5},{8,10},{9,11},{10,... | collective-permute-start | bytes 319496 | tf_op jit(solution)/shard_map/bring_clouds/ppermute | solution.py:39
  5.2 2.6 %part_links.4 = (bf16[1024,256]{1,0:T(8,128)(2,1)S(1)}, bf16[1024,256]{1,0:T(8,128)(2,1)S(1)}) custom-call(f32[104,256]{1,0:T(8,128)S(1)} %get-tuple-element.100.ids_ref.refs_0_), custom_call_target="tpu_custom_call" | custom-call | flops 1048576000 | bytes 524288 | tf_op jit(solution)/shard_map/bring_clouds/part_links/pallas_call | solution.py:287
  7.9 2.6 %part_links.5 = (bf16[1024,256]{1,0:T(8,128)(2,1)S(1)}, bf16[1024,256]{1,0:T(8,128)(2,1)S(1)}) custom-call(f32[104,256]{1,0:T(8,128)S(1)} %collective-permute-done.ids_ref.refs_1_), custom_call_target="tpu_custom_call" | custom-call | flops 1048576000 | bytes 524288 | tf_op jit(solution)/shard_map/bring_clouds/part_links/pallas_call | solution.py:287
  10.8 4.4 %first_tables.1 = (f32[1024,128]{1,0:T(8,128)S(1)}, f32[40,1024]{1,0:T(8,128)S(1)}, f32[1024,128]{1,0:T(8,128)S(1)}, f32[1024,128]{1,0:T(8,128)S(1)}, f32[1024,1...) custom-call(f32[104,256]{1,0:T(8,128)S(1)} %get-tuple-element.100.ids_ref.refs_0_, ...), custom_call_target="tpu_custom_call" | custom-call | tf_op jit(solution)/shard_map/layer_one/first_tables/pallas_call | solution.py:353
  15.1 1.6 collective-permute-start.5
  17.1 1.1 collective-permute-done.5
  18.2 2.1 %collective-permute-done.4 = f32[2,128]{1,0:T(2,128)S(1)} collective-permute-done((f32[2,128]{1,0:T(2,128)S(1)}, f32[2,128]{1,0:T(2,128)S(1)}, u32[]{:S(2)}, u32[]{:S(2)}) %collective-permute-start.4) | collective-permute-done | bytes 1056 | tf_op jit(solution)/shard_map/layer_one/ppermute | solution.py:39
  20.3 1.6 collective-permute-start.6
  21.9 1.3 part_links.7.refs_3_
  23.2 0.7 collective-permute-done.6
  24.0 3.7 %collective-permute-start.9 = (f32[2,128]{1,0:T(2,128)S(1)}, f32[2,128]{1,0:T(2,128)S(1)}, u32[]{:S(2)}, u32[]{:S(2)}) collective-permute-start(f32[2,128]{1,0:T(2,128)S(1)} %pad_maximum_fusion.5), channel_id=1, source_target_pairs={{0,24},{4,28},{8,16},{12,20},{16,8},{20,12},{24,0},{28,4},{1,25},{... | collective-permute-start | bytes 3080 | tf_op jit(solution)/shard_map/layer_one/ppermute | solution.py:39
  27.6 0.8 collective-permute-start.7
  28.4 1.3 part_links.6.refs_2_
  29.7 2.3 %collective-permute-done.8 = f32[2,128]{1,0:T(2,128)S(1)} collective-permute-done((f32[2,128]{1,0:T(2,128)S(1)}, f32[2,128]{1,0:T(2,128)S(1)}, u32[]{:S(2)}, u32[]{:S(2)}) %collective-permute-start.8) | collective-permute-done | bytes 1056 | tf_op jit(solution)/shard_map/layer_one/ppermute | solution.py:39
  32.1 16.4 %edges.2 = (f32[1024,128]{1,0:T(8,128)S(1)}, f32[20,1024,128]{2,1,0:T(8,128)}, f32[1024,128]{1,0:T(8,128)S(1)}, f32[1024,128]{1,0:T(8,128)S(1)}, f32[1024,128]{1,0:T(8,128)S(1)}, /*index=5*/f32[1024,128]{1,0:T(8,128)S(1)}) custom-call(f32[1024,128]{1,0:T(8,128)S(1)} %get-tuple-element.107.x_ref, f32[1024,128]{1,0:T(8,128)S(1)} %get-tuple-element.108.a_ref, ...), custom_call_target="tpu_custom_call" | custom-call | tf_op jit(solution)/shard_map/layer_one/edges/pallas_call | solution.py:486
  48.5 2.7 %second_tables.1 = (f32[1024,256]{1,0:T(8,128)S(1)}, f32[1024,256]{1,0:T(8,128)S(1)}, f32[1024,256]{1,0:T(8,128)S(1)}, f32[1024,128]{1,0:T(8,128)S(1)}, f32[2,256]{1,0:T(2,128)S(1)}) custom-call(f32[1024,128]{1,0:T(8,128)S(1)} %get-tuple-element.112.x_ref, f32[256,256]{1,0:T(8,128)S(1)} %get-tuple-element.113.weight_ref, ...), custom_call_target="tpu_custom_call" | custom-call | tf_op jit(solution)/shard_map/layer_two/second_tables/pallas_call | solution.py:378
  51.3 0.6 collective-permute-start.11
  51.9 1.3 collective-permute-start.10
  53.1 1.1 collective-permute-done.12
  54.3 0.7 collective-permute-done.11
  55.0 1.6 collective-permute-start.13
  56.5 2.1 %collective-permute-done.13 = f32[2,256]{1,0:T(2,128)S(1)} collective-permute-done((f32[2,256]{1,0:T(2,128)S(1)}, f32[2,256]{1,0:T(2,128)S(1)}, u32[]{:S(2)}, u32[]{:S(2)}) %collective-permute-start.13) | collective-permute-done | bytes 2080 | tf_op jit(solution)/shard_map/layer_two/ppermute | solution.py:39
  58.6 1.5 collective-permute-start.16
  60.2 0.6 collective-permute-start.15
  60.8 2.3 %collective-permute-start.14 = (f32[2,256]{1,0:T(2,128)S(1)}, f32[2,256]{1,0:T(2,128)S(1)}, u32[]{:S(2)}, u32[]{:S(2)}) collective-permute-start(f32[2,256]{1,0:T(2,128)S(1)} %pad_maximum_fusion.2), channel_id=1, source_target_pairs={{0,8},{4,12},{8,0},{12,4},{16,24},{20,28},{24,16},{28,20},{1,9},{5... | collective-permute-start | bytes 6152 | tf_op jit(solution)/shard_map/layer_two/ppermute | solution.py:39
  63.1 1.3 split.13
  64.5 0.6 collective-permute-start.18
  65.1 1.2 collective-permute-start.19
  66.4 30.5 %edges.3 = (f32[1024,256]{1,0:T(8,128)S(1)}, f32[20,1024,256]{2,1,0:T(8,128)}, f32[1024,256]{1,0:T(8,128)S(1)}, f32[1024,256]{1,0:T(8,128)S(1)}, f32[1024,256]{1,0:T(8,128)S(1)}, /*index=5*/f32[1024,256]{1,0:T(8,128)S(1)}) custom-call(f32[1024,128]{1,0:T(8,128)S(1)} %get-tuple-element.107.x_ref, f32[1024,256]{1,0:T(8,128)S(1)} %get-tuple-element.116.a_ref, ...), custom_call_target="tpu_custom_call" | custom-call | tf_op jit(solution)/shard_map/layer_two/edges/pallas_call | solution.py:486
  96.9 0.9 pools.1
  98.2 0.6 collective-permute-start.21
  98.7 1.0 collective-permute-start.22
  99.7 13.5 %scatter.5.refs_0_ = f32[1024,256]{1,0:T(8,128)S(1)} custom-call(f32[40,1024]{1,0:T(8,128)S(1)} %get-tuple-element.138.ids_ref, f32[1024,256]{1,0:T(8,128)S(1)} %get-tuple-element.146.grad_ref, f32[1,256]{1,0:T(1,128)S(1)} %get-tuple-element.140.largest_ref, f32[20,1024,256]{2,1,0:T(8,128)} %get-tuple-element.141.weight_ref), custom_call_target="tpu_custom_call" | custom-call | flops 12884901888 | bytes 12582912 | tf_op jit(solution)/shard_map/layer_two_back/scatter/pallas_call | solution.py:593
  113.2 1.5 collective-permute-start.25
  115.1 2.6 %collective-permute-start.23 = (f32[2,256]{1,0:T(2,128)S(1)}, f32[2,256]{1,0:T(2,128)S(1)}, u32[]{:S(2)}, u32[]{:S(2)}) collective-permute-start(f32[2,256]{1,0:T(2,128)S(1)} %add_add_fusion.5), channel_id=1, source_target_pairs={{0,8},{4,12},{8,0},{12,4},{16,24},{20,28},{24,16},{28,20},{1,9},{5... | collective-permute-start | bytes 6152 | tf_op jit(solution)/shard_map/layer_two_back/ppermute | solution.py:39
  117.7 9.7 %scatter.6.refs_1_ = f32[1024,256]{1,0:T(8,128)S(1)} custom-call(f32[40,1024]{1,0:T(8,128)S(1)} %get-tuple-element.138.ids_ref, f32[1024,256]{1,0:T(8,128)S(1)} %get-tuple-element.146.grad_ref, f32[1,256]{1,0:T(1,128)S(1)} %get-tuple-element.140.largest_ref, f32[20,1024,256]{2,1,0:T(8,128)} %get-tuple-element.141.weight_ref), custom_call_target="tpu_custom_call" | custom-call | flops 8589934592 | bytes 8388608 | tf_op jit(solution)/shard_map/layer_two_back/scatter/pallas_call | solution.py:593
  127.4 1.6 collective-permute-start.26
  129.0 2.1 %collective-permute-done.26 = f32[2,256]{1,0:T(2,128)S(1)} collective-permute-done((f32[2,256]{1,0:T(2,128)S(1)}, f32[2,256]{1,0:T(2,128)S(1)}, u32[]{:S(2)}, u32[]{:S(2)}) %collective-permute-start.26) | collective-permute-done | bytes 2080 | tf_op jit(solution)/shard_map/layer_two_back/ppermute | solution.py:39
  131.1 3.1 %middle.1 = (f32[72,256]{1,0:T(8,128)S(1)}, f32[72,256]{1,0:T(8,128)S(1)}, f32[72,256]{1,0:T(8,128)S(1)}, f32[72,256]{1,0:T(8,128)S(1)}, f32[1024,128]{1,0:T(8,1...) custom-call(s32[1]{0:T(128)} %bitcast.me_ref, f32[1024,256]{1,0:T(8,128)S(1)} %get-tuple-element.134.own_ref, ...), custom_call_target="tpu_custom_call" | custom-call | tf_op jit(solution)/shard_map/layer_two_back/middle/pallas_call | solution.py:690
  134.2 0.5 collective-permute-start.28
  134.7 1.3 collective-permute-start.29
  136.0 6.4 %scatter.7.refs_0_ = f32[1024,128]{1,0:T(8,128)S(1)} custom-call(f32[40,1024]{1,0:T(8,128)S(1)} %get-tuple-element.138.ids_ref, f32[1024,128]{1,0:T(8,128)S(1)} %get-tuple-element.173.grad_ref, f32[1,128]{1,0:T(1,128)S(1)} %slice.169.largest_ref, f32[20,1024,128]{2,1,0:T(8,128)} %get-tuple-element.163.weight_ref), custom_call_target="tpu_custom_call" | custom-call | flops 4294967296 | bytes 4194304 | tf_op jit(solution)/shard_map/layer_one_back/scatter/pallas_call | solution.py:593
  142.5 1.5 collective-permute-start.32
  144.0 2.9 %collective-permute-start.30 = (f32[72,256]{1,0:T(8,128)S(1)}, f32[72,256]{1,0:T(8,128)S(1)}, u32[]{:S(2)}, u32[]{:S(2)}) collective-permute-start(f32[72,256]{1,0:T(8,128)S(1)} %add_add_fusion.1), channel_id=1, source_target_pairs={{0,8},{4,12},{8,0},{12,4},{16,24},{20,28},{24,16},{28,20},{1,9},{5... | collective-permute-start | bytes 221192 | tf_op jit(solution)/shard_map/layer_one_back/ppermute | solution.py:39
  147.0 6.7 %scatter.8.refs_1_ = f32[1024,128]{1,0:T(8,128)S(1)} custom-call(f32[40,1024]{1,0:T(8,128)S(1)} %get-tuple-element.138.ids_ref, f32[1024,128]{1,0:T(8,128)S(1)} %get-tuple-element.173.grad_ref, f32[1,128]{1,0:T(1,128)S(1)} %slice.169.largest_ref, f32[20,1024,128]{2,1,0:T(8,128)} %get-tuple-element.163.weight_ref), custom_call_target="tpu_custom_call" | custom-call | flops 4294967296 | bytes 4194304 | tf_op jit(solution)/shard_map/layer_one_back/scatter/pallas_call | solution.py:593
  153.7 1.6 collective-permute-start.33
  155.3 3.9 %scatter.9.refs_2_ = f32[1024,128]{1,0:T(8,128)S(1)} custom-call(f32[40,1024]{1,0:T(8,128)S(1)} %get-tuple-element.138.ids_ref, f32[1024,128]{1,0:T(8,128)S(1)} %get-tuple-element.173.grad_ref, f32[1,128]{1,0:T(1,128)S(1)} %slice.169.largest_ref, f32[20,1024,128]{2,1,0:T(8,128)} %get-tuple-element.163.weight_ref), custom_call_target="tpu_custom_call" | custom-call | flops 2147483648 | bytes 2097152 | tf_op jit(solution)/shard_map/layer_one_back/scatter/pallas_call | solution.py:593
  159.3 1.4 last.1
  160.8 0.8 collective-permute-start.35
  161.6 1.1 collective-permute-start.34
  162.6 2.0 %collective-permute-done.36 = f32[64,256]{1,0:T(8,128)S(1)} collective-permute-done((f32[64,256]{1,0:T(8,128)S(1)}, f32[64,256]{1,0:T(8,128)S(1)}, u32[]{:S(2)}, u32[]{:S(2)}) %collective-permute-start.36) | collective-permute-done | bytes 65568 | tf_op jit(solution)/shard_map/layer_one_back/ppermute | solution.py:39
  164.6 1.1 collective-permute-done.35
  166.0 0.5 collective-permute-start.40
  166.5 1.0 unpack_output.1
  167.6 0.6 slice.187
  168.1 1.3 collective-permute-start.38
  169.6 0.8 collective-permute-done.40
  170.4 1.5 collective-permute-start.43
  172.0 2.8 %collective-permute-start.41 = (f32[64,256]{1,0:T(8,128)S(1)}, f32[64,256]{1,0:T(8,128)S(1)}, u32[]{:S(2)}, u32[]{:S(2)}) collective-permute-start(f32[64,256]{1,0:T(8,128)S(1)} %add.272), channel_id=1, source_target_pairs={{0,8},{4,12},{8,0},{12,4},{16,24},{20,28},{24,16},{28,20},{1,9},{5... | collective-permute-start | bytes 196616 | tf_op jit(solution)/shard_map/layer_one_back/ppermute | solution.py:39
  175.5 0.8 unpack_grad.1
  176.4 0.9 collective-permute-done.43
  177.3 1.7 collective-permute-done.42
  179.0 0.6 pad_maximum_fusion
  (74 shorter events, 3.7 us)
Async XLA Ops:
  0.6 96.2 %copy-start.1 = (f32[4,256]{1,0:T(4,128)S(1)}, f32[4,256]{1,0:T(4,128)}, u32[]{:S(2)}) copy-start(f32[4,256]{1,0:T(4,128)} %gmean_ref.1) | copy-start | bytes 12292
  0.7 96.2 %copy-start = (f32[4,256]{1,0:T(4,128)S(1)}, f32[4,256]{1,0:T(4,128)}, u32[]{:S(2)}) copy-start(f32[4,256]{1,0:T(4,128)} %gmax_ref.1) | copy-start | bytes 12292
  2.1 5.8 %collective-permute-start = (f32[104,256]{1,0:T(8,128)S(1)}, f32[104,256]{1,0:T(8,128)S(1)}, u32[]{:S(2)}, u32[]{:S(2)}) collective-permute-start(f32[104,256]{1,0:T(8,128)S(1)} %get-tuple-element.101), channel_id=1, source_target_pairs={{0,1},{1,0},{2,3},{3,2},{4,5},{5,4},{6,7},{7,6},{8,9},{9,8},{10,11... | collective-permute-start | bytes 319496 | tf_op jit(solution)/shard_map/bring_clouds/ppermute | solution.py:39
  2.6 8.0 %collective-permute-start.1 = (f32[104,256]{1,0:T(8,128)S(1)}, f32[104,256]{1,0:T(8,128)S(1)}, u32[]{:S(2)}, u32[]{:S(2)}) collective-permute-start(f32[104,256]{1,0:T(8,128)S(1)} %get-tuple-element.102), channel_id=1, source_target_pairs={{0,2},{1,3},{2,0},{3,1},{4,6},{5,7},{6,4},{7,5},{8,10},{9,11},{10,... | collective-permute-start | bytes 319496 | tf_op jit(solution)/shard_map/bring_clouds/ppermute | solution.py:39
  5.2 5.6 %collective-permute-start.2 = (f32[104,256]{1,0:T(8,128)S(1)}, f32[104,256]{1,0:T(8,128)S(1)}, u32[]{:S(2)}, u32[]{:S(2)}) collective-permute-start(f32[104,256]{1,0:T(8,128)S(1)} %get-tuple-element.103), channel_id=1, source_target_pairs={{0,3},{1,2},{2,1},{3,0},{4,7},{5,6},{6,5},{7,4},{8,11},{9,10},{10,... | collective-permute-start | bytes 319496 | tf_op jit(solution)/shard_map/bring_clouds/ppermute | solution.py:39
  15.1 3.1 %collective-permute-start.5 = (f32[2,128]{1,0:T(2,128)S(1)}, f32[2,128]{1,0:T(2,128)S(1)}, u32[]{:S(2)}, u32[]{:S(2)}) collective-permute-start(f32[2,128]{1,0:T(2,128)S(1)} %get-tuple-element.110.local_ref), channel_id=1, source_target_pairs={{0,3},{1,2},{2,1},{3,0},{4,7},{5,6},{6,5},{7,4},{8,11},{9,10},{10,... | collective-permute-start | bytes 3080 | tf_op jit(solution)/shard_map/layer_one/ppermute | solution.py:39
  16.7 3.6 %collective-permute-start.4 = (f32[2,128]{1,0:T(2,128)S(1)}, f32[2,128]{1,0:T(2,128)S(1)}, u32[]{:S(2)}, u32[]{:S(2)}) collective-permute-start(f32[2,128]{1,0:T(2,128)S(1)} %get-tuple-element.110.local_ref), channel_id=1, source_target_pairs={{0,2},{1,3},{2,0},{3,1},{4,6},{5,7},{6,4},{7,5},{8,10},{9,11},{10,... | collective-permute-start | bytes 3080 | tf_op jit(solution)/shard_map/layer_one/ppermute | solution.py:39
  16.9 3.3 %collective-permute-start.3 = (f32[2,128]{1,0:T(2,128)S(1)}, f32[2,128]{1,0:T(2,128)S(1)}, u32[]{:S(2)}, u32[]{:S(2)}) collective-permute-start(f32[2,128]{1,0:T(2,128)S(1)} %get-tuple-element.110.local_ref), channel_id=1, source_target_pairs={{0,1},{1,0},{2,3},{3,2},{4,5},{5,4},{6,7},{7,6},{8,9},{9,8},{10,11... | collective-permute-start | bytes 3080 | tf_op jit(solution)/shard_map/layer_one/ppermute | solution.py:39
  20.3 3.6 %collective-permute-start.6 = (f32[2,128]{1,0:T(2,128)S(1)}, f32[2,128]{1,0:T(2,128)S(1)}, u32[]{:S(2)}, u32[]{:S(2)}) collective-permute-start(f32[2,128]{1,0:T(2,128)S(1)} %pad_maximum_fusion.4), channel_id=1, source_target_pairs={{0,4},{4,0},{8,12},{12,8},{16,20},{20,16},{24,28},{28,24},{1,5},{5... | collective-permute-start | bytes 3080 | tf_op jit(solution)/shard_map/layer_one/ppermute | solution.py:39
  24.0 5.8 %collective-permute-start.9 = (f32[2,128]{1,0:T(2,128)S(1)}, f32[2,128]{1,0:T(2,128)S(1)}, u32[]{:S(2)}, u32[]{:S(2)}) collective-permute-start(f32[2,128]{1,0:T(2,128)S(1)} %pad_maximum_fusion.5), channel_id=1, source_target_pairs={{0,24},{4,28},{8,16},{12,20},{16,8},{20,12},{24,0},{28,4},{1,25},{... | collective-permute-start | bytes 3080 | tf_op jit(solution)/shard_map/layer_one/ppermute | solution.py:39
  27.6 4.5 %collective-permute-start.8 = (f32[2,128]{1,0:T(2,128)S(1)}, f32[2,128]{1,0:T(2,128)S(1)}, u32[]{:S(2)}, u32[]{:S(2)}) collective-permute-start(f32[2,128]{1,0:T(2,128)S(1)} %pad_maximum_fusion.5), channel_id=1, source_target_pairs={{0,16},{4,20},{8,24},{12,28},{16,0},{20,4},{24,8},{28,12},{1,17},{... | collective-permute-start | bytes 3080 | tf_op jit(solution)/shard_map/layer_one/ppermute | solution.py:39
  27.6 4.5 %collective-permute-start.7 = (f32[2,128]{1,0:T(2,128)S(1)}, f32[2,128]{1,0:T(2,128)S(1)}, u32[]{:S(2)}, u32[]{:S(2)}) collective-permute-start(f32[2,128]{1,0:T(2,128)S(1)} %pad_maximum_fusion.5), channel_id=1, source_target_pairs={{0,8},{4,12},{8,0},{12,4},{16,24},{20,28},{24,16},{28,20},{1,9},{5... | collective-permute-start | bytes 3080 | tf_op jit(solution)/shard_map/layer_one/ppermute | solution.py:39
  51.2 3.1 %collective-permute-start.12 = (f32[2,256]{1,0:T(2,128)S(1)}, f32[2,256]{1,0:T(2,128)S(1)}, u32[]{:S(2)}, u32[]{:S(2)}) collective-permute-start(f32[2,256]{1,0:T(2,128)S(1)} %get-tuple-element.118.local_ref), channel_id=1, source_target_pairs={{0,3},{1,2},{2,1},{3,0},{4,7},{5,6},{6,5},{7,4},{8,11},{9,10},{10,... | collective-permute-start | bytes 6152 | tf_op jit(solution)/shard_map/layer_two/ppermute | solution.py:39
  51.3 3.7 %collective-permute-start.11 = (f32[2,256]{1,0:T(2,128)S(1)}, f32[2,256]{1,0:T(2,128)S(1)}, u32[]{:S(2)}, u32[]{:S(2)}) collective-permute-start(f32[2,256]{1,0:T(2,128)S(1)} %get-tuple-element.118.local_ref), channel_id=1, source_target_pairs={{0,2},{1,3},{2,0},{3,1},{4,6},{5,7},{6,4},{7,5},{8,10},{9,11},{10,... | collective-permute-start | bytes 6152 | tf_op jit(solution)/shard_map/layer_two/ppermute | solution.py:39
  51.9 3.1 %collective-permute-start.10 = (f32[2,256]{1,0:T(2,128)S(1)}, f32[2,256]{1,0:T(2,128)S(1)}, u32[]{:S(2)}, u32[]{:S(2)}) collective-permute-start(f32[2,256]{1,0:T(2,128)S(1)} %get-tuple-element.118.local_ref), channel_id=1, source_target_pairs={{0,1},{1,0},{2,3},{3,2},{4,5},{5,4},{6,7},{7,6},{8,9},{9,8},{10,11... | collective-permute-start | bytes 6152 | tf_op jit(solution)/shard_map/layer_two/ppermute | solution.py:39
  55.0 3.7 %collective-permute-start.13 = (f32[2,256]{1,0:T(2,128)S(1)}, f32[2,256]{1,0:T(2,128)S(1)}, u32[]{:S(2)}, u32[]{:S(2)}) collective-permute-start(f32[2,256]{1,0:T(2,128)S(1)} %pad_maximum_fusion.1), channel_id=1, source_target_pairs={{0,4},{4,0},{8,12},{12,8},{16,20},{20,16},{24,28},{28,24},{1,5},{5... | collective-permute-start | bytes 6152 | tf_op jit(solution)/shard_map/layer_two/ppermute | solution.py:39
  58.6 6.4 %collective-permute-start.16 = (f32[2,256]{1,0:T(2,128)S(1)}, f32[2,256]{1,0:T(2,128)S(1)}, u32[]{:S(2)}, u32[]{:S(2)}) collective-permute-start(f32[2,256]{1,0:T(2,128)S(1)} %pad_maximum_fusion.2), channel_id=1, source_target_pairs={{0,24},{4,28},{8,16},{12,20},{16,8},{20,12},{24,0},{28,4},{1,25},{... | collective-permute-start | bytes 6152 | tf_op jit(solution)/shard_map/layer_two/ppermute | solution.py:39
  60.2 6.2 %collective-permute-start.15 = (f32[2,256]{1,0:T(2,128)S(1)}, f32[2,256]{1,0:T(2,128)S(1)}, u32[]{:S(2)}, u32[]{:S(2)}) collective-permute-start(f32[2,256]{1,0:T(2,128)S(1)} %pad_maximum_fusion.2), channel_id=1, source_target_pairs={{0,16},{4,20},{8,24},{12,28},{16,0},{20,4},{24,8},{28,12},{1,17},{... | collective-permute-start | bytes 6152 | tf_op jit(solution)/shard_map/layer_two/ppermute | solution.py:39
  60.8 5.5 %collective-permute-start.14 = (f32[2,256]{1,0:T(2,128)S(1)}, f32[2,256]{1,0:T(2,128)S(1)}, u32[]{:S(2)}, u32[]{:S(2)}) collective-permute-start(f32[2,256]{1,0:T(2,128)S(1)} %pad_maximum_fusion.2), channel_id=1, source_target_pairs={{0,8},{4,12},{8,0},{12,4},{16,24},{20,28},{24,16},{28,20},{1,9},{5... | collective-permute-start | bytes 6152 | tf_op jit(solution)/shard_map/layer_two/ppermute | solution.py:39
  64.4 32.5 %collective-permute-start.17 = (f32[256,256]{1,0:T(8,128)S(1)}, f32[256,256]{1,0:T(8,128)S(1)}, u32[]{:S(2)}, u32[]{:S(2)}) collective-permute-start(f32[256,256]{1,0:T(8,128)S(1)} %get-tuple-element.124), channel_id=1, source_target_pairs={{0,1},{1,0},{2,3},{3,2},{4,5},{5,4},{6,7},{7,6},{8,9},{9,8},{10,11... | collective-permute-start | bytes 786440 | tf_op jit(solution)/shard_map/bring_cotangents/ppermute | solution.py:39
  64.5 32.4 %collective-permute-start.18 = (f32[256,256]{1,0:T(8,128)S(1)}, f32[256,256]{1,0:T(8,128)S(1)}, u32[]{:S(2)}, u32[]{:S(2)}) collective-permute-start(f32[256,256]{1,0:T(8,128)S(1)} %get-tuple-element.125), channel_id=1, source_target_pairs={{0,2},{1,3},{2,0},{3,1},{4,6},{5,7},{6,4},{7,5},{8,10},{9,11},{10,... | collective-permute-start | bytes 786440 | tf_op jit(solution)/shard_map/bring_cotangents/ppermute | solution.py:39
  65.1 31.8 %collective-permute-start.19 = (f32[256,256]{1,0:T(8,128)S(1)}, f32[256,256]{1,0:T(8,128)S(1)}, u32[]{:S(2)}, u32[]{:S(2)}) collective-permute-start(f32[256,256]{1,0:T(8,128)S(1)} %get-tuple-element.126), channel_id=1, source_target_pairs={{0,3},{1,2},{2,1},{3,0},{4,7},{5,6},{6,5},{7,4},{8,11},{9,10},{10,... | collective-permute-start | bytes 786440 | tf_op jit(solution)/shard_map/bring_cotangents/ppermute | solution.py:39
  97.8 15.4 %collective-permute-start.20 = (f32[264,256]{1,0:T(8,128)S(1)}, f32[264,256]{1,0:T(8,128)S(1)}, u32[]{:S(2)}, u32[]{:S(2)}) collective-permute-start(f32[264,256]{1,0:T(8,128)S(1)} %get-tuple-element.128), channel_id=1, source_target_pairs={{0,1},{1,0},{2,3},{3,2},{4,5},{5,4},{6,7},{7,6},{8,9},{9,8},{10,11... | collective-permute-start | bytes 811016 | tf_op jit(solution)/shard_map/pools/ppermute | solution.py:39
  98.2 15.0 %collective-permute-start.21 = (f32[264,256]{1,0:T(8,128)S(1)}, f32[264,256]{1,0:T(8,128)S(1)}, u32[]{:S(2)}, u32[]{:S(2)}) collective-permute-start(f32[264,256]{1,0:T(8,128)S(1)} %get-tuple-element.129), channel_id=1, source_target_pairs={{0,2},{1,3},{2,0},{3,1},{4,6},{5,7},{6,4},{7,5},{8,10},{9,11},{10,... | collective-permute-start | bytes 811016 | tf_op jit(solution)/shard_map/pools/ppermute | solution.py:39
  98.7 14.5 %collective-permute-start.22 = (f32[264,256]{1,0:T(8,128)S(1)}, f32[264,256]{1,0:T(8,128)S(1)}, u32[]{:S(2)}, u32[]{:S(2)}) collective-permute-start(f32[264,256]{1,0:T(8,128)S(1)} %get-tuple-element.130), channel_id=1, source_target_pairs={{0,3},{1,2},{2,1},{3,0},{4,7},{5,6},{6,5},{7,4},{8,11},{9,10},{10,... | collective-permute-start | bytes 811016 | tf_op jit(solution)/shard_map/pools/ppermute | solution.py:39
  113.2 14.2 %collective-permute-start.25 = (f32[2,256]{1,0:T(2,128)S(1)}, f32[2,256]{1,0:T(2,128)S(1)}, u32[]{:S(2)}, u32[]{:S(2)}) collective-permute-start(f32[2,256]{1,0:T(2,128)S(1)} %add_add_fusion.5), channel_id=1, source_target_pairs={{0,24},{4,28},{8,16},{12,20},{16,8},{20,12},{24,0},{28,4},{1,25},{... | collective-permute-start | bytes 6152 | tf_op jit(solution)/shard_map/layer_two_back/ppermute | solution.py:39
  114.8 12.6 %collective-permute-start.24 = (f32[2,256]{1,0:T(2,128)S(1)}, f32[2,256]{1,0:T(2,128)S(1)}, u32[]{:S(2)}, u32[]{:S(2)}) collective-permute-start(f32[2,256]{1,0:T(2,128)S(1)} %add_add_fusion.5), channel_id=1, source_target_pairs={{0,16},{4,20},{8,24},{12,28},{16,0},{20,4},{24,8},{28,12},{1,17},{... | collective-permute-start | bytes 6152 | tf_op jit(solution)/shard_map/layer_two_back/ppermute | solution.py:39
  115.1 12.3 %collective-permute-start.23 = (f32[2,256]{1,0:T(2,128)S(1)}, f32[2,256]{1,0:T(2,128)S(1)}, u32[]{:S(2)}, u32[]{:S(2)}) collective-permute-start(f32[2,256]{1,0:T(2,128)S(1)} %add_add_fusion.5), channel_id=1, source_target_pairs={{0,8},{4,12},{8,0},{12,4},{16,24},{20,28},{24,16},{28,20},{1,9},{5... | collective-permute-start | bytes 6152 | tf_op jit(solution)/shard_map/layer_two_back/ppermute | solution.py:39
  127.4 3.7 %collective-permute-start.26 = (f32[2,256]{1,0:T(2,128)S(1)}, f32[2,256]{1,0:T(2,128)S(1)}, u32[]{:S(2)}, u32[]{:S(2)}) collective-permute-start(f32[2,256]{1,0:T(2,128)S(1)} %add_add_fusion.4), channel_id=1, source_target_pairs={{0,4},{4,0},{8,12},{12,8},{16,20},{20,16},{24,28},{28,24},{1,5},{5... | collective-permute-start | bytes 6152 | tf_op jit(solution)/shard_map/layer_two_back/ppermute | solution.py:39
  134.2 8.3 %collective-permute-start.27 = (f32[72,256]{1,0:T(8,128)S(1)}, f32[72,256]{1,0:T(8,128)S(1)}, u32[]{:S(2)}, u32[]{:S(2)}) collective-permute-start(f32[72,256]{1,0:T(8,128)S(1)} %get-tuple-element.159), channel_id=1, source_target_pairs={{0,1},{1,0},{2,3},{3,2},{4,5},{5,4},{6,7},{7,6},{8,9},{9,8},{10,11... | collective-permute-start | bytes 221192 | tf_op jit(solution)/shard_map/layer_one_back/ppermute | solution.py:39
  134.2 8.3 %collective-permute-start.28 = (f32[72,256]{1,0:T(8,128)S(1)}, f32[72,256]{1,0:T(8,128)S(1)}, u32[]{:S(2)}, u32[]{:S(2)}) collective-permute-start(f32[72,256]{1,0:T(8,128)S(1)} %get-tuple-element.160), channel_id=1, source_target_pairs={{0,2},{1,3},{2,0},{3,1},{4,6},{5,7},{6,4},{7,5},{8,10},{9,11},{10,... | collective-permute-start | bytes 221192 | tf_op jit(solution)/shard_map/layer_one_back/ppermute | solution.py:39
  134.7 7.8 %collective-permute-start.29 = (f32[72,256]{1,0:T(8,128)S(1)}, f32[72,256]{1,0:T(8,128)S(1)}, u32[]{:S(2)}, u32[]{:S(2)}) collective-permute-start(f32[72,256]{1,0:T(8,128)S(1)} %get-tuple-element.161), channel_id=1, source_target_pairs={{0,3},{1,2},{2,1},{3,0},{4,7},{5,6},{6,5},{7,4},{8,11},{9,10},{10,... | collective-permute-start | bytes 221192 | tf_op jit(solution)/shard_map/layer_one_back/ppermute | solution.py:39
  142.5 11.1 %collective-permute-start.32 = (f32[72,256]{1,0:T(8,128)S(1)}, f32[72,256]{1,0:T(8,128)S(1)}, u32[]{:S(2)}, u32[]{:S(2)}) collective-permute-start(f32[72,256]{1,0:T(8,128)S(1)} %add_add_fusion.1), channel_id=1, source_target_pairs={{0,24},{4,28},{8,16},{12,20},{16,8},{20,12},{24,0},{28,4},{1,25},{... | collective-permute-start | bytes 221192 | tf_op jit(solution)/shard_map/layer_one_back/ppermute | solution.py:39
  144.0 9.6 %collective-permute-start.31 = (f32[72,256]{1,0:T(8,128)S(1)}, f32[72,256]{1,0:T(8,128)S(1)}, u32[]{:S(2)}, u32[]{:S(2)}) collective-permute-start(f32[72,256]{1,0:T(8,128)S(1)} %add_add_fusion.1), channel_id=1, source_target_pairs={{0,16},{4,20},{8,24},{12,28},{16,0},{20,4},{24,8},{28,12},{1,17},{... | collective-permute-start | bytes 221192 | tf_op jit(solution)/shard_map/layer_one_back/ppermute | solution.py:39
  144.0 9.6 %collective-permute-start.30 = (f32[72,256]{1,0:T(8,128)S(1)}, f32[72,256]{1,0:T(8,128)S(1)}, u32[]{:S(2)}, u32[]{:S(2)}) collective-permute-start(f32[72,256]{1,0:T(8,128)S(1)} %add_add_fusion.1), channel_id=1, source_target_pairs={{0,8},{4,12},{8,0},{12,4},{16,24},{20,28},{24,16},{28,20},{1,9},{5... | collective-permute-start | bytes 221192 | tf_op jit(solution)/shard_map/layer_one_back/ppermute | solution.py:39
  153.7 5.5 %collective-permute-start.33 = (f32[72,256]{1,0:T(8,128)S(1)}, f32[72,256]{1,0:T(8,128)S(1)}, u32[]{:S(2)}, u32[]{:S(2)}) collective-permute-start(f32[72,256]{1,0:T(8,128)S(1)} %add_add_fusion), channel_id=1, source_target_pairs={{0,4},{4,0},{8,12},{12,8},{16,20},{20,16},{24,28},{28,24},{1,5},{5... | collective-permute-start | bytes 221192 | tf_op jit(solution)/shard_map/layer_one_back/ppermute | solution.py:39
  160.7 3.9 %collective-permute-start.36 = (f32[64,256]{1,0:T(8,128)S(1)}, f32[64,256]{1,0:T(8,128)S(1)}, u32[]{:S(2)}, u32[]{:S(2)}) collective-permute-start(f32[64,256]{1,0:T(8,128)S(1)} %get-tuple-element.176), channel_id=1, source_target_pairs={{0,3},{1,2},{2,1},{3,0},{4,7},{5,6},{6,5},{7,4},{8,11},{9,10},{10,... | collective-permute-start | bytes 196616 | tf_op jit(solution)/shard_map/layer_one_back/ppermute | solution.py:39
  160.8 5.0 %collective-permute-start.35 = (f32[64,256]{1,0:T(8,128)S(1)}, f32[64,256]{1,0:T(8,128)S(1)}, u32[]{:S(2)}, u32[]{:S(2)}) collective-permute-start(f32[64,256]{1,0:T(8,128)S(1)} %get-tuple-element.176), channel_id=1, source_target_pairs={{0,2},{1,3},{2,0},{3,1},{4,6},{5,7},{6,4},{7,5},{8,10},{9,11},{10,... | collective-permute-start | bytes 196616 | tf_op jit(solution)/shard_map/layer_one_back/ppermute | solution.py:39
  161.6 4.2 %collective-permute-start.34 = (f32[64,256]{1,0:T(8,128)S(1)}, f32[64,256]{1,0:T(8,128)S(1)}, u32[]{:S(2)}, u32[]{:S(2)}) collective-permute-start(f32[64,256]{1,0:T(8,128)S(1)} %get-tuple-element.176), channel_id=1, source_target_pairs={{0,1},{1,0},{2,3},{3,2},{4,5},{5,4},{6,7},{7,6},{8,9},{9,8},{10,11... | collective-permute-start | bytes 196616 | tf_op jit(solution)/shard_map/layer_one_back/ppermute | solution.py:39
  165.8 6.2 %collective-permute-start.37 = (f32[128,256]{1,0:T(8,128)S(1)}, f32[128,256]{1,0:T(8,128)S(1)}, u32[]{:S(2)}, u32[]{:S(2)}) collective-permute-start(f32[128,256]{1,0:T(8,128)S(1)} %get-tuple-element.182), channel_id=1, source_target_pairs={{0,1},{1,0},{2,3},{3,2},{4,5},{5,4},{6,7},{7,6},{8,9},{9,8},{10,11... | collective-permute-start | bytes 393224 | tf_op jit(solution)/shard_map/layer_one_back/ppermute | solution.py:39
  166.0 4.4 %collective-permute-start.40 = (f32[64,256]{1,0:T(8,128)S(1)}, f32[64,256]{1,0:T(8,128)S(1)}, u32[]{:S(2)}, u32[]{:S(2)}) collective-permute-start(f32[64,256]{1,0:T(8,128)S(1)} %add_add_fusion.3), channel_id=1, source_target_pairs={{0,4},{4,0},{8,12},{12,8},{16,20},{20,16},{24,28},{28,24},{1,5},{5... | collective-permute-start | bytes 196616 | tf_op jit(solution)/shard_map/layer_one_back/ppermute | solution.py:39
  168.1 7.2 %collective-permute-start.38 = (f32[128,256]{1,0:T(8,128)S(1)}, f32[128,256]{1,0:T(8,128)S(1)}, u32[]{:S(2)}, u32[]{:S(2)}) collective-permute-start(f32[128,256]{1,0:T(8,128)S(1)} %get-tuple-element.183), channel_id=1, source_target_pairs={{0,2},{1,3},{2,0},{3,1},{4,6},{5,7},{6,4},{7,5},{8,10},{9,11},{10,... | collective-permute-start | bytes 393224 | tf_op jit(solution)/shard_map/layer_one_back/ppermute | solution.py:39
  169.4 6.1 %collective-permute-start.39 = (f32[128,256]{1,0:T(8,128)S(1)}, f32[128,256]{1,0:T(8,128)S(1)}, u32[]{:S(2)}, u32[]{:S(2)}) collective-permute-start(f32[128,256]{1,0:T(8,128)S(1)} %get-tuple-element.184), channel_id=1, source_target_pairs={{0,3},{1,2},{2,1},{3,0},{4,7},{5,6},{6,5},{7,4},{8,11},{9,10},{10,... | collective-permute-start | bytes 393224 | tf_op jit(solution)/shard_map/layer_one_back/ppermute | solution.py:39
  170.4 6.9 %collective-permute-start.43 = (f32[64,256]{1,0:T(8,128)S(1)}, f32[64,256]{1,0:T(8,128)S(1)}, u32[]{:S(2)}, u32[]{:S(2)}) collective-permute-start(f32[64,256]{1,0:T(8,128)S(1)} %add.272), channel_id=1, source_target_pairs={{0,24},{4,28},{8,16},{12,20},{16,8},{20,12},{24,0},{28,4},{1,25},{... | collective-permute-start | bytes 196616 | tf_op jit(solution)/shard_map/layer_one_back/ppermute | solution.py:39
  171.9 7.1 %collective-permute-start.42 = (f32[64,256]{1,0:T(8,128)S(1)}, f32[64,256]{1,0:T(8,128)S(1)}, u32[]{:S(2)}, u32[]{:S(2)}) collective-permute-start(f32[64,256]{1,0:T(8,128)S(1)} %add.272), channel_id=1, source_target_pairs={{0,16},{4,20},{8,24},{12,28},{16,0},{20,4},{24,8},{28,12},{1,17},{... | collective-permute-start | bytes 196616 | tf_op jit(solution)/shard_map/layer_one_back/ppermute | solution.py:39
  172.0 6.9 %collective-permute-start.41 = (f32[64,256]{1,0:T(8,128)S(1)}, f32[64,256]{1,0:T(8,128)S(1)}, u32[]{:S(2)}, u32[]{:S(2)}) collective-permute-start(f32[64,256]{1,0:T(8,128)S(1)} %add.272), channel_id=1, source_target_pairs={{0,8},{4,12},{8,0},{12,4},{16,24},{20,28},{24,16},{28,20},{1,9},{5... | collective-permute-start | bytes 196616 | tf_op jit(solution)/shard_map/layer_one_back/ppermute | solution.py:39

commit v4 on v3

--- a/solution.py
+++ b/solution.py
@@ -20,6 +20,10 @@
 
 def in_hbm(*shape):
     return pltpu.HBM(shape, jnp.float32)
+
+
+def in_vmem(*shape):
+    return pltpu.VMEM(shape, jnp.float32)
 
 
 def from_hbm(x):
@@ -390,9 +394,10 @@
 
 
 def edge_kernel(
-    edges, layer, slots, first, tile, x_ref, a_ref, b_ref, stat_ref, small_ref,
-    out_ref, weight_ref, inv_ref, slope_ref, moment_ref, ysum_ref, table, centre, held, bounded,
+    edges, layer, slots, first, tile, away, x_ref, a_ref, b_ref, stat_ref, small_ref, *refs
 ):
+    out_ref, inv_ref, slope_ref, moment_ref, ysum_ref = refs[:5]
+    share_refs, (table, centre, held, bounded) = refs[5:-4], refs[-4:]
     points, width = a_ref.shape
     step = pl.program_id(0)
     block = 8
@@ -413,6 +418,14 @@
         bounded[0] = (jnp.max(reach) < 60.0).astype(jnp.int32)
 
     rows = pl.ds(pl.multiple_of(step * tile, tile), tile)
+
+    def keep(k, start, value):
+        if k < away:
+            share_refs[0][k, pl.ds(start, block), :] = value
+        else:
+            at = pl.ds(pl.multiple_of(step * tile + start, block), block)
+            share_refs[-1][k - away, at, :] = value
+
     columns = lax.broadcasted_iota(jnp.int32, (tile, points), 1).astype(jnp.float32)
 
     def gather(ids):
@@ -441,7 +454,7 @@
                 fall = jnp.exp2((-0.2 * LOG2E) * jnp.log(grown) - t)
                 share = grown * fall
                 part = fall + 0.25 * share
-                weight_ref[k, at, :] = part
+                keep(k, start, part)
                 totals = [total + term for total, term in zip(totals, (share, part, part * t, t))]
             finish(at, 0.0, totals)
 
@@ -472,7 +485,7 @@
                 level, grown = rise(t)
                 share = jnp.exp2(level - peak)
                 part = share * (1.0 / grown + 0.25)
-                weight_ref[k, at, :] = part
+                keep(k, pl.multiple_of(b * block, block), part)
                 totals = [total + term for total, term in zip(totals, (share, part, part * t, t))]
             finish(at, peak * (1.0 / LOG2E), totals)
             return carry
@@ -480,24 +493,32 @@
         lax.fori_loop(0, tile // block, some, 0)
 
 
-def edge_forward(edges, layer, slots, first, tile, x, a, b, stat, small):
+def edge_forward(edges, layer, slots, first, tile, away, x, a, b, stat, small):
     points, width = a.shape
     some = pl.BlockSpec((tile, width), lambda step: (step, 0))
-    return pl.pallas_call(
-        functools.partial(edge_kernel, edges, layer, slots, first, tile),
+    specs, shapes = [some] * 5, [f32(points, width)] * 5
+    if away:
+        specs.append(pl.BlockSpec((away, tile, width), lambda step: (0, step, 0)))
+        shapes.append(in_hbm(away, points, width))
+    if away < slots:
+        specs.append(VMEM)
+        shapes.append(in_vmem(slots - away, points, width))
+    results = pl.pallas_call(
+        functools.partial(edge_kernel, edges, layer, slots, first, tile, away),
         grid=(points // tile,),
         in_specs=[VMEM] * 5,
-        out_specs=[some, pl.BlockSpec((slots, tile, width), lambda step: (0, step, 0))] + [some] * 4,
-        out_shape=[f32(points, width), in_hbm(slots, points, width)] + [f32(points, width)] * 4,
+        out_specs=specs,
+        out_shape=shapes,
         scratch_shapes=[
             pltpu.VMEM((points, 2 * width), jnp.bfloat16),
             pltpu.VMEM((points, width), jnp.float32),
             pltpu.VMEM((slots, tile, width), jnp.float32),
             pltpu.SMEM((1,), jnp.int32),
         ],
-        compiler_params=params(24),
+        compiler_params=params(20),
         name="edges",
     )(x, a, b, stat, small)
+    return *results[:5], results[5:]
 
 
 def pool_kernel(me_ref, out_ref, inv_ref, slope_ref, moment_ref, gmax_ref, gmean_ref, *refs):
@@ -542,13 +563,13 @@
         pool_kernel,
         in_specs=[SMEM] + [VMEM] * (6 + count),
         out_shape=[f32(rows + 8, width)] * count + [f32(points, width)] * 2 + [f32(1, width)],
-        compiler_params=params(16),
+        compiler_params=params(8),
         name="pools",
     )(me, out, inv, slope, moment, grad_max, grad_mean, *acts)
     return results[:count], *results[count:]
 
 
-def scatter_kernel(first, group, small_rest, ids_ref, grad_ref, largest_ref, weight_ref, sum_ref):
+def scatter_kernel(first, start, group, resident, small_rest, ids_ref, grad_ref, largest_ref, weight_ref, sum_ref):
     step = pl.program_id(0)
     points, width = grad_ref.shape
     rows = lax.broadcasted_iota(jnp.int32, (points, points), 0).astype(jnp.float32)
@@ -556,7 +577,7 @@
     picks, small_picks, terms, rests = [], [], [], []
     for g in range(group):
         here = ids_ref[pl.ds(first + step * group + g, 1), :] == rows
-        value = grad_ref[...] * weight_ref[g]
+        value = grad_ref[...] * weight_ref[start + step * group + g if resident else g]
         picks.append(jnp.where(here, 1.0, 0.0).astype(jnp.bfloat16))
         if small_rest:
             high = value.astype(jnp.bfloat16)
@@ -587,26 +608,28 @@
         sum_ref[...] += total
 
 
-def scatter(ids, first, grad, largest, weight, start, stop, group):
+def scatter(ids, first, resident, grad, largest, weight, start, stop, group):
     points, width = grad.shape
     edges = (stop - start) * points
     return pl.pallas_call(
-        functools.partial(scatter_kernel, first + start, group, width >= 256),
+        functools.partial(scatter_kernel, first, start, group, resident, width >= 256),
         grid=((stop - start) // group,),
         in_specs=[
             VMEM,
             VMEM,
             VMEM,
-            pl.BlockSpec((group, points, width), lambda step: (start // group + step, 0, 0)),
+            VMEM
+            if resident
+            else pl.BlockSpec((group, points, width), lambda step: (start // group + step, 0, 0)),
         ],
         out_specs=VMEM,
         out_shape=f32(points, width),
-        compiler_params=params(36),
+        compiler_params=params(24),
         cost_estimate=pl.CostEstimate(
             flops=4 * edges * points * width, bytes_accessed=4 * edges * width, transcendentals=0
         ),
         name="scatter",
-    )(ids, grad, largest, from_hbm(weight))
+    )(ids, grad, largest, weight if resident else from_hbm(weight))
 
 
 def point_grads(edges, slots, own, inward_grads, ysum, inward, degree, local, stat, sums, gain, shift):
@@ -693,7 +716,7 @@
         out_shape=[f32(2 * width // count + 8, outs)] * count
         + [f32(points, width), f32(points, width), f32(1, outs)],
         scratch_shapes=[pltpu.VMEM((2 * width, outs), jnp.float32)],
-        compiler_params=params(32),
+        compiler_params=params(24),
         name="middle",
     )(me, *operands, *reached)
     return results[:count], *results[count:]
@@ -735,7 +758,7 @@
     results = pl.pallas_call(
         functools.partial(last_kernel, edges, slots, count),
         out_shape=[f32(1, outs), f32(width, 2 * outs)] + [f32(width + joined.shape[0] - 8, lanes)] * count,
-        compiler_params=params(32),
+        compiler_params=params(16),
         name="last",
     )(own, ysum, inward, degree, local, stat, joined, small, x, weight, *reached)
     return results[0], results[1], results[2:]
@@ -784,14 +807,14 @@
         late = [part_links(part, firsts[1:], slots, points) for part in parts[count // 2 :]]
         links = [links[-1] for links in early + late]
         stat_one = join_stats(local_one, local_edges)
-        hidden, share_one, inv_one, slope_one, moment_one, ysum_one = edge_forward(
-            edges, 0, slots, width, 128, x, a_one, b_one, stat_one, small
+        hidden, inv_one, slope_one, moment_one, ysum_one, share_one = edge_forward(
+            edges, 0, slots, width, 128, 0, x, a_one, b_one, stat_one, small
         )
     with jax.named_scope("layer_two"):
         a_two, b_two, in_two, deg_two, local_two = second_tables(hidden, weight_two, links, slots)
         stat_two = join_stats(local_two, local_edges)
-        out, share_two, inv_two, slope_two, moment_two, ysum_two = edge_forward(
-            edges, 1, slots, width + slots, 128, x, a_two, b_two, stat_two, small
+        out, inv_two, slope_two, moment_two, ysum_two, share_two = edge_forward(
+            edges, 1, slots, width + slots, 128, slots - 8, x, a_two, b_two, stat_two, small
         )
     with jax.named_scope("pools"):
         out_parts, scaled_two, own_two, largest_two = pools(
@@ -800,11 +823,19 @@
         out_parts = to_owner(out_parts)
         output, pool_max, pool_mean = unpack_output(me, out_parts)
 
-    def pieces(first, scaled, largest, share, *cuts):
+    def pieces(first, away, scaled, largest, shares, *cuts):
         def piece(start, stop):
-            return lambda ready: scatter(
-                ids, first, scaled if ready is None else after(scaled, ready), largest, share, start, stop, 4
-            )
+            near = start >= away
+            offset = away if near else 0
+
+            def run(ready):
+                grad = scaled if ready is None else after(scaled, ready)
+                return scatter(
+                    ids, first + start, near, grad, largest, shares[-1 if near else 0],
+                    start - offset, stop - offset, 4,
+                )
+
+            return run
 
         return [piece(*cut) for cut in zip((0, *cuts), (*cuts, slots))]
 
@@ -812,7 +843,7 @@
         sums_two, reached = sum_beside(
             lambda received: pair_sum([part[rows + 2 : rows + 4] for part in received]),
             out_parts,
-            pieces(slots, scaled_two, largest_two, share_two, slots - 8),
+            pieces(slots, slots - 8, scaled_two, largest_two, share_two, slots - 8),
         )
         wgrad_parts, scaled_one, own_one, gain_grad_two = middle(
             edges, slots, count, me, own_two, ysum_two, in_two, deg_two, local_two, stat_two, sums_two,
@@ -822,7 +853,7 @@
         joined, reached = sum_beside(
             lambda received: pair_sum(list(received)),
             to_owner(wgrad_parts),
-            pieces(0, scaled_one, scaled_one[:1], share_one, slots - 12, slots - 4),
+            pieces(0, 0, scaled_one, scaled_one[:1], share_one, slots - 12, slots - 4),
         )
         gain_grad_one, wgrad_one, grad_parts = last(
             edges, slots, count, own_one, ysum_one, in_one, deg_one, local_one, stat_one, joined,

time: 180 us -> 174 us (0.967)
  Pallas kernels: 112 us -> 104 us
    pallas_call x5, Pallas kernels: 40.2 us -> 33.7 us  [scatter(): pl.pallas_call(functools.partial(scatter_kernel, first, start, group, res...]
  transfers between devices with their start and end apart: 44 -> 44, of which waited for: 15 -> 15; matrix products, arithmetic and copies ran while one was open for 1% -> 1% of each run, Pallas kernels for 46% -> 43%
where the time goes in v4:
time: 174 us
  Pallas kernels  104 us (60%)
  starting transfers between devices  46.3 us (27%)
  waiting for transfers between devices  19.7 us (11%)
    ppermute x44, starting transfers between devices, exchange(): return lax.ppermute(x, axes, [(i, i ^ mask) for i in range(size)])  46.3 us
    pallas_call x2, Pallas kernels, edge_forward(): pl.pallas_call(functools.partial(edge_kernel, edges, layer, slots, first,...  45.9 us
    pallas_call x5, Pallas kernels, scatter(): pl.pallas_call(functools.partial(scatter_kernel, first, start, group, res...  33.7 us
    ppermute x44, waiting for transfers between devices, exchange(): return lax.ppermute(x, axes, [(i, i ^ mask) for i in range(size)])  19.7 us
    pallas_call x4, Pallas kernels, part_links(): pl.pallas_call(functools.partial(links_kernel, firsts, slots), out_shape=...  7.93 us
    pallas_call x1, Pallas kernels, first_tables(): pl.pallas_call(functools.partial(first_kernel, slots, width, count), out_...  4.37 us
  transfers between devices with their start and end apart: 44, of which 15 were waited for; matrix products, arithmetic and copies ran while one was open for 1% of the time, Pallas kernels for 43%

profile of v4, /device:TPU:0, one launch (start us, length us, event | category | flops | bytes accessed | tf_op | source)
XLA Modules:
  0.0 173.5 jit_solution(15397730969251652106)
XLA Ops:
  0.7 1.4 pack.1
  2.1 0.5 collective-permute-start
  2.6 2.6 %collective-permute-start.1 = (f32[104,256]{1,0:T(8,128)S(1)}, f32[104,256]{1,0:T(8,128)S(1)}, u32[]{:S(2)}, u32[]{:S(2)}) collective-permute-start(f32[104,256]{1,0:T(8,128)S(1)} %get-tuple-element.103), channel_id=1, source_target_pairs={{0,2},{1,3},{2,0},{3,1},{4,6},{5,7},{6,4},{7,5},{8,10},{9,11},{10,... | collective-permute-start | bytes 319496 | tf_op jit(solution)/shard_map/bring_clouds/ppermute | solution.py:43
  5.2 2.6 %part_links.4 = (bf16[1024,256]{1,0:T(8,128)(2,1)S(1)}, bf16[1024,256]{1,0:T(8,128)(2,1)S(1)}) custom-call(f32[104,256]{1,0:T(8,128)S(1)} %get-tuple-element.101.ids_ref.refs_0_), custom_call_target="tpu_custom_call" | custom-call | flops 1048576000 | bytes 524288 | tf_op jit(solution)/shard_map/bring_clouds/part_links/pallas_call | solution.py:291
  7.9 2.6 %part_links.5 = (bf16[1024,256]{1,0:T(8,128)(2,1)S(1)}, bf16[1024,256]{1,0:T(8,128)(2,1)S(1)}) custom-call(f32[104,256]{1,0:T(8,128)S(1)} %collective-permute-done.ids_ref.refs_1_), custom_call_target="tpu_custom_call" | custom-call | flops 1048576000 | bytes 524288 | tf_op jit(solution)/shard_map/bring_clouds/part_links/pallas_call | solution.py:291
  10.7 4.4 %first_tables.1 = (f32[1024,128]{1,0:T(8,128)S(1)}, f32[40,1024]{1,0:T(8,128)S(1)}, f32[1024,128]{1,0:T(8,128)S(1)}, f32[1024,128]{1,0:T(8,128)S(1)}, f32[1024,1...) custom-call(f32[104,256]{1,0:T(8,128)S(1)} %get-tuple-element.101.ids_ref.refs_0_, ...), custom_call_target="tpu_custom_call" | custom-call | tf_op jit(solution)/shard_map/layer_one/first_tables/pallas_call | solution.py:357
  15.1 1.6 collective-permute-start.5
  17.0 1.1 collective-permute-done.5
  18.2 2.1 %collective-permute-done.4 = f32[2,128]{1,0:T(2,128)S(1)} collective-permute-done((f32[2,128]{1,0:T(2,128)S(1)}, f32[2,128]{1,0:T(2,128)S(1)}, u32[]{:S(2)}, u32[]{:S(2)}) %collective-permute-start.4) | collective-permute-done | bytes 1056 | tf_op jit(solution)/shard_map/layer_one/ppermute | solution.py:43
  20.3 1.6 collective-permute-start.6
  21.9 1.3 part_links.7.refs_3_
  23.2 0.7 collective-permute-done.6
  23.9 3.7 %collective-permute-start.9 = (f32[2,128]{1,0:T(2,128)S(1)}, f32[2,128]{1,0:T(2,128)S(1)}, u32[]{:S(2)}, u32[]{:S(2)}) collective-permute-start(f32[2,128]{1,0:T(2,128)S(1)} %pad_maximum_fusion.5), channel_id=1, source_target_pairs={{0,24},{4,28},{8,16},{12,20},{16,8},{20,12},{24,0},{28,4},{1,25},{... | collective-permute-start | bytes 3080 | tf_op jit(solution)/shard_map/layer_one/ppermute | solution.py:43
  27.6 0.8 collective-permute-start.7
  28.4 1.3 part_links.6.refs_2_
  29.7 2.3 %collective-permute-done.8 = f32[2,128]{1,0:T(2,128)S(1)} collective-permute-done((f32[2,128]{1,0:T(2,128)S(1)}, f32[2,128]{1,0:T(2,128)S(1)}, u32[]{:S(2)}, u32[]{:S(2)}) %collective-permute-start.8) | collective-permute-done | bytes 1056 | tf_op jit(solution)/shard_map/layer_one/ppermute | solution.py:43
  32.1 15.3 %edges.2 = (f32[1024,128]{1,0:T(8,128)S(1)}, f32[1024,128]{1,0:T(8,128)S(1)}, f32[1024,128]{1,0:T(8,128)S(1)}, f32[1024,128]{1,0:T(8,128)S(1)}, f32[1024,128]{1,0:T(8,128)S(1)}, /*index=5*/f32[20,1024,128]{2,1,0:T(8,128)S(1)}) custom-call(f32[1024,128]{1,0:T(8,128)S(1)} %get-tuple-element.108.x_ref, f32[1024,128]{1,0:T(8,128)S(1)} %get-tuple-element.109.a_ref, ...), custom_call_target="tpu_custom_call" | custom-call | tf_op jit(solution)/shard_map/layer_one/edges/pallas_call | solution.py:506
  47.4 2.6 %second_tables.1 = (f32[1024,256]{1,0:T(8,128)S(1)}, f32[1024,256]{1,0:T(8,128)S(1)}, f32[1024,256]{1,0:T(8,128)S(1)}, f32[1024,128]{1,0:T(8,128)S(1)}, f32[2,256]{1,0:T(2,128)S(1)}) custom-call(f32[1024,128]{1,0:T(8,128)S(1)} %get-tuple-element.113.x_ref, f32[256,256]{1,0:T(8,128)S(1)} %get-tuple-element.114.weight_ref, ...), custom_call_target="tpu_custom_call" | custom-call | tf_op jit(solution)/shard_map/layer_two/second_tables/pallas_call | solution.py:382
  50.1 0.6 collective-permute-start.11
  50.7 1.3 collective-permute-start.10
  52.0 1.1 collective-permute-done.12
  53.1 0.7 collective-permute-done.11
  53.8 1.6 collective-permute-start.13
  55.4 2.1 %collective-permute-done.13 = f32[2,256]{1,0:T(2,128)S(1)} collective-permute-done((f32[2,256]{1,0:T(2,128)S(1)}, f32[2,256]{1,0:T(2,128)S(1)}, u32[]{:S(2)}, u32[]{:S(2)}) %collective-permute-start.13) | collective-permute-done | bytes 2080 | tf_op jit(solution)/shard_map/layer_two/ppermute | solution.py:43
  57.5 1.5 collective-permute-start.16
  59.0 0.6 collective-permute-start.15
  59.7 2.3 %collective-permute-start.14 = (f32[2,256]{1,0:T(2,128)S(1)}, f32[2,256]{1,0:T(2,128)S(1)}, u32[]{:S(2)}, u32[]{:S(2)}) collective-permute-start(f32[2,256]{1,0:T(2,128)S(1)} %pad_maximum_fusion.2), channel_id=1, source_target_pairs={{0,8},{4,12},{8,0},{12,4},{16,24},{20,28},{24,16},{28,20},{1,9},{5... | collective-permute-start | bytes 6152 | tf_op jit(solution)/shard_map/layer_two/ppermute | solution.py:43
  61.9 1.3 split.13
  63.3 0.6 collective-permute-start.18
  63.9 1.3 collective-permute-start.19
  65.2 30.6 %edges.3 = (f32[1024,256]{1,0:T(8,128)S(1)}, f32[1024,256]{1,0:T(8,128)S(1)}, f32[1024,256]{1,0:T(8,128)S(1)}, f32[1024,256]{1,0:T(8,128)S(1)}, f32[1024,256]{1,...) custom-call(f32[1024,128]{1,0:T(8,128)S(1)} %get-tuple-element.108.x_ref, ...), custom_call_target="tpu_custom_call" | custom-call | tf_op jit(solution)/shard_map/layer_two/edges/pallas_call | solution.py:506
  95.9 0.9 pools.1
  97.7 1.0 collective-permute-start.22
  98.7 13.7 %scatter.5.refs_0_ = f32[1024,256]{1,0:T(8,128)S(1)} custom-call(f32[40,1024]{1,0:T(8,128)S(1)} %get-tuple-element.139.ids_ref, f32[1024,256]{1,0:T(8,128)S(1)} %get-tuple-element.147.grad_ref, f32[1,256]{1,0:T(1,128)S(1)} %get-tuple-element.141.largest_ref, f32[12,1024,256]{2,1,0:T(8,128)} %get-tuple-element.142.weight_ref), custom_call_target="tpu_custom_call" | custom-call | flops 12884901888 | bytes 12582912 | tf_op jit(solution)/shard_map/layer_two_back/scatter/pallas_call | solution.py:614
  112.4 1.5 collective-permute-start.25
  114.3 2.6 %collective-permute-start.23 = (f32[2,256]{1,0:T(2,128)S(1)}, f32[2,256]{1,0:T(2,128)S(1)}, u32[]{:S(2)}, u32[]{:S(2)}) collective-permute-start(f32[2,256]{1,0:T(2,128)S(1)} %add_add_fusion.5), channel_id=1, source_target_pairs={{0,8},{4,12},{8,0},{12,4},{16,24},{20,28},{24,16},{28,20},{1,9},{5... | collective-permute-start | bytes 6152 | tf_op jit(solution)/shard_map/layer_two_back/ppermute | solution.py:43
  116.9 7.7 %scatter.6.refs_1_ = f32[1024,256]{1,0:T(8,128)S(1)} custom-call(f32[40,1024]{1,0:T(8,128)S(1)} %get-tuple-element.139.ids_ref, f32[1024,256]{1,0:T(8,128)S(1)} %get-tuple-element.147.grad_ref, f32[1,256]{1,0:T(1,128)S(1)} %get-tuple-element.141.largest_ref, f32[8,1024,256]{2,1,0:T(8,128)S(1)} %get-tuple-element.148.weight_ref), custom_call_target="tpu_custom_call" | custom-call | flops 8589934592 | bytes 8388608 | tf_op jit(solution)/shard_map/layer_two_back/scatter/pallas_call | solution.py:614
  124.6 1.6 collective-permute-start.26
  126.2 2.1 %collective-permute-done.26 = f32[2,256]{1,0:T(2,128)S(1)} collective-permute-done((f32[2,256]{1,0:T(2,128)S(1)}, f32[2,256]{1,0:T(2,128)S(1)}, u32[]{:S(2)}, u32[]{:S(2)}) %collective-permute-start.26) | collective-permute-done | bytes 2080 | tf_op jit(solution)/shard_map/layer_two_back/ppermute | solution.py:43
  128.3 3.1 %middle.1 = (f32[72,256]{1,0:T(8,128)S(1)}, f32[72,256]{1,0:T(8,128)S(1)}, f32[72,256]{1,0:T(8,128)S(1)}, f32[72,256]{1,0:T(8,128)S(1)}, f32[1024,128]{1,0:T(8,1...) custom-call(s32[1]{0:T(128)} %bitcast.me_ref, f32[1024,256]{1,0:T(8,128)S(1)} %get-tuple-element.135.own_ref, ...), custom_call_target="tpu_custom_call" | custom-call | tf_op jit(solution)/shard_map/layer_two_back/middle/pallas_call | solution.py:713
  131.3 0.5 collective-permute-start.28
  131.8 1.3 collective-permute-start.29
  133.2 4.9 %scatter.7.refs_0_ = f32[1024,128]{1,0:T(8,128)S(1)} custom-call(f32[40,1024]{1,0:T(8,128)S(1)} %get-tuple-element.139.ids_ref, f32[1024,128]{1,0:T(8,128)S(1)} %get-tuple-element.175.grad_ref, f32[1,128]{1,0:T(1,128)S(1)} %slice.169.largest_ref, f32[20,1024,128]{2,1,0:T(8,128)S(1)} %get-tuple-element.165.weight_ref), custom_call_target="tpu_custom_call" | custom-call | flops 4294967296 | bytes 4194304 | tf_op jit(solution)/shard_map/layer_one_back/scatter/pallas_call | solution.py:614
  138.1 1.5 collective-permute-start.32
  139.6 2.9 %collective-permute-start.30 = (f32[72,256]{1,0:T(8,128)S(1)}, f32[72,256]{1,0:T(8,128)S(1)}, u32[]{:S(2)}, u32[]{:S(2)}) collective-permute-start(f32[72,256]{1,0:T(8,128)S(1)} %add_add_fusion.1), channel_id=1, source_target_pairs={{0,8},{4,12},{8,0},{12,4},{16,24},{20,28},{24,16},{28,20},{1,9},{5... | collective-permute-start | bytes 221192 | tf_op jit(solution)/shard_map/layer_one_back/ppermute | solution.py:43
  142.6 5.1 %scatter.8.refs_1_ = f32[1024,128]{1,0:T(8,128)S(1)} custom-call(f32[40,1024]{1,0:T(8,128)S(1)} %get-tuple-element.139.ids_ref, f32[1024,128]{1,0:T(8,128)S(1)} %get-tuple-element.175.grad_ref, f32[1,128]{1,0:T(1,128)S(1)} %slice.169.largest_ref, f32[20,1024,128]{2,1,0:T(8,128)S(1)} %get-tuple-element.165.weight_ref), custom_call_target="tpu_custom_call" | custom-call | flops 4294967296 | bytes 4194304 | tf_op jit(solution)/shard_map/layer_one_back/scatter/pallas_call | solution.py:614
  147.7 1.6 collective-permute-start.33
  149.3 2.4 %scatter.9.refs_2_ = f32[1024,128]{1,0:T(8,128)S(1)} custom-call(f32[40,1024]{1,0:T(8,128)S(1)} %get-tuple-element.139.ids_ref, f32[1024,128]{1,0:T(8,128)S(1)} %get-tuple-element.175.grad_ref, f32[1,128]{1,0:T(1,128)S(1)} %slice.169.largest_ref, f32[20,1024,128]{2,1,0:T(8,128)S(1)} %get-tuple-element.165.weight_ref), custom_call_target="tpu_custom_call" | custom-call | flops 2147483648 | bytes 2097152 | tf_op jit(solution)/shard_map/layer_one_back/scatter/pallas_call | solution.py:614
  152.2 1.4 last.1
  153.7 0.8 collective-permute-start.35
  154.5 1.1 collective-permute-start.34
  155.5 2.0 %collective-permute-done.36 = f32[64,256]{1,0:T(8,128)S(1)} collective-permute-done((f32[64,256]{1,0:T(8,128)S(1)}, f32[64,256]{1,0:T(8,128)S(1)}, u32[]{:S(2)}, u32[]{:S(2)}) %collective-permute-start.36) | collective-permute-done | bytes 65568 | tf_op jit(solution)/shard_map/layer_one_back/ppermute | solution.py:43
  157.6 1.1 collective-permute-done.35
  158.9 1.5 collective-permute-start.40
  160.4 1.0 unpack_output.1
  161.5 0.6 slice.187
  162.0 1.3 collective-permute-start.38
  163.5 1.5 collective-permute-start.43
  165.0 2.9 %collective-permute-start.41 = (f32[64,256]{1,0:T(8,128)S(1)}, f32[64,256]{1,0:T(8,128)S(1)}, u32[]{:S(2)}, u32[]{:S(2)}) collective-permute-start(f32[64,256]{1,0:T(8,128)S(1)} %add.272), channel_id=1, source_target_pairs={{0,8},{4,12},{8,0},{12,4},{16,24},{20,28},{24,16},{28,20},{1,9},{5... | collective-permute-start | bytes 196616 | tf_op jit(solution)/shard_map/layer_one_back/ppermute | solution.py:43
  167.9 0.5 slice_bitcast_fusion
  168.5 1.0 collective-permute-done.39.refs_3_
  169.5 0.8 unpack_grad.1
  170.4 2.5 %collective-permute-done.42 = f32[64,256]{1,0:T(8,128)S(1)} collective-permute-done((f32[64,256]{1,0:T(8,128)S(1)}, f32[64,256]{1,0:T(8,128)S(1)}, u32[]{:S(2)}, u32[]{:S(2)}) %collective-permute-start.42) | collective-permute-done | bytes 65568 | tf_op jit(solution)/shard_map/layer_one_back/ppermute | solution.py:43
  172.9 0.6 pad_maximum_fusion
  (74 shorter events, 3.4 us)
Async XLA Ops:
  2.1 5.8 %collective-permute-start = (f32[104,256]{1,0:T(8,128)S(1)}, f32[104,256]{1,0:T(8,128)S(1)}, u32[]{:S(2)}, u32[]{:S(2)}) collective-permute-start(f32[104,256]{1,0:T(8,128)S(1)} %get-tuple-element.102), channel_id=1, source_target_pairs={{0,1},{1,0},{2,3},{3,2},{4,5},{5,4},{6,7},{7,6},{8,9},{9,8},{10,11... | collective-permute-start | bytes 319496 | tf_op jit(solution)/shard_map/bring_clouds/ppermute | solution.py:43
  2.6 8.0 %collective-permute-start.1 = (f32[104,256]{1,0:T(8,128)S(1)}, f32[104,256]{1,0:T(8,128)S(1)}, u32[]{:S(2)}, u32[]{:S(2)}) collective-permute-start(f32[104,256]{1,0:T(8,128)S(1)} %get-tuple-element.103), channel_id=1, source_target_pairs={{0,2},{1,3},{2,0},{3,1},{4,6},{5,7},{6,4},{7,5},{8,10},{9,11},{10,... | collective-permute-start | bytes 319496 | tf_op jit(solution)/shard_map/bring_clouds/ppermute | solution.py:43
  5.2 5.6 %collective-permute-start.2 = (f32[104,256]{1,0:T(8,128)S(1)}, f32[104,256]{1,0:T(8,128)S(1)}, u32[]{:S(2)}, u32[]{:S(2)}) collective-permute-start(f32[104,256]{1,0:T(8,128)S(1)} %get-tuple-element.104), channel_id=1, source_target_pairs={{0,3},{1,2},{2,1},{3,0},{4,7},{5,6},{6,5},{7,4},{8,11},{9,10},{10,... | collective-permute-start | bytes 319496 | tf_op jit(solution)/shard_map/bring_clouds/ppermute | solution.py:43
  5.2 90.7 %copy-start = (f32[4,256]{1,0:T(4,128)S(1)}, f32[4,256]{1,0:T(4,128)}, u32[]{:S(2)}) copy-start(f32[4,256]{1,0:T(4,128)} %gmax_ref.1) | copy-start | bytes 12292
  5.2 90.7 %copy-start.1 = (f32[4,256]{1,0:T(4,128)S(1)}, f32[4,256]{1,0:T(4,128)}, u32[]{:S(2)}) copy-start(f32[4,256]{1,0:T(4,128)} %gmean_ref.1) | copy-start | bytes 12292
  15.1 3.1 %collective-permute-start.5 = (f32[2,128]{1,0:T(2,128)S(1)}, f32[2,128]{1,0:T(2,128)S(1)}, u32[]{:S(2)}, u32[]{:S(2)}) collective-permute-start(f32[2,128]{1,0:T(2,128)S(1)} %get-tuple-element.111.local_ref), channel_id=1, source_target_pairs={{0,3},{1,2},{2,1},{3,0},{4,7},{5,6},{6,5},{7,4},{8,11},{9,10},{10,... | collective-permute-start | bytes 3080 | tf_op jit(solution)/shard_map/layer_one/ppermute | solution.py:43
  16.7 3.6 %collective-permute-start.4 = (f32[2,128]{1,0:T(2,128)S(1)}, f32[2,128]{1,0:T(2,128)S(1)}, u32[]{:S(2)}, u32[]{:S(2)}) collective-permute-start(f32[2,128]{1,0:T(2,128)S(1)} %get-tuple-element.111.local_ref), channel_id=1, source_target_pairs={{0,2},{1,3},{2,0},{3,1},{4,6},{5,7},{6,4},{7,5},{8,10},{9,11},{10,... | collective-permute-start | bytes 3080 | tf_op jit(solution)/shard_map/layer_one/ppermute | solution.py:43
  17.0 3.3 %collective-permute-start.3 = (f32[2,128]{1,0:T(2,128)S(1)}, f32[2,128]{1,0:T(2,128)S(1)}, u32[]{:S(2)}, u32[]{:S(2)}) collective-permute-start(f32[2,128]{1,0:T(2,128)S(1)} %get-tuple-element.111.local_ref), channel_id=1, source_target_pairs={{0,1},{1,0},{2,3},{3,2},{4,5},{5,4},{6,7},{7,6},{8,9},{9,8},{10,11... | collective-permute-start | bytes 3080 | tf_op jit(solution)/shard_map/layer_one/ppermute | solution.py:43
  20.3 3.6 %collective-permute-start.6 = (f32[2,128]{1,0:T(2,128)S(1)}, f32[2,128]{1,0:T(2,128)S(1)}, u32[]{:S(2)}, u32[]{:S(2)}) collective-permute-start(f32[2,128]{1,0:T(2,128)S(1)} %pad_maximum_fusion.4), channel_id=1, source_target_pairs={{0,4},{4,0},{8,12},{12,8},{16,20},{20,16},{24,28},{28,24},{1,5},{5... | collective-permute-start | bytes 3080 | tf_op jit(solution)/shard_map/layer_one/ppermute | solution.py:43
  23.9 5.8 %collective-permute-start.9 = (f32[2,128]{1,0:T(2,128)S(1)}, f32[2,128]{1,0:T(2,128)S(1)}, u32[]{:S(2)}, u32[]{:S(2)}) collective-permute-start(f32[2,128]{1,0:T(2,128)S(1)} %pad_maximum_fusion.5), channel_id=1, source_target_pairs={{0,24},{4,28},{8,16},{12,20},{16,8},{20,12},{24,0},{28,4},{1,25},{... | collective-permute-start | bytes 3080 | tf_op jit(solution)/shard_map/layer_one/ppermute | solution.py:43
  27.6 4.5 %collective-permute-start.8 = (f32[2,128]{1,0:T(2,128)S(1)}, f32[2,128]{1,0:T(2,128)S(1)}, u32[]{:S(2)}, u32[]{:S(2)}) collective-permute-start(f32[2,128]{1,0:T(2,128)S(1)} %pad_maximum_fusion.5), channel_id=1, source_target_pairs={{0,16},{4,20},{8,24},{12,28},{16,0},{20,4},{24,8},{28,12},{1,17},{... | collective-permute-start | bytes 3080 | tf_op jit(solution)/shard_map/layer_one/ppermute | solution.py:43
  27.6 4.5 %collective-permute-start.7 = (f32[2,128]{1,0:T(2,128)S(1)}, f32[2,128]{1,0:T(2,128)S(1)}, u32[]{:S(2)}, u32[]{:S(2)}) collective-permute-start(f32[2,128]{1,0:T(2,128)S(1)} %pad_maximum_fusion.5), channel_id=1, source_target_pairs={{0,8},{4,12},{8,0},{12,4},{16,24},{20,28},{24,16},{28,20},{1,9},{5... | collective-permute-start | bytes 3080 | tf_op jit(solution)/shard_map/layer_one/ppermute | solution.py:43
  50.0 3.1 %collective-permute-start.12 = (f32[2,256]{1,0:T(2,128)S(1)}, f32[2,256]{1,0:T(2,128)S(1)}, u32[]{:S(2)}, u32[]{:S(2)}) collective-permute-start(f32[2,256]{1,0:T(2,128)S(1)} %get-tuple-element.119.local_ref), channel_id=1, source_target_pairs={{0,3},{1,2},{2,1},{3,0},{4,7},{5,6},{6,5},{7,4},{8,11},{9,10},{10,... | collective-permute-start | bytes 6152 | tf_op jit(solution)/shard_map/layer_two/ppermute | solution.py:43
  50.1 3.7 %collective-permute-start.11 = (f32[2,256]{1,0:T(2,128)S(1)}, f32[2,256]{1,0:T(2,128)S(1)}, u32[]{:S(2)}, u32[]{:S(2)}) collective-permute-start(f32[2,256]{1,0:T(2,128)S(1)} %get-tuple-element.119.local_ref), channel_id=1, source_target_pairs={{0,2},{1,3},{2,0},{3,1},{4,6},{5,7},{6,4},{7,5},{8,10},{9,11},{10,... | collective-permute-start | bytes 6152 | tf_op jit(solution)/shard_map/layer_two/ppermute | solution.py:43
  50.7 3.1 %collective-permute-start.10 = (f32[2,256]{1,0:T(2,128)S(1)}, f32[2,256]{1,0:T(2,128)S(1)}, u32[]{:S(2)}, u32[]{:S(2)}) collective-permute-start(f32[2,256]{1,0:T(2,128)S(1)} %get-tuple-element.119.local_ref), channel_id=1, source_target_pairs={{0,1},{1,0},{2,3},{3,2},{4,5},{5,4},{6,7},{7,6},{8,9},{9,8},{10,11... | collective-permute-start | bytes 6152 | tf_op jit(solution)/shard_map/layer_two/ppermute | solution.py:43
  53.8 3.7 %collective-permute-start.13 = (f32[2,256]{1,0:T(2,128)S(1)}, f32[2,256]{1,0:T(2,128)S(1)}, u32[]{:S(2)}, u32[]{:S(2)}) collective-permute-start(f32[2,256]{1,0:T(2,128)S(1)} %pad_maximum_fusion.1), channel_id=1, source_target_pairs={{0,4},{4,0},{8,12},{12,8},{16,20},{20,16},{24,28},{28,24},{1,5},{5... | collective-permute-start | bytes 6152 | tf_op jit(solution)/shard_map/layer_two/ppermute | solution.py:43
  57.5 6.4 %collective-permute-start.16 = (f32[2,256]{1,0:T(2,128)S(1)}, f32[2,256]{1,0:T(2,128)S(1)}, u32[]{:S(2)}, u32[]{:S(2)}) collective-permute-start(f32[2,256]{1,0:T(2,128)S(1)} %pad_maximum_fusion.2), channel_id=1, source_target_pairs={{0,24},{4,28},{8,16},{12,20},{16,8},{20,12},{24,0},{28,4},{1,25},{... | collective-permute-start | bytes 6152 | tf_op jit(solution)/shard_map/layer_two/ppermute | solution.py:43
  59.0 6.2 %collective-permute-start.15 = (f32[2,256]{1,0:T(2,128)S(1)}, f32[2,256]{1,0:T(2,128)S(1)}, u32[]{:S(2)}, u32[]{:S(2)}) collective-permute-start(f32[2,256]{1,0:T(2,128)S(1)} %pad_maximum_fusion.2), channel_id=1, source_target_pairs={{0,16},{4,20},{8,24},{12,28},{16,0},{20,4},{24,8},{28,12},{1,17},{... | collective-permute-start | bytes 6152 | tf_op jit(solution)/shard_map/layer_two/ppermute | solution.py:43
  59.7 5.5 %collective-permute-start.14 = (f32[2,256]{1,0:T(2,128)S(1)}, f32[2,256]{1,0:T(2,128)S(1)}, u32[]{:S(2)}, u32[]{:S(2)}) collective-permute-start(f32[2,256]{1,0:T(2,128)S(1)} %pad_maximum_fusion.2), channel_id=1, source_target_pairs={{0,8},{4,12},{8,0},{12,4},{16,24},{20,28},{24,16},{28,20},{1,9},{5... | collective-permute-start | bytes 6152 | tf_op jit(solution)/shard_map/layer_two/ppermute | solution.py:43
  63.2 32.6 %collective-permute-start.17 = (f32[256,256]{1,0:T(8,128)S(1)}, f32[256,256]{1,0:T(8,128)S(1)}, u32[]{:S(2)}, u32[]{:S(2)}) collective-permute-start(f32[256,256]{1,0:T(8,128)S(1)} %get-tuple-element.125), channel_id=1, source_target_pairs={{0,1},{1,0},{2,3},{3,2},{4,5},{5,4},{6,7},{7,6},{8,9},{9,8},{10,11... | collective-permute-start | bytes 786440 | tf_op jit(solution)/shard_map/bring_cotangents/ppermute | solution.py:43
  63.3 32.5 %collective-permute-start.18 = (f32[256,256]{1,0:T(8,128)S(1)}, f32[256,256]{1,0:T(8,128)S(1)}, u32[]{:S(2)}, u32[]{:S(2)}) collective-permute-start(f32[256,256]{1,0:T(8,128)S(1)} %get-tuple-element.126), channel_id=1, source_target_pairs={{0,2},{1,3},{2,0},{3,1},{4,6},{5,7},{6,4},{7,5},{8,10},{9,11},{10,... | collective-permute-start | bytes 786440 | tf_op jit(solution)/shard_map/bring_cotangents/ppermute | solution.py:43
  63.9 32.0 %collective-permute-start.19 = (f32[256,256]{1,0:T(8,128)S(1)}, f32[256,256]{1,0:T(8,128)S(1)}, u32[]{:S(2)}, u32[]{:S(2)}) collective-permute-start(f32[256,256]{1,0:T(8,128)S(1)} %get-tuple-element.127), channel_id=1, source_target_pairs={{0,3},{1,2},{2,1},{3,0},{4,7},{5,6},{6,5},{7,4},{8,11},{9,10},{10,... | collective-permute-start | bytes 786440 | tf_op jit(solution)/shard_map/bring_cotangents/ppermute | solution.py:43
  96.8 15.6 %collective-permute-start.20 = (f32[264,256]{1,0:T(8,128)S(1)}, f32[264,256]{1,0:T(8,128)S(1)}, u32[]{:S(2)}, u32[]{:S(2)}) collective-permute-start(f32[264,256]{1,0:T(8,128)S(1)} %get-tuple-element.129), channel_id=1, source_target_pairs={{0,1},{1,0},{2,3},{3,2},{4,5},{5,4},{6,7},{7,6},{8,9},{9,8},{10,11... | collective-permute-start | bytes 811016 | tf_op jit(solution)/shard_map/pools/ppermute | solution.py:43
  97.2 15.2 %collective-permute-start.21 = (f32[264,256]{1,0:T(8,128)S(1)}, f32[264,256]{1,0:T(8,128)S(1)}, u32[]{:S(2)}, u32[]{:S(2)}) collective-permute-start(f32[264,256]{1,0:T(8,128)S(1)} %get-tuple-element.130), channel_id=1, source_target_pairs={{0,2},{1,3},{2,0},{3,1},{4,6},{5,7},{6,4},{7,5},{8,10},{9,11},{10,... | collective-permute-start | bytes 811016 | tf_op jit(solution)/shard_map/pools/ppermute | solution.py:43
  97.7 14.7 %collective-permute-start.22 = (f32[264,256]{1,0:T(8,128)S(1)}, f32[264,256]{1,0:T(8,128)S(1)}, u32[]{:S(2)}, u32[]{:S(2)}) collective-permute-start(f32[264,256]{1,0:T(8,128)S(1)} %get-tuple-element.131), channel_id=1, source_target_pairs={{0,3},{1,2},{2,1},{3,0},{4,7},{5,6},{6,5},{7,4},{8,11},{9,10},{10,... | collective-permute-start | bytes 811016 | tf_op jit(solution)/shard_map/pools/ppermute | solution.py:43
  112.4 12.1 %collective-permute-start.25 = (f32[2,256]{1,0:T(2,128)S(1)}, f32[2,256]{1,0:T(2,128)S(1)}, u32[]{:S(2)}, u32[]{:S(2)}) collective-permute-start(f32[2,256]{1,0:T(2,128)S(1)} %add_add_fusion.5), channel_id=1, source_target_pairs={{0,24},{4,28},{8,16},{12,20},{16,8},{20,12},{24,0},{28,4},{1,25},{... | collective-permute-start | bytes 6152 | tf_op jit(solution)/shard_map/layer_two_back/ppermute | solution.py:43
  113.9 10.6 %collective-permute-start.24 = (f32[2,256]{1,0:T(2,128)S(1)}, f32[2,256]{1,0:T(2,128)S(1)}, u32[]{:S(2)}, u32[]{:S(2)}) collective-permute-start(f32[2,256]{1,0:T(2,128)S(1)} %add_add_fusion.5), channel_id=1, source_target_pairs={{0,16},{4,20},{8,24},{12,28},{16,0},{20,4},{24,8},{28,12},{1,17},{... | collective-permute-start | bytes 6152 | tf_op jit(solution)/shard_map/layer_two_back/ppermute | solution.py:43
  114.3 10.3 %collective-permute-start.23 = (f32[2,256]{1,0:T(2,128)S(1)}, f32[2,256]{1,0:T(2,128)S(1)}, u32[]{:S(2)}, u32[]{:S(2)}) collective-permute-start(f32[2,256]{1,0:T(2,128)S(1)} %add_add_fusion.5), channel_id=1, source_target_pairs={{0,8},{4,12},{8,0},{12,4},{16,24},{20,28},{24,16},{28,20},{1,9},{5... | collective-permute-start | bytes 6152 | tf_op jit(solution)/shard_map/layer_two_back/ppermute | solution.py:43
  124.6 3.7 %collective-permute-start.26 = (f32[2,256]{1,0:T(2,128)S(1)}, f32[2,256]{1,0:T(2,128)S(1)}, u32[]{:S(2)}, u32[]{:S(2)}) collective-permute-start(f32[2,256]{1,0:T(2,128)S(1)} %add_add_fusion.4), channel_id=1, source_target_pairs={{0,4},{4,0},{8,12},{12,8},{16,20},{20,16},{24,28},{28,24},{1,5},{5... | collective-permute-start | bytes 6152 | tf_op jit(solution)/shard_map/layer_two_back/ppermute | solution.py:43
  131.3 6.7 %collective-permute-start.27 = (f32[72,256]{1,0:T(8,128)S(1)}, f32[72,256]{1,0:T(8,128)S(1)}, u32[]{:S(2)}, u32[]{:S(2)}) collective-permute-start(f32[72,256]{1,0:T(8,128)S(1)} %get-tuple-element.161), channel_id=1, source_target_pairs={{0,1},{1,0},{2,3},{3,2},{4,5},{5,4},{6,7},{7,6},{8,9},{9,8},{10,11... | collective-permute-start | bytes 221192 | tf_op jit(solution)/shard_map/layer_one_back/ppermute | solution.py:43
  131.3 6.7 %collective-permute-start.28 = (f32[72,256]{1,0:T(8,128)S(1)}, f32[72,256]{1,0:T(8,128)S(1)}, u32[]{:S(2)}, u32[]{:S(2)}) collective-permute-start(f32[72,256]{1,0:T(8,128)S(1)} %get-tuple-element.162), channel_id=1, source_target_pairs={{0,2},{1,3},{2,0},{3,1},{4,6},{5,7},{6,4},{7,5},{8,10},{9,11},{10,... | collective-permute-start | bytes 221192 | tf_op jit(solution)/shard_map/layer_one_back/ppermute | solution.py:43
  131.8 6.2 %collective-permute-start.29 = (f32[72,256]{1,0:T(8,128)S(1)}, f32[72,256]{1,0:T(8,128)S(1)}, u32[]{:S(2)}, u32[]{:S(2)}) collective-permute-start(f32[72,256]{1,0:T(8,128)S(1)} %get-tuple-element.163), channel_id=1, source_target_pairs={{0,3},{1,2},{2,1},{3,0},{4,7},{5,6},{6,5},{7,4},{8,11},{9,10},{10,... | collective-permute-start | bytes 221192 | tf_op jit(solution)/shard_map/layer_one_back/ppermute | solution.py:43
  138.1 9.6 %collective-permute-start.32 = (f32[72,256]{1,0:T(8,128)S(1)}, f32[72,256]{1,0:T(8,128)S(1)}, u32[]{:S(2)}, u32[]{:S(2)}) collective-permute-start(f32[72,256]{1,0:T(8,128)S(1)} %add_add_fusion.1), channel_id=1, source_target_pairs={{0,24},{4,28},{8,16},{12,20},{16,8},{20,12},{24,0},{28,4},{1,25},{... | collective-permute-start | bytes 221192 | tf_op jit(solution)/shard_map/layer_one_back/ppermute | solution.py:43
  139.6 8.1 %collective-permute-start.31 = (f32[72,256]{1,0:T(8,128)S(1)}, f32[72,256]{1,0:T(8,128)S(1)}, u32[]{:S(2)}, u32[]{:S(2)}) collective-permute-start(f32[72,256]{1,0:T(8,128)S(1)} %add_add_fusion.1), channel_id=1, source_target_pairs={{0,16},{4,20},{8,24},{12,28},{16,0},{20,4},{24,8},{28,12},{1,17},{... | collective-permute-start | bytes 221192 | tf_op jit(solution)/shard_map/layer_one_back/ppermute | solution.py:43
  139.6 8.1 %collective-permute-start.30 = (f32[72,256]{1,0:T(8,128)S(1)}, f32[72,256]{1,0:T(8,128)S(1)}, u32[]{:S(2)}, u32[]{:S(2)}) collective-permute-start(f32[72,256]{1,0:T(8,128)S(1)} %add_add_fusion.1), channel_id=1, source_target_pairs={{0,8},{4,12},{8,0},{12,4},{16,24},{20,28},{24,16},{28,20},{1,9},{5... | collective-permute-start | bytes 221192 | tf_op jit(solution)/shard_map/layer_one_back/ppermute | solution.py:43
  147.7 4.4 %collective-permute-start.33 = (f32[72,256]{1,0:T(8,128)S(1)}, f32[72,256]{1,0:T(8,128)S(1)}, u32[]{:S(2)}, u32[]{:S(2)}) collective-permute-start(f32[72,256]{1,0:T(8,128)S(1)} %add_add_fusion), channel_id=1, source_target_pairs={{0,4},{4,0},{8,12},{12,8},{16,20},{20,16},{24,28},{28,24},{1,5},{5... | collective-permute-start | bytes 221192 | tf_op jit(solution)/shard_map/layer_one_back/ppermute | solution.py:43
  153.6 3.9 %collective-permute-start.36 = (f32[64,256]{1,0:T(8,128)S(1)}, f32[64,256]{1,0:T(8,128)S(1)}, u32[]{:S(2)}, u32[]{:S(2)}) collective-permute-start(f32[64,256]{1,0:T(8,128)S(1)} %get-tuple-element.178), channel_id=1, source_target_pairs={{0,3},{1,2},{2,1},{3,0},{4,7},{5,6},{6,5},{7,4},{8,11},{9,10},{10,... | collective-permute-start | bytes 196616 | tf_op jit(solution)/shard_map/layer_one_back/ppermute | solution.py:43
  153.7 5.0 %collective-permute-start.35 = (f32[64,256]{1,0:T(8,128)S(1)}, f32[64,256]{1,0:T(8,128)S(1)}, u32[]{:S(2)}, u32[]{:S(2)}) collective-permute-start(f32[64,256]{1,0:T(8,128)S(1)} %get-tuple-element.178), channel_id=1, source_target_pairs={{0,2},{1,3},{2,0},{3,1},{4,6},{5,7},{6,4},{7,5},{8,10},{9,11},{10,... | collective-permute-start | bytes 196616 | tf_op jit(solution)/shard_map/layer_one_back/ppermute | solution.py:43
  154.5 4.2 %collective-permute-start.34 = (f32[64,256]{1,0:T(8,128)S(1)}, f32[64,256]{1,0:T(8,128)S(1)}, u32[]{:S(2)}, u32[]{:S(2)}) collective-permute-start(f32[64,256]{1,0:T(8,128)S(1)} %get-tuple-element.178), channel_id=1, source_target_pairs={{0,1},{1,0},{2,3},{3,2},{4,5},{5,4},{6,7},{7,6},{8,9},{9,8},{10,11... | collective-permute-start | bytes 196616 | tf_op jit(solution)/shard_map/layer_one_back/ppermute | solution.py:43
  158.7 6.3 %collective-permute-start.37 = (f32[128,256]{1,0:T(8,128)S(1)}, f32[128,256]{1,0:T(8,128)S(1)}, u32[]{:S(2)}, u32[]{:S(2)}) collective-permute-start(f32[128,256]{1,0:T(8,128)S(1)} %get-tuple-element.184), channel_id=1, source_target_pairs={{0,1},{1,0},{2,3},{3,2},{4,5},{5,4},{6,7},{7,6},{8,9},{9,8},{10,11... | collective-permute-start | bytes 393224 | tf_op jit(solution)/shard_map/layer_one_back/ppermute | solution.py:43
  158.9 4.6 %collective-permute-start.40 = (f32[64,256]{1,0:T(8,128)S(1)}, f32[64,256]{1,0:T(8,128)S(1)}, u32[]{:S(2)}, u32[]{:S(2)}) collective-permute-start(f32[64,256]{1,0:T(8,128)S(1)} %add_add_fusion.3), channel_id=1, source_target_pairs={{0,4},{4,0},{8,12},{12,8},{16,20},{20,16},{24,28},{28,24},{1,5},{5... | collective-permute-start | bytes 196616 | tf_op jit(solution)/shard_map/layer_one_back/ppermute | solution.py:43
  162.0 6.4 %collective-permute-start.38 = (f32[128,256]{1,0:T(8,128)S(1)}, f32[128,256]{1,0:T(8,128)S(1)}, u32[]{:S(2)}, u32[]{:S(2)}) collective-permute-start(f32[128,256]{1,0:T(8,128)S(1)} %get-tuple-element.185), channel_id=1, source_target_pairs={{0,2},{1,3},{2,0},{3,1},{4,6},{5,7},{6,4},{7,5},{8,10},{9,11},{10,... | collective-permute-start | bytes 393224 | tf_op jit(solution)/shard_map/layer_one_back/ppermute | solution.py:43
  163.3 6.1 %collective-permute-start.39 = (f32[128,256]{1,0:T(8,128)S(1)}, f32[128,256]{1,0:T(8,128)S(1)}, u32[]{:S(2)}, u32[]{:S(2)}) collective-permute-start(f32[128,256]{1,0:T(8,128)S(1)} %get-tuple-element.186), channel_id=1, source_target_pairs={{0,3},{1,2},{2,1},{3,0},{4,7},{5,6},{6,5},{7,4},{8,11},{9,10},{10,... | collective-permute-start | bytes 393224 | tf_op jit(solution)/shard_map/layer_one_back/ppermute | solution.py:43
  163.5 6.9 %collective-permute-start.43 = (f32[64,256]{1,0:T(8,128)S(1)}, f32[64,256]{1,0:T(8,128)S(1)}, u32[]{:S(2)}, u32[]{:S(2)}) collective-permute-start(f32[64,256]{1,0:T(8,128)S(1)} %add.272), channel_id=1, source_target_pairs={{0,24},{4,28},{8,16},{12,20},{16,8},{20,12},{24,0},{28,4},{1,25},{... | collective-permute-start | bytes 196616 | tf_op jit(solution)/shard_map/layer_one_back/ppermute | solution.py:43
  165.0 7.9 %collective-permute-start.42 = (f32[64,256]{1,0:T(8,128)S(1)}, f32[64,256]{1,0:T(8,128)S(1)}, u32[]{:S(2)}, u32[]{:S(2)}) collective-permute-start(f32[64,256]{1,0:T(8,128)S(1)} %add.272), channel_id=1, source_target_pairs={{0,16},{4,20},{8,24},{12,28},{16,0},{20,4},{24,8},{28,12},{1,17},{... | collective-permute-start | bytes 196616 | tf_op jit(solution)/shard_map/layer_one_back/ppermute | solution.py:43
  165.0 7.8 %collective-permute-start.41 = (f32[64,256]{1,0:T(8,128)S(1)}, f32[64,256]{1,0:T(8,128)S(1)}, u32[]{:S(2)}, u32[]{:S(2)}) collective-permute-start(f32[64,256]{1,0:T(8,128)S(1)} %add.272), channel_id=1, source_target_pairs={{0,8},{4,12},{8,0},{12,4},{16,24},{20,28},{24,16},{28,20},{1,9},{5... | collective-permute-start | bytes 196616 | tf_op jit(solution)/shard_map/layer_one_back/ppermute | solution.py:43
